TPU v7x, 256 devices: a whole 4x4x8 slice. The times are simulated.
256 devices in a mesh: dp: 4 (over x), seq: 64 (over y, z, core).
Axes of the slice: x: 4, y: 4, z: 8, core: 2. Of those that a mesh axis runs over, the one named last changes fastest.
Arguments:
- tokens: bfloat16 [4, 8192, 1024], P('dp', 'seq'), may hold values from -16 to 16
- qkv_weight: bfloat16 [1024, 3072], P('dp'), may hold values from -0.1875 to 0.1875
- out_gain: bfloat16 [1024], replicated, may hold values from 0.099609375 to 1.8984375
- out_grad: bfloat16 [4, 8192, 1024], P('dp', 'seq'), may hold values from -0.125 to 0.125
Outputs:
- attended: bfloat16 [4, 8192, 1024], P('dp', 'seq')
- input_grad: bfloat16 [4, 8192, 1024], P('dp', 'seq')
- weight_grad: float32 [1024, 3072], P(('dp', 'seq'))
- gain_grad: float32 [1024], replicated
All inputs are finite; a program needn't handle non-finite values.
Results may differ from a plain program's by a relative error of at most 0.014.
Values may be sent and summed in bfloat16 or wider, within the bound.
No kernel may reach another device: no remote copies, remote signals or barrier semaphores. Data moves between devices by JAX's collectives and lax.ppermute only.
A program may use at most 192 MiB of HBM per device.

v0:
```python
import jax
import jax.numpy as jnp
from jax import lax
from jax.sharding import PartitionSpec as P

HEADS = 8
HEAD_DIM = 128


EPSILON = 1e-05
HIGH = lax.Precision.HIGHEST


def prefix(x, axis, join, neutral, backward):
    count = lax.axis_size(axis)
    place = lax.axis_index(axis)
    ahead = count - 1 - place if backward else place
    gathered = lax.all_gather(x.astype(jnp.bfloat16), axis)
    state = jnp.zeros_like(x) + jnp.asarray(neutral, x.dtype)

    def one(lap, state):
        source = count - 1 - lap if backward else lap
        return join(state, lax.dynamic_index_in_dim(gathered, source, 0, False).astype(x.dtype))

    return lax.fori_loop(0, ahead, one, state)


def add_states(earlier, later):
    return earlier + later


def local(tokens, qkv_weight, out_gain, out_grad):
    replicas = lax.axis_size("dp")
    weights_all = lax.all_gather(qkv_weight, "dp", axis=0, tiled=True)
    inputs = tokens[0]
    block_len = inputs.shape[0]
    inner = out_gain.shape[0]
    projected = jnp.dot(inputs, weights_all, preferred_element_type=jnp.float32).astype(
        jnp.bfloat16
    )
    query_rows = projected[:, :inner].reshape(block_len, HEADS, HEAD_DIM)
    key_rows = projected[:, inner : 2 * inner].reshape(block_len, HEADS, HEAD_DIM)
    value_rows = projected[:, 2 * inner :].reshape(block_len, HEADS, HEAD_DIM)
    kv_local = jnp.einsum("chd,che->hde", key_rows, value_rows, preferred_element_type=jnp.float32)
    prefix_state = prefix(kv_local, "seq", add_states, jnp.zeros_like(kv_local), False)
    positions = lax.iota(jnp.int32, block_len)
    causal_mask = (positions[:, None] >= positions[None, :]).astype(jnp.float32)
    scores = (
        jnp.einsum("thd,shd->hts", query_rows, key_rows, preferred_element_type=jnp.float32)
        * causal_mask
    ).astype(jnp.bfloat16)
    intra_part = jnp.einsum("hts,she->the", scores, value_rows, preferred_element_type=jnp.float32)
    inter_part = jnp.einsum(
        "thd,hde->the", query_rows.astype(jnp.float32), prefix_state, precision=HIGH
    )
    mixed_state = inter_part + intra_part
    inverse_rms = lax.rsqrt(jnp.mean(mixed_state * mixed_state, axis=-1, keepdims=True) + EPSILON)
    normed = mixed_state * inverse_rms
    gain_heads = out_gain.astype(jnp.float32).reshape(HEADS, HEAD_DIM)
    attended = (gain_heads * normed).astype(jnp.bfloat16).reshape(block_len, inner)
    upstream = out_grad[0].astype(jnp.float32).reshape(block_len, HEADS, HEAD_DIM)
    gain_local = jnp.sum(upstream * normed, axis=0).reshape(inner)
    gain_total = lax.psum(gain_local, ("dp", "seq")) / replicas
    normed_grad = upstream * gain_heads
    mixed_grad = (
        inverse_rms
        * (normed_grad - normed * jnp.mean(normed_grad * normed, axis=-1, keepdims=True))
    ).astype(jnp.bfloat16)
    grad_local = jnp.einsum(
        "thd,the->hde", query_rows, mixed_grad, preferred_element_type=jnp.float32
    )
    suffix_state = prefix(grad_local, "seq", add_states, jnp.zeros_like(grad_local), True)
    score_grad = (
        jnp.einsum("the,she->hts", mixed_grad, value_rows, preferred_element_type=jnp.float32)
        * causal_mask
    ).astype(jnp.bfloat16)
    query_grad = jnp.einsum(
        "hts,shd->thd", score_grad, key_rows, preferred_element_type=jnp.float32
    )
    query_grad = query_grad + jnp.einsum(
        "the,hde->thd", mixed_grad.astype(jnp.float32), prefix_state, precision=HIGH
    )
    key_grad = jnp.einsum(
        "hts,thd->shd", score_grad, query_rows, preferred_element_type=jnp.float32
    )
    key_grad = key_grad + jnp.einsum(
        "she,hde->shd", value_rows.astype(jnp.float32), suffix_state, precision=HIGH
    )
    value_grad = jnp.einsum("hts,the->she", scores, mixed_grad, preferred_element_type=jnp.float32)
    value_grad = value_grad + jnp.einsum(
        "shd,hde->she", key_rows.astype(jnp.float32), suffix_state, precision=HIGH
    )
    projected_grad = jnp.concatenate(
        [
            query_grad.reshape(block_len, inner),
            key_grad.reshape(block_len, inner),
            value_grad.reshape(block_len, inner),
        ],
        axis=1,
    ).astype(jnp.bfloat16)
    input_grad = lax.dot_general(
        projected_grad, weights_all, (((1,), (1,)), ((), ())), preferred_element_type=jnp.float32
    ).astype(jnp.bfloat16)
    weight_grad = lax.psum_scatter(
        lax.dot_general(
            inputs, projected_grad, (((0,), (0,)), ((), ())), preferred_element_type=jnp.float32
        ),
        ("dp", "seq"),
        scatter_dimension=0,
        tiled=True,
    )
    weight_grad = weight_grad / replicas
    return (attended[None], input_grad[None], weight_grad, gain_total)


def solution(mesh):
    placed = (P("dp", "seq", None), P("dp", None), P(), P("dp", "seq", None))
    return jax.shard_map(
        local,
        mesh=mesh,
        in_specs=placed,
        out_specs=(P("dp", "seq", None), P("dp", "seq", None), P(("dp", "seq"), None), P()),
        check_vma=False,
    )
```

profile of v0, /device:TPU:1, one launch (start us, length us, event | category | flops | bytes accessed | tf_op | source)
XLA Modules:
  0.0 720.6 jit_solution(1560643054625333339)
XLA Ops:
  8.0 73.9 %all-gather.6.cloned.1.call-done = bf16[1024,3072]{1,0:T(8,128)(2,1)} async-done(((bf16[256,3072]{1,0:T(8,128)(2,1)}), bf16[1024,3072]{1,0:T(8,128)(2,1)}) %all-gather.6.cloned.1.call-update) | async-done | bytes 6291472 | tf_op jit(solution)/shard_map/all_gather | solution.py:34
  81.9 3.8 convolution_convert_fusion
  87.8 100.5 %all-gather.8.cloned.1.call-done = bf16[512,128,128]{2,1,0:T(8,128)(2,1)} async-done(((bf16[8,128,128]{2,1,0:T(8,128)(2,1)}), bf16[512,128,128]{2,1,0:T(8,128)(2,1)}) %all-gather.8.cloned.1.call-update) | async-done | bytes 16777232 | tf_op jit(solution)/shard_map/all_gather | solution.py:18
  188.3 1.1 while.22
  193.1 161.3 %all-gather.10.cloned.1.call-done = bf16[512,128,128]{2,1,0:T(8,128)(2,1)} async-done(((bf16[8,128,128]{2,1,0:T(8,128)(2,1)}), bf16[512,128,128]{2,1,0:T(8,128)(2,1)}) %all-gather.10.cloned.1.call-update) | async-done | bytes 16777232 | tf_op jit(solution)/shard_map/all_gather | solution.py:18
  354.5 67.7 %while.23 = (s32[]{:T(128)}, f32[8,128,128]{2,1,0:T(8,128)S(1)}, s32[]{:T(128)}, bf16[64,8,128,128]{3,2,1,0:T(8,128)(2,1)}, s32[]{:T(128)}, /*index=5*/s32[]{:T(128)}, s32[]{:T(128)}, s32[]{:T(128)}) while((s32[]{:T(128)}, f32[8,128,128]{2,1,0:T(8,128)S(1)}, s32[]{:T(128)}, bf16[64,8,128,128]{3,2,1,0:T(8,128)(2,1)}, s32[]{:T(128)}, ...), condition=%wide.region_5.6_spmd, body=%wide.region_4.5_spmd.sunk | while | flops 262150 | bytes 1310863 | solution.py:25
  354.5 1.1 convert_add_fusion.5
  355.6 1.1 convert_add_fusion.5
  357.8 1.1 convert_add_fusion.5
  358.9 1.1 convert_add_fusion.5
  360.0 1.1 convert_add_fusion.5
  362.2 1.1 convert_add_fusion.5
  363.3 1.1 convert_add_fusion.5
  366.5 1.1 convert_add_fusion.5
  367.6 1.1 convert_add_fusion.5
  369.8 1.1 convert_add_fusion.5
  370.9 1.1 convert_add_fusion.5
  372.0 1.1 convert_add_fusion.5
  374.2 1.1 convert_add_fusion.5
  375.3 1.1 convert_add_fusion.5
  376.4 1.1 convert_add_fusion.5
  378.5 1.1 convert_add_fusion.5
  379.6 1.1 convert_add_fusion.5
  380.7 1.1 convert_add_fusion.5
  382.9 1.1 convert_add_fusion.5
  384.0 1.1 convert_add_fusion.5
  423.9 6.3 convolution_bitcast_fusion
  431.1 74.7 %psum.7 = f32[1024]{0:T(1024)S(1)} all-reduce(f32[1024]{0:T(1024)S(1)} %bitcast.100), channel_id=1, replica_groups=mesh['dp'=4,'seq'=64] {'dp','seq'}, use_global_device_ids=true, to_apply=%region_8.9 | all-reduce | flops 1024 | bytes 8192 | tf_op jit(solution)/shard_map/psum | solution.py:63
  506.4 5.9 fusion.6
  512.3 198.8 %all-reduce.3.cloned.1.call-done = f32[1024,3072]{0,1:T(8,128)} async-done(((f32[1024,3072]{0,1:T(8,128)}), f32[1024,3072]{0,1:T(8,128)}) %all-reduce.3.cloned.1.call-update) | async-done | bytes 12582928
  711.1 1.9 dynamic-slice_multiply_fusion
  713.0 1.1 copy.47
  (86 shorter events, 55.7 us)
Async XLA Ops:
  7.2 74.7 %copy-start = (bf16[1,128,1024]{2,1,0:T(8,128)(2,1)S(1)}, bf16[1,128,1024]{2,1,0:T(8,128)(2,1)}, u32[]{:S(2)}) copy-start(bf16[1,128,1024]{2,1,0:T(8,128)(2,1)} %param.8) | copy-start | bytes 786436
  7.2 74.7 %all-gather.6.cloned.1.call-start = ((), (), s32[]{:S(2)}) async-start(), calls=%async_computation | async-start | bytes 7864320 | tf_op jit(solution)/shard_map/all_gather | solution.py:34
  7.9 180.4 %all-gather.8.cloned.1.call-start = ((), (), s32[]{:S(2)}) async-start(), calls=%async_computation.1 | async-start | bytes 17039360 | tf_op jit(solution)/shard_map/all_gather | solution.py:18
  85.6 1.5 copy-start.2
  85.8 1.5 copy-start.3
  87.1 267.4 %all-gather.10.cloned.1.call-start = ((), (), s32[]{:S(2)}) async-start(), calls=%async_computation.2 | async-start | bytes 17039360 | tf_op jit(solution)/shard_map/all_gather | solution.py:18
  192.1 519.0 %all-reduce.3.cloned.1.call-start = ((), (), s32[]{:S(2)}) async-start(), calls=%async_computation.3 | async-start | bytes 25165824
  711.1 3.0 copy-start.1
Sparse Core Ops, SparseCore 0:
  9.8 71.9 all-gather.5
  87.2 101.0 all-gather.7
  192.2 162.2 all-gather.9
  430.4 280.6 all-reduce.2
where the time goes:
time: 724 us; the launch traced here: 721 us
  waiting for transfers between devices  535 us (74%)
  blocking collectives  74.7 us (10%)
  other arithmetic  70.6 us (10%)
  matrix products  21.9 us (3%)
  between operations  14 us (2%)
    all_gather x2, waiting for transfers between devices, prefix(): gathered = lax.all_gather(x.astype(jnp.bfloat16), axis)  262 us
    unnamed x5, waiting for transfers between devices  200 us
    psum x1, blocking collectives, local(): gain_total = lax.psum(gain_local, ('dp', 'seq')) / replicas  74.7 us
    all_gather x1, waiting for transfers between devices, local(): weights_all = lax.all_gather(qkv_weight, 'dp', axis=0, tiled=True)  73.9 us
    add x63, other arithmetic, add_states(): return earlier + later  67.4 us
  transfers between devices with their start and end apart: 4, of which 4 were waited for; matrix products, arithmetic and copies ran while one was open for 1% of the time, Pallas kernels for 0%

commit v1 on v0

v1 whole, which is shorter than its diff:
```python
import jax
import jax.numpy as jnp
from jax import lax
from jax.sharding import Mesh, PartitionSpec as P

HEADS = 8
HEAD_DIM = 128
EPSILON = 1e-05
BF = jnp.bfloat16
F32 = jnp.float32

SEQ = ("yh", "yl", "zh", "zm", "zl", "c")
CUBE = ("yl", "zl", "c")
RUN = ("zh", "zm")
ALL = ("dp",) + SEQ
SWAP = [(0, 1), (1, 0)]


def swap(x, axis):
    return lax.ppermute(x, axis, SWAP)


def ordered(mine, other, axis):
    first = lax.axis_index(axis) == 0
    return jnp.where(first, jnp.stack([mine, other]), jnp.stack([other, mine]))


def dot(a, b, contract, out=F32):
    return lax.dot_general(a, b, ((contract[0], contract[1]), ((), ())), preferred_element_type=F32).astype(out)


def gather_cube(block):
    half = block.shape[1] // 2
    left, right = block[:, :half], block[:, half:]
    left = ordered(left, swap(left, "yl"), "yl")
    right = ordered(right, swap(right, "zl"), "zl")
    left_far = swap(left, "zl")
    right_far = swap(right, "yl")
    left = jnp.swapaxes(ordered(left, left_far, "zl"), 0, 1)
    right = ordered(right, right_far, "yl")
    both = jnp.concatenate([left, right], axis=-1)
    core = swap(both, "c")
    full = ordered(both, core, "c")
    return jnp.transpose(full, (1, 2, 0, 3, 4)).reshape(8 * block.shape[0], block.shape[1])


def parts3(x):
    high = x.astype(BF)
    rest = x - high.astype(F32)
    middle = rest.astype(BF)
    return high, middle, (rest - middle.astype(F32)).astype(BF)


def exchange(states, extra, backward):
    d = states.shape[-1]
    rows = 16
    def pack(s, e):
        pad = jnp.zeros((rows - 3, d), BF)
        return jnp.concatenate([s.reshape(-1, d).astype(BF), e, pad], axis=0)
    place = lax.axis_index(RUN)
    payload = pack(states, extra)
    mine = payload.astype(F32)
    total = mine
    near = jnp.zeros((2 * d, d), F32)
    for k in (1, 2, 3):
        got = lax.ppermute(payload, RUN, [(i, i ^ k) for i in range(4)]).astype(F32)
        total = total + got
        source = place ^ k
        use = (source > place) if backward else (source < place)
        near = near + jnp.where(use, got[: 2 * d], 0.0)
    term = total[2 * d : 2 * d + 3].sum(axis=0)
    both = total[:d] + total[d : 2 * d]
    far = swap(pack(both, jnp.stack(parts3(term))), "yh").astype(F32)
    yh = lax.axis_index("yh")
    cross = jnp.where((yh == 0) if backward else (yh == 1), far[:d], 0.0)
    near = near.reshape(2, d, d)
    if backward:
        state = jnp.stack([near[0] + total[d : 2 * d] + cross, near[1] + cross])
    else:
        state = jnp.stack([near[0] + cross, near[1] + total[:d] + cross])
    return state, term + far[d : d + 3].sum(axis=0)


def local(tokens, qkv_weight, out_gain, out_grad):
    replicas = lax.axis_size("dp")
    d = HEAD_DIM
    block = tokens[0]
    n, width = block.shape
    inner = out_gain.shape[0]
    depth = qkv_weight.shape[0]
    head = lax.axis_index(CUBE)
    core = lax.axis_index("c")
    dp = lax.axis_index("dp")

    everyone = gather_cube(block)

    w_head = lax.dynamic_index_in_dim(qkv_weight.reshape(depth, 3, HEADS, d), head, 2, False).reshape(depth, 3 * d)
    pieces = jnp.zeros((replicas, depth, 3 * d), BF)
    pieces = lax.dynamic_update_index_in_dim(pieces, w_head, dp, 0)
    for k in range(1, replicas):
        got = lax.ppermute(w_head, "dp", [(i, (i + k) % replicas) for i in range(replicas)])
        pieces = lax.dynamic_update_index_in_dim(pieces, got, lax.rem(dp - k + replicas, replicas), 0)
    w_cols = pieces.reshape(replicas * depth, 3 * d)

    upstream = lax.all_to_all(
        jnp.swapaxes(out_grad[0].reshape(n, HEADS, d), 0, 1), CUBE, 0, 0, tiled=True
    ).reshape(2, 4 * n, d)

    w_half = lax.dynamic_slice_in_dim(qkv_weight, core * (depth // 2), depth // 2, 0)
    w_mine = lax.all_gather(w_half, "dp", axis=0, tiled=True)
    w_other = swap(w_mine, "c")

    projected = dot(everyone, w_cols, ((1,), (0,)), BF).reshape(2, 4 * n, 3, d)
    query, key, value = projected[:, :, 0], projected[:, :, 1], projected[:, :, 2]
    kv = jnp.einsum("scd,sce->sde", key, value, preferred_element_type=F32)
    before, _ = exchange(kv, jnp.zeros((3, d), BF), False)
    before = before.astype(BF)
    rows = lax.iota(jnp.int32, 4 * n)
    causal = rows[:, None] >= rows[None, :]
    scores = jnp.where(causal, jnp.einsum("std,sud->stu", query, key, preferred_element_type=F32), 0.0).astype(BF)
    mixed = jnp.einsum("stu,sue->ste", scores, value, preferred_element_type=F32)
    mixed = mixed + jnp.einsum("std,sde->ste", query, before, preferred_element_type=F32)
    inverse_rms = lax.rsqrt(jnp.mean(mixed * mixed, axis=-1, keepdims=True) + EPSILON)
    normed = mixed * inverse_rms
    gain = lax.dynamic_slice_in_dim(out_gain, head * d, d, 0).astype(F32)
    attended_head = (gain * normed).astype(BF)
    up = upstream.astype(F32)
    gain_part = jnp.sum(up * normed, axis=(0, 1))
    normed_grad = up * gain
    mixed_grad = (
        inverse_rms * (normed_grad - normed * jnp.mean(normed_grad * normed, axis=-1, keepdims=True))
    ).astype(BF)
    grads = jnp.einsum("std,ste->sde", query, mixed_grad, preferred_element_type=F32)
    after, gain_sum = exchange(grads, jnp.stack(parts3(gain_part)), True)
    after = after.astype(BF)

    gain_rows = jnp.concatenate([jnp.stack(parts3(gain_sum)), jnp.zeros((13, d), BF)], axis=0)
    sent = jnp.concatenate(
        [attended_head.reshape(HEADS, n, d), jnp.broadcast_to(gain_rows[None], (HEADS, 16, d))], axis=1
    )
    back = lax.all_to_all(sent, CUBE, 0, 0, tiled=True)
    attended = jnp.swapaxes(back[:, :n], 0, 1).reshape(n, inner)
    gain_all = back[:, n : n + 3].astype(F32).sum(axis=1)
    gain_total = gain_all
    for k in range(1, replicas):
        gain_total = gain_total + lax.ppermute(gain_all, "dp", [(i, (i + k) % replicas) for i in range(replicas)])
    gain_grad = gain_total.reshape(inner) / replicas

    score_grad = jnp.where(
        causal, jnp.einsum("ste,sue->stu", mixed_grad, value, preferred_element_type=F32), 0.0
    ).astype(BF)
    query_grad = jnp.einsum("stu,sud->std", score_grad, key, preferred_element_type=F32)
    query_grad = query_grad + jnp.einsum("ste,sde->std", mixed_grad, before, preferred_element_type=F32)
    key_grad = jnp.einsum("stu,std->sud", score_grad, query, preferred_element_type=F32)
    key_grad = key_grad + jnp.einsum("sue,sde->sud", value, after, preferred_element_type=F32)
    value_grad = jnp.einsum("stu,ste->sue", scores, mixed_grad, preferred_element_type=F32)
    value_grad = value_grad + jnp.einsum("sud,sde->sue", key, after, preferred_element_type=F32)
    projected_grad = jnp.concatenate([query_grad, key_grad, value_grad], axis=-1).astype(BF).reshape(8 * n, 3 * d)

    home = lax.all_to_all(projected_grad.reshape(HEADS, n, 3 * d), CUBE, 0, 0, tiled=True)
    home = jnp.transpose(home.reshape(HEADS, n, 3, d), (1, 2, 0, 3)).reshape(n, 3 * inner)
    part_mine = dot(home, w_mine, ((1,), (1,)), BF).reshape(n, replicas, 1, depth // 2)
    part_other = dot(home, w_other, ((1,), (1,)), BF).reshape(n, replicas, 1, depth // 2)
    input_grad = jnp.where(
        core == 0,
        jnp.concatenate([part_mine, part_other], axis=2),
        jnp.concatenate([part_other, part_mine], axis=2),
    ).reshape(n, width)

    weight_part = dot(everyone, projected_grad, ((0,), (0,)), BF)
    shared = lax.all_to_all(weight_part.reshape(256, width // 256, 3 * d), ALL, 0, 0, tiled=True)
    shared = shared.reshape(replicas, 2, 2, 4, 2, 2, width // 256, 3, d).astype(F32)
    weight_grad = jnp.transpose(shared.sum(axis=(0, 1, 3)), (3, 4, 0, 1, 2, 5)).reshape(width // 256, 3 * inner)
    weight_grad = weight_grad / replicas
    return (attended[None], input_grad[None], weight_grad, gain_grad)


def solution(mesh):
    fine = Mesh(mesh.devices.reshape(mesh.devices.shape[0], 2, 2, 2, 2, 2, 2), ALL)
    rows = P("dp", SEQ, None)
    return jax.shard_map(
        local,
        mesh=fine,
        in_specs=(rows, P("dp", None), P(), rows),
        out_specs=(rows, rows, P(ALL, None), P()),
        check_vma=False,
    )
```

time: 724 us -> 187 us (0.26)
  waiting for transfers between devices: 535 us -> 42.9 us
  blocking collectives: 74.7 us -> 0 us
  starting transfers between devices: 0.16 us -> 63.1 us
  other arithmetic: 70.6 us -> 18.5 us
  local copies, waits for them, and re-layouts: 2.78 us -> 29 us
    all_gather x3 -> x1, waiting for transfers between devices: 336 us -> 0.01 us  [local(): w_mine = lax.all_gather(w_half, 'dp', axis=0, tiled=True)]
    unnamed x5 -> x1, waiting for transfers between devices: 200 us -> 0.02 us
    psum x1 -> x0, blocking collectives: 74.7 us -> none  [local(): gain_total = lax.psum(gain_local, ('dp', 'seq')) / replicas]
    add x63 -> x4, other arithmetic: 67.4 us -> 1.85 us  [the longest x2 1.13 us: exchange(): total = total + got]
    ppermute x0 -> x20, starting transfers between devices: none -> 36.5 us  [the longest x8 13.4 us: swap(): return lax.ppermute(x, axis, SWAP)]
    all_to_all x0 -> x4, starting transfers between devices: none -> 26.6 us  [the longest x1 9.16 us: local(): lax.all_to_all(weight_part.reshape(256, width // 256, 3 * d), ALL, 0, 0,...]
    all_to_all x0 -> x4, waiting for transfers between devices: none -> 25.5 us  [the longest x1 18.5 us: local(): lax.all_to_all(weight_part.reshape(256, width // 256, 3 * d), ALL, 0, 0,...]
    ppermute x0 -> x20, waiting for transfers between devices: none -> 17.4 us  [the longest x8 9.63 us: swap(): return lax.ppermute(x, axis, SWAP)]
  transfers between devices with their start and end apart: 4 -> 25, of which waited for: 4 -> 7; matrix products, arithmetic and copies ran while one was open for 1% -> 31% of each run, Pallas kernels for 0% -> 0%
where the time goes in v1:
time: 187 us; the launch traced here: 186 us
  starting transfers between devices  63.1 us (34%)
  waiting for transfers between devices  42.9 us (23%)
  local copies, waits for them, and re-layouts  29 us (16%)
  other arithmetic  18.5 us (10%)
  matrix products  17.8 us (10%)
  between operations  14.7 us (8%)
    all_to_all x1, waiting for transfers between devices, local(): lax.all_to_all(weight_part.reshape(256, width // 256, 3 * d), ALL, 0, 0,...  18.5 us
    ppermute x8, starting transfers between devices, swap(): return lax.ppermute(x, axis, SWAP)  13.4 us
    ppermute x6, starting transfers between devices, exchange(): got = lax.ppermute(payload, RUN, [(i, i ^ k) for i in range(4)]).astype(F32)  13.1 us
    dot_general x4, matrix products, dot(): lax.dot_general(a, b, ((contract[0], contract[1]), ((), ())), preferred_e...  11.8 us
    ppermute x8, waiting for transfers between devices, swap(): return lax.ppermute(x, axis, SWAP)  9.63 us
    all_to_all x1, starting transfers between devices, local(): lax.all_to_all(weight_part.reshape(256, width // 256, 3 * d), ALL, 0, 0,...  9.16 us
    ppermute x6, waiting for transfers between devices, exchange(): got = lax.ppermute(payload, RUN, [(i, i ^ k) for i in range(4)]).astype(F32)  7.74 us
    all_to_all x1, starting transfers between devices, local(): back = lax.all_to_all(sent, CUBE, 0, 0, tiled=True)  7.13 us
  transfers between devices with their start and end apart: 25, of which 7 were waited for; matrix products, arithmetic and copies ran while one was open for 31% of the time, Pallas kernels for 0%

profile of v1, /device:TPU:1, one launch (start us, length us, event | category | flops | bytes accessed | tf_op | source)
XLA Modules:
  0.0 186.0 jit_solution(6673686858190061624)
XLA Ops:
  8.3 2.6 %collective-permute-start.2 = (bf16[128,512]{1,0:T(8,128)(2,1)S(1)}, bf16[128,512]{1,0:T(8,128)(2,1)S(1)}, u32[]{:S(2)}, u32[]{:S(2)}) collective-permute-start(bf16[128,512]{1,0:T(8,128)(2,1)S(1)} %get-tuple-element.17), channel_id=1, source_target_pairs={{0,2},{2,0},{1,3},{3,1},{4,6},{6,4},{5,7},{7,5},{8,10},{10,8},{9,1... | collective-permute-start | bytes 393224 | tf_op jit(solution)/shard_map/ppermute | solution.py:20
  12.1 1.7 copy.105
  15.1 2.5 %collective-permute-start.6 = (bf16[256,384]{0,1:T(8,128)(2,1)S(1)}, bf16[256,384]{0,1:T(8,128)(2,1)}, u32[]{:S(2)}, u32[]{:S(2)}) collective-permute-start(bf16[256,384]{0,1:T(8,128)(2,1)S(1)} %bitcast.182), channel_id=1, source_target_pairs={{0,128},{64,192},{128,0},{192,64},{1,129},{65,193},{129,1},{193,65... | collective-permute-start | bytes 589832 | tf_op jit(solution)/shard_map/ppermute | solution.py:101
  19.5 5.4 %all-to-all-start = ((bf16[8,128,128]{2,1,0:T(8,128)(2,1)}), bf16[8,128,128]{2,1,0:T(8,128)(2,1)S(1)}, u32[]{:S(2)}, u32[]{:S(2)}) async-start(bf16[8,128,128]{2,1,0:T(8,128)(2,1)} %bitcast.160), calls=%async_computation | async-start | bytes 524288 | tf_op jit(solution)/shard_map/all_to_all | solution.py:105
  25.0 1.5 collective-permute-start.3
  27.9 7.9 %collective-permute-done.3 = bf16[2,128,512]{2,1,0:T(8,128)(2,1)S(1)} collective-permute-done((bf16[2,128,512]{2,1,0:T(8,128)(2,1)S(1)}, bf16[2,128,512]{2,1,0:T(8,128)(2,1)S(1)}, u32[]{:S(2)}, u32[]{:S(2)}) %collective-permute-start.3) | collective-permute-done | bytes 262176 | tf_op jit(solution)/shard_map/ppermute | solution.py:20
  45.3 1.7 maximum_select_fusion
  47.0 2.8 %convolution_convert_fusion.1 = bf16[1024,384]{1,0:T(8,128)(2,1)S(1)} fusion(bf16[1024,1024]{1,0:T(8,128)(2,1)} %bitcast.15, bf16[1024,384]{1,0:T(8,128)(2,1)S(1)} %bitcast.185), kind=kOutput, calls=%fused_computation.4 | convolution fusion | flops 805699584 | bytes 3670016 | tf_op jit(solution)/shard_map/dot_general | solution.py:29
  51.8 5.3 %collective-permute-start.10 = (bf16[272,128]{1,0:T(8,128)(2,1)S(1)}, bf16[272,128]{1,0:T(8,128)(2,1)S(1)}, u32[]{:S(2)}, u32[]{:S(2)}) collective-permute-start(bf16[272,128]{1,0:T(8,128)(2,1)S(1)} %pad_maximum_fusion.3), channel_id=1, source_target_pairs={{0,12},{4,8},{8,4},{12,0},{1,13},{5,9},{9,5},{13,1},{2,14},{6,10},... | collective-permute-start | bytes 208904 | tf_op jit(solution)/shard_map/ppermute | solution.py:66
  59.8 1.7 collective-permute-done.8
  61.5 6.0 %collective-permute-done.9 = bf16[272,128]{1,0:T(8,128)(2,1)S(1)} collective-permute-done((bf16[272,128]{1,0:T(8,128)(2,1)S(1)}, bf16[272,128]{1,0:T(8,128)(2,1)S(1)}, u32[]{:S(2)}, u32[]{:S(2)}) %collective-permute-start.9) | collective-permute-done | bytes 69664 | tf_op jit(solution)/shard_map/ppermute | solution.py:66
  67.8 2.8 %collective-permute-start.11 = (bf16[144,128]{1,0:T(8,128)(2,1)S(1)}, bf16[144,128]{1,0:T(8,128)(2,1)S(1)}, u32[]{:S(2)}, u32[]{:S(2)}) collective-permute-start(bf16[144,128]{1,0:T(8,128)(2,1)S(1)} %concatenate.78), channel_id=1, source_target_pairs={{0,32},{32,0},{1,33},{33,1},{2,34},{34,2},{3,35},{35,3},{4,36},{36... | collective-permute-start | bytes 110600 | tf_op jit(solution)/shard_map/ppermute | solution.py:20
  70.7 1.7 collective-permute-done.11
  75.0 2.5 %concatenate.79 = bf16[272,128]{1,0:T(8,128)(2,1)} concatenate(bf16[256,128]{1,0:T(8,128)(2,1)S(1)} %bitcast.192, bf16[1,128]{1,0:T(2,128)(2,1)S(1)} %bitcast_convert_fusion.1, bf16[1,128]{1,0:T(2,128)(2,1)S(1)} %get-tuple-element.29, bf16[1,128]{1,0:T(2,128)(2,1)S(1)} %get-tuple-element.28, bf16[13,128]{1,0:T(8,128)(2,1)S(1)} %broadcast.59), dimensions={0} | concatenate | bytes 139264 | tf_op jit(solution)/shard_map/concatenate | solution.py:59
  77.5 2.5 %collective-permute-start.13 = (bf16[272,128]{1,0:T(8,128)(2,1)}, bf16[272,128]{1,0:T(8,128)(2,1)S(1)}, u32[]{:S(2)}, u32[]{:S(2)}) collective-permute-start(bf16[272,128]{1,0:T(8,128)(2,1)} %concatenate.79), channel_id=1, source_target_pairs={{0,8},{4,12},{8,0},{12,4},{1,9},{5,13},{9,1},{13,5},{2,10},{6,14},... | collective-permute-start | bytes 208904 | tf_op jit(solution)/shard_map/ppermute | solution.py:66
  80.0 3.1 %collective-permute-start.14 = (bf16[272,128]{1,0:T(8,128)(2,1)}, bf16[272,128]{1,0:T(8,128)(2,1)}, u32[]{:S(2)}, u32[]{:S(2)}) collective-permute-start(bf16[272,128]{1,0:T(8,128)(2,1)} %concatenate.79), channel_id=1, source_target_pairs={{0,12},{4,8},{8,4},{12,0},{1,13},{5,9},{9,5},{13,1},{2,14},{6,10},... | collective-permute-start | bytes 208904 | tf_op jit(solution)/shard_map/ppermute | solution.py:66
  83.4 1.4 select_convert_fusion
  86.0 1.8 copy.120
  91.8 3.9 %concatenate.80 = bf16[144,128]{1,0:T(8,128)(2,1)} concatenate(bf16[128,128]{1,0:T(8,128)(2,1)} %fusion.22, bf16[1,128]{1,0:T(2,128)(2,1)} %bitcast_convert_fusion, bf16[1,128]{1,0:T(2,128)(2,1)} %get-tuple-element.27, bf16[1,128]{1,0:T(2,128)(2,1)} %get-tuple-element.26, bf16[13,128]{1,0:T(8,128)(2,1)S(1)} %broadcast.59), dimensions={0} | concatenate | bytes 73728 | tf_op jit(solution)/shard_map/concatenate | solution.py:59
  95.7 2.9 %collective-permute-start.15 = (bf16[144,128]{1,0:T(8,128)(2,1)}, bf16[144,128]{1,0:T(8,128)(2,1)S(1)}, u32[]{:S(2)}, u32[]{:S(2)}) collective-permute-start(bf16[144,128]{1,0:T(8,128)(2,1)} %concatenate.80), channel_id=1, source_target_pairs={{0,32},{32,0},{1,33},{33,1},{2,34},{34,2},{3,35},{35,3},{4,36},{36... | collective-permute-start | bytes 110600 | tf_op jit(solution)/shard_map/ppermute | solution.py:20
  103.4 7.1 %all-to-all-start.1 = ((bf16[8,144,128]{2,1,0:T(8,128)(2,1)}), bf16[8,144,128]{2,1,0:T(8,128)(2,1)}, u32[]{:S(2)}, u32[]{:S(2)}) async-start(bf16[8,144,128]{2,1,0:T(8,128)(2,1)} %pad_maximum_fusion.2), calls=%async_computation.1 | async-start | bytes 589824 | tf_op jit(solution)/shard_map/all_to_all | solution.py:141
  114.4 2.1 %all-to-all-done.1 = bf16[8,144,128]{2,1,0:T(8,128)(2,1)} async-done(((bf16[8,144,128]{2,1,0:T(8,128)(2,1)}), bf16[8,144,128]{2,1,0:T(8,128)(2,1)}, u32[]{:S(2)}, u32[]{:S(2)}) %all-to-all-start.1) | async-done | bytes 294944 | tf_op jit(solution)/shard_map/all_to_all | solution.py:141
  116.5 5.0 %all-to-all-start.2 = ((bf16[8,128,384]{1,2,0:T(8,128)(2,1)}), bf16[8,128,384]{1,2,0:T(8,128)(2,1)S(1)}, u32[]{:S(2)}, u32[]{:S(2)}) async-start(bf16[8,128,384]{1,2,0:T(8,128)(2,1)} %pad_maximum_fusion.1), calls=%async_computation.2 | async-start | bytes 1572864 | tf_op jit(solution)/shard_map/all_to_all | solution.py:160
  121.7 2.9 %convolution_convert_fusion = bf16[1024,384]{1,0:T(8,128)(2,1)S(1)} fusion(bf16[1024,1024]{1,0:T(8,128)(2,1)} %bitcast.15, bf16[1024,128]{1,0:T(8,128)(2,1)S(1)} %bitcast.180, bf16[1024,128]{1,0:T(8,128)(2,1)S(1)} %bitcast.178, bf16[1024,128]{1,0:T(8,128)(2,1)S(1)} %bitcast.176), kind=kOutput, calls=%fused_computation.3 | convolution fusion | flops 808058880 | bytes 3670016 | tf_op jit(solution)/shard_map/dot_general | solution.py:29
  125.6 4.9 %all-to-all-done.2 = bf16[8,128,384]{1,2,0:T(8,128)(2,1)S(1)} async-done(((bf16[8,128,384]{1,2,0:T(8,128)(2,1)}), bf16[8,128,384]{1,2,0:T(8,128)(2,1)S(1)}, u32[]{:S(2)}, u32[]{:S(2)}) %all-to-all-start.2) | async-done | bytes 786464 | tf_op jit(solution)/shard_map/all_to_all | solution.py:160
  130.5 9.2 %all-to-all-start.3 = ((bf16[256,4,384]{2,1,0:T(4,128)(2,1)}), bf16[256,4,384]{2,1,0:T(4,128)(2,1)S(1)}, u32[]{:S(2)}, u32[]{:S(2)}) async-start(bf16[256,4,384]{2,1,0:T(4,128)(2,1)} %reshape.390), calls=%async_computation.3 | async-start | bytes 1572864 | tf_op jit(solution)/shard_map/all_to_all | solution.py:171
  140.4 1.5 collective-permute-start.17
  141.9 2.4 %collective-permute-start.18 = (f32[8,128]{1,0:T(8,128)S(1)}, f32[8,128]{1,0:T(8,128)S(1)}, u32[]{:S(2)}, u32[]{:S(2)}) collective-permute-start(f32[8,128]{1,0:T(8,128)S(1)} %convert_reduce_fusion), channel_id=1, source_target_pairs={{0,128},{64,192},{128,0},{192,64},{1,129},{65,193},{129,1},{193,65... | collective-permute-start | bytes 12296 | tf_op jit(solution)/shard_map/ppermute | solution.py:146
  148.1 18.5 %all-to-all-done.3 = bf16[256,4,384]{2,1,0:T(4,128)(2,1)S(1)} async-done(((bf16[256,4,384]{2,1,0:T(4,128)(2,1)}), bf16[256,4,384]{2,1,0:T(4,128)(2,1)S(1)}, u32[]{:S(2)}, u32[]{:S(2)}) %all-to-all-start.3) | async-done | bytes 786464 | tf_op jit(solution)/shard_map/all_to_all | solution.py:171
  167.8 2.5 %reshape.392 = f32[4,2,2,4,2,2,4,3,128]{8,7,5,4,3,2,1,0,6:T(4,128)S(1)} reshape(f32[256,4,384]{2,0,1:T(8,128)} %copy_convert_fusion) | data formatting | bytes 3145728 | tf_op jit(solution)/shard_map/convert_element_type | solution.py:172
  171.5 3.1 %convolution_convert_fusion.3 = bf16[128,512]{1,0:T(8,128)(2,1)S(1)} fusion(bf16[128,3072]{0,1:T(8,128)(2,1)S(1)} %bitcast.162, bf16[512,3072]{1,0:T(8,128)(2,1)} %all-gather.2.cloned.1.call-done), kind=kOutput, calls=%fused_computation.13 | convolution fusion | flops 402718720 | bytes 4063232 | tf_op jit(solution)/shard_map/dot_general | solution.py:29
  174.6 3.1 %convolution_convert_fusion.2 = bf16[128,512]{1,0:T(8,128)(2,1)S(1)} fusion(bf16[128,3072]{0,1:T(8,128)(2,1)S(1)} %bitcast.163, bf16[512,3072]{1,0:T(8,128)(2,1)} %collective-permute-done.16), kind=kOutput, calls=%fused_computation.12 | convolution fusion | flops 402718720 | bytes 4063232 | tf_op jit(solution)/shard_map/dot_general | solution.py:29
  (149 shorter events, 47.5 us)
Async XLA Ops:
  7.2 11.6 %copy-start.11 = (bf16[1,128,1024]{2,1,0:T(8,128)(2,1)S(1)}, bf16[1,128,1024]{2,1,0:T(8,128)(2,1)}, u32[]{:S(2)}) copy-start(bf16[1,128,1024]{2,1,0:T(8,128)(2,1)} %param.7) | copy-start | bytes 786436
  8.3 16.7 %collective-permute-start.2 = (bf16[128,512]{1,0:T(8,128)(2,1)S(1)}, bf16[128,512]{1,0:T(8,128)(2,1)S(1)}, u32[]{:S(2)}, u32[]{:S(2)}) collective-permute-start(bf16[128,512]{1,0:T(8,128)(2,1)S(1)} %get-tuple-element.17), channel_id=1, source_target_pairs={{0,2},{2,0},{1,3},{3,1},{4,6},{6,4},{5,7},{7,5},{8,10},{10,8},{9,1... | collective-permute-start | bytes 393224 | tf_op jit(solution)/shard_map/ppermute | solution.py:20
  10.8 15.7 %collective-permute-start = (bf16[128,512]{1,0:T(8,128)(2,1)S(1)}, bf16[128,512]{1,0:T(8,128)(2,1)S(1)}, u32[]{:S(2)}, u32[]{:S(2)}) collective-permute-start(bf16[128,512]{1,0:T(8,128)(2,1)S(1)} %get-tuple-element.18), channel_id=1, source_target_pairs={{0,16},{16,0},{1,17},{17,1},{2,18},{18,2},{3,19},{19,3},{4,20},{20... | collective-permute-start | bytes 393224 | tf_op jit(solution)/shard_map/ppermute | solution.py:20
  13.8 27.0 %collective-permute-start.5 = (bf16[256,384]{0,1:T(8,128)(2,1)S(1)}, bf16[256,384]{0,1:T(8,128)(2,1)}, u32[]{:S(2)}, u32[]{:S(2)}) collective-permute-start(bf16[256,384]{0,1:T(8,128)(2,1)S(1)} %bitcast.181), channel_id=1, source_target_pairs={{0,64},{64,128},{128,192},{192,0},{1,65},{65,129},{129,193},{193,1... | collective-permute-start | bytes 589832 | tf_op jit(solution)/shard_map/ppermute | solution.py:101
  15.1 26.8 %collective-permute-start.6 = (bf16[256,384]{0,1:T(8,128)(2,1)S(1)}, bf16[256,384]{0,1:T(8,128)(2,1)}, u32[]{:S(2)}, u32[]{:S(2)}) collective-permute-start(bf16[256,384]{0,1:T(8,128)(2,1)S(1)} %bitcast.182), channel_id=1, source_target_pairs={{0,128},{64,192},{128,0},{192,64},{1,129},{65,193},{129,1},{193,65... | collective-permute-start | bytes 589832 | tf_op jit(solution)/shard_map/ppermute | solution.py:101
  17.6 25.5 %collective-permute-start.7 = (bf16[256,384]{0,1:T(8,128)(2,1)S(1)}, bf16[256,384]{0,1:T(8,128)(2,1)S(1)}, u32[]{:S(2)}, u32[]{:S(2)}) collective-permute-start(bf16[256,384]{0,1:T(8,128)(2,1)S(1)} %bitcast.183), channel_id=1, source_target_pairs={{0,192},{64,0},{128,64},{192,128},{1,193},{65,1},{129,65},{193,129... | collective-permute-start | bytes 589832 | tf_op jit(solution)/shard_map/ppermute | solution.py:101
  19.5 53.7 %all-to-all-start = ((bf16[8,128,128]{2,1,0:T(8,128)(2,1)}), bf16[8,128,128]{2,1,0:T(8,128)(2,1)S(1)}, u32[]{:S(2)}, u32[]{:S(2)}) async-start(bf16[8,128,128]{2,1,0:T(8,128)(2,1)} %bitcast.160), calls=%async_computation | async-start | bytes 524288 | tf_op jit(solution)/shard_map/all_to_all | solution.py:105
  24.9 96.5 %all-gather.2.cloned.1.call-start = ((), (), s32[]{:S(2)}) async-start(), calls=%async_computation.4 | async-start | bytes 3932160 | tf_op jit(solution)/shard_map/all_gather | solution.py:110
  25.0 10.8 %collective-permute-start.3 = (bf16[2,128,512]{2,1,0:T(8,128)(2,1)S(1)}, bf16[2,128,512]{2,1,0:T(8,128)(2,1)S(1)}, u32[]{:S(2)}, u32[]{:S(2)}) collective-permute-start(bf16[2,128,512]{2,1,0:T(8,128)(2,1)S(1)} %maximum_select_fusion.6), channel_id=1, source_target_pairs={{0,16},{16,0},{1,17},{17,1},{2,18},{18,2},{3,19},{19,3},{4,20},{20... | collective-permute-start | bytes 786440 | tf_op jit(solution)/shard_map/ppermute | solution.py:20
  26.5 9.3 %collective-permute-start.1 = (bf16[2,128,512]{2,1,0:T(8,128)(2,1)S(1)}, bf16[2,128,512]{2,1,0:T(8,128)(2,1)S(1)}, u32[]{:S(2)}, u32[]{:S(2)}) collective-permute-start(bf16[2,128,512]{2,1,0:T(8,128)(2,1)S(1)} %maximum_select_fusion.4), channel_id=1, source_target_pairs={{0,2},{2,0},{1,3},{3,1},{4,6},{6,4},{5,7},{7,5},{8,10},{10,8},{9,1... | collective-permute-start | bytes 786440 | tf_op jit(solution)/shard_map/ppermute | solution.py:20
  35.7 2.2 %copy-start.2 = (bf16[256,3072]{1,0:T(8,128)(2,1)S(1)}, bf16[256,3072]{1,0:T(8,128)(2,1)}, u32[]{:S(2)}) copy-start(bf16[256,3072]{1,0:T(8,128)(2,1)} %param.5) | copy-start | bytes 4718596
  37.1 8.3 %collective-permute-start.4 = (bf16[2,2,128,1024]{3,2,1,0:T(8,128)(2,1)}, bf16[2,2,128,1024]{3,2,1,0:T(8,128)(2,1)S(1)}, u32[]{:S(2)}, u32[]{:S(2)}) collective-permute-start(bf16[2,2,128,1024]{3,2,1,0:T(8,128)(2,1)} %get-tuple-element.10), channel_id=1, source_target_pairs={{0,1},{1,0},{2,3},{3,2},{4,5},{5,4},{6,7},{7,6},{8,9},{9,8},{10,11... | collective-permute-start | bytes 3145736 | tf_op jit(solution)/shard_map/ppermute | solution.py:20
  51.3 8.0 %copy-start.12 = (pred[512,512]{1,0:T(8,128)(4,1)S(1)}, pred[512,512]{1,0:T(8,128)(4,1)}, u32[]{:S(2)}) copy-start(pred[512,512]{1,0:T(8,128)(4,1)} %iota_compare_fusion) | copy-start | bytes 786436
  51.4 16.3 %copy-start = (bf16[2,512,128]{2,1,0:T(8,128)(2,1)}, bf16[2,512,128]{2,1,0:T(8,128)(2,1)S(1)}, u32[]{:S(2)}) copy-start(bf16[2,512,128]{2,1,0:T(8,128)(2,1)S(1)} %get-tuple-element.35) | copy-start | bytes 786436
  51.8 8.0 %collective-permute-start.10 = (bf16[272,128]{1,0:T(8,128)(2,1)S(1)}, bf16[272,128]{1,0:T(8,128)(2,1)S(1)}, u32[]{:S(2)}, u32[]{:S(2)}) collective-permute-start(bf16[272,128]{1,0:T(8,128)(2,1)S(1)} %pad_maximum_fusion.3), channel_id=1, source_target_pairs={{0,12},{4,8},{8,4},{12,0},{1,13},{5,9},{9,5},{13,1},{2,14},{6,10},... | collective-permute-start | bytes 208904 | tf_op jit(solution)/shard_map/ppermute | solution.py:66
  57.0 4.5 %collective-permute-start.8 = (bf16[272,128]{1,0:T(8,128)(2,1)S(1)}, bf16[272,128]{1,0:T(8,128)(2,1)S(1)}, u32[]{:S(2)}, u32[]{:S(2)}) collective-permute-start(bf16[272,128]{1,0:T(8,128)(2,1)S(1)} %pad_maximum_fusion.3), channel_id=1, source_target_pairs={{0,4},{4,0},{8,12},{12,8},{1,5},{5,1},{9,13},{13,9},{2,6},{6,2},{1... | collective-permute-start | bytes 208904 | tf_op jit(solution)/shard_map/ppermute | solution.py:66
  58.1 9.3 %collective-permute-start.9 = (bf16[272,128]{1,0:T(8,128)(2,1)S(1)}, bf16[272,128]{1,0:T(8,128)(2,1)S(1)}, u32[]{:S(2)}, u32[]{:S(2)}) collective-permute-start(bf16[272,128]{1,0:T(8,128)(2,1)S(1)} %pad_maximum_fusion.3), channel_id=1, source_target_pairs={{0,8},{4,12},{8,0},{12,4},{1,9},{5,13},{9,1},{13,5},{2,10},{6,14},... | collective-permute-start | bytes 208904 | tf_op jit(solution)/shard_map/ppermute | solution.py:66
  67.8 4.6 %collective-permute-start.11 = (bf16[144,128]{1,0:T(8,128)(2,1)S(1)}, bf16[144,128]{1,0:T(8,128)(2,1)S(1)}, u32[]{:S(2)}, u32[]{:S(2)}) collective-permute-start(bf16[144,128]{1,0:T(8,128)(2,1)S(1)} %concatenate.78), channel_id=1, source_target_pairs={{0,32},{32,0},{1,33},{33,1},{2,34},{34,2},{3,35},{35,3},{4,36},{36... | collective-permute-start | bytes 110600 | tf_op jit(solution)/shard_map/ppermute | solution.py:20
  74.6 10.2 %copy-start.1 = (bf16[2,512,128]{2,1,0:T(8,128)(2,1)S(1)}, bf16[2,512,128]{2,1,0:T(8,128)(2,1)}, u32[]{:S(2)}) copy-start(bf16[2,512,128]{2,1,0:T(8,128)(2,1)} %copy-done) | copy-start | bytes 786436
  77.5 10.3 %collective-permute-start.12 = (bf16[272,128]{1,0:T(8,128)(2,1)}, bf16[272,128]{1,0:T(8,128)(2,1)S(1)}, u32[]{:S(2)}, u32[]{:S(2)}) collective-permute-start(bf16[272,128]{1,0:T(8,128)(2,1)} %concatenate.79), channel_id=1, source_target_pairs={{0,4},{4,0},{8,12},{12,8},{1,5},{5,1},{9,13},{13,9},{2,6},{6,2},{1... | collective-permute-start | bytes 208904 | tf_op jit(solution)/shard_map/ppermute | solution.py:66
  77.5 10.3 %collective-permute-start.13 = (bf16[272,128]{1,0:T(8,128)(2,1)}, bf16[272,128]{1,0:T(8,128)(2,1)S(1)}, u32[]{:S(2)}, u32[]{:S(2)}) collective-permute-start(bf16[272,128]{1,0:T(8,128)(2,1)} %concatenate.79), channel_id=1, source_target_pairs={{0,8},{4,12},{8,0},{12,4},{1,9},{5,13},{9,1},{13,5},{2,10},{6,14},... | collective-permute-start | bytes 208904 | tf_op jit(solution)/shard_map/ppermute | solution.py:66
  80.0 9.0 %collective-permute-start.14 = (bf16[272,128]{1,0:T(8,128)(2,1)}, bf16[272,128]{1,0:T(8,128)(2,1)}, u32[]{:S(2)}, u32[]{:S(2)}) collective-permute-start(bf16[272,128]{1,0:T(8,128)(2,1)} %concatenate.79), channel_id=1, source_target_pairs={{0,12},{4,8},{8,4},{12,0},{1,13},{5,9},{9,5},{13,1},{2,14},{6,10},... | collective-permute-start | bytes 208904 | tf_op jit(solution)/shard_map/ppermute | solution.py:66
  84.8 17.9 %copy-start.3 = (bf16[2,512,128]{2,1,0:T(8,128)(2,1)S(1)}, bf16[2,512,128]{2,1,0:T(8,128)(2,1)}, u32[]{:S(2)}) copy-start(bf16[2,512,128]{2,1,0:T(8,128)(2,1)} %get-tuple-element.11) | copy-start | bytes 786436
  95.7 6.3 %collective-permute-start.15 = (bf16[144,128]{1,0:T(8,128)(2,1)}, bf16[144,128]{1,0:T(8,128)(2,1)S(1)}, u32[]{:S(2)}, u32[]{:S(2)}) collective-permute-start(bf16[144,128]{1,0:T(8,128)(2,1)} %concatenate.80), channel_id=1, source_target_pairs={{0,32},{32,0},{1,33},{33,1},{2,34},{34,2},{3,35},{35,3},{4,36},{36... | collective-permute-start | bytes 110600 | tf_op jit(solution)/shard_map/ppermute | solution.py:20
  103.4 13.1 %all-to-all-start.1 = ((bf16[8,144,128]{2,1,0:T(8,128)(2,1)}), bf16[8,144,128]{2,1,0:T(8,128)(2,1)}, u32[]{:S(2)}, u32[]{:S(2)}) async-start(bf16[8,144,128]{2,1,0:T(8,128)(2,1)} %pad_maximum_fusion.2), calls=%async_computation.1 | async-start | bytes 589824 | tf_op jit(solution)/shard_map/all_to_all | solution.py:141
  113.2 8.5 %copy-start.5 = (bf16[2,512,128]{2,1,0:T(8,128)(2,1)S(1)}, bf16[2,512,128]{2,1,0:T(8,128)(2,1)}, u32[]{:S(2)}) copy-start(bf16[2,512,128]{2,1,0:T(8,128)(2,1)} %fusion) | copy-start | bytes 786436
  116.5 14.0 %all-to-all-start.2 = ((bf16[8,128,384]{1,2,0:T(8,128)(2,1)}), bf16[8,128,384]{1,2,0:T(8,128)(2,1)S(1)}, u32[]{:S(2)}, u32[]{:S(2)}) async-start(bf16[8,128,384]{1,2,0:T(8,128)(2,1)} %pad_maximum_fusion.1), calls=%async_computation.2 | async-start | bytes 1572864 | tf_op jit(solution)/shard_map/all_to_all | solution.py:160
  121.4 53.1 %collective-permute-start.16 = (bf16[512,3072]{1,0:T(8,128)(2,1)}, bf16[512,3072]{1,0:T(8,128)(2,1)}, u32[]{:S(2)}, u32[]{:S(2)}) collective-permute-start(bf16[512,3072]{1,0:T(8,128)(2,1)} %all-gather.2.cloned.1.call-done), channel_id=1, source_target_pairs={{0,1},{1,0},{2,3},{3,2},{4,5},{5,4},{6,7},{7,6},{8,9},{9,8},{10,11... | collective-permute-start | bytes 9437192 | tf_op jit(solution)/shard_map/ppermute | solution.py:20
  130.5 36.1 %all-to-all-start.3 = ((bf16[256,4,384]{2,1,0:T(4,128)(2,1)}), bf16[256,4,384]{2,1,0:T(4,128)(2,1)S(1)}, u32[]{:S(2)}, u32[]{:S(2)}) async-start(bf16[256,4,384]{2,1,0:T(4,128)(2,1)} %reshape.390), calls=%async_computation.3 | async-start | bytes 1572864 | tf_op jit(solution)/shard_map/all_to_all | solution.py:171
  140.4 7.0 %collective-permute-start.17 = (f32[8,128]{1,0:T(8,128)S(1)}, f32[8,128]{1,0:T(8,128)S(1)}, u32[]{:S(2)}, u32[]{:S(2)}) collective-permute-start(f32[8,128]{1,0:T(8,128)S(1)} %convert_reduce_fusion), channel_id=1, source_target_pairs={{0,64},{64,128},{128,192},{192,0},{1,65},{65,129},{129,193},{193,1... | collective-permute-start | bytes 12296 | tf_op jit(solution)/shard_map/ppermute | solution.py:146
  141.9 5.6 %collective-permute-start.18 = (f32[8,128]{1,0:T(8,128)S(1)}, f32[8,128]{1,0:T(8,128)S(1)}, u32[]{:S(2)}, u32[]{:S(2)}) collective-permute-start(f32[8,128]{1,0:T(8,128)S(1)} %convert_reduce_fusion), channel_id=1, source_target_pairs={{0,128},{64,192},{128,0},{192,64},{1,129},{65,193},{129,1},{193,65... | collective-permute-start | bytes 12296 | tf_op jit(solution)/shard_map/ppermute | solution.py:146
  144.3 3.2 %collective-permute-start.19 = (f32[8,128]{1,0:T(8,128)S(1)}, f32[8,128]{1,0:T(8,128)S(1)}, u32[]{:S(2)}, u32[]{:S(2)}) collective-permute-start(f32[8,128]{1,0:T(8,128)S(1)} %convert_reduce_fusion), channel_id=1, source_target_pairs={{0,192},{64,0},{128,64},{192,128},{1,193},{65,1},{129,65},{193,129... | collective-permute-start | bytes 12296 | tf_op jit(solution)/shard_map/ppermute | solution.py:146
  (6 other events, 6.3 us)
Sparse Core Ops, SparseCore 0:
  39.0 41.0 all-gather.1

commit v2 on v0

v2 whole, which is shorter than its diff:
```python
import jax
import jax.numpy as jnp
from jax import lax
from jax.experimental import pallas as pl
from jax.experimental.pallas import tpu as pltpu
from jax.sharding import Mesh, PartitionSpec as P

HEADS = 8
HEAD_DIM = 128
EPSILON = 1e-05
BF = jnp.bfloat16
F32 = jnp.float32

SEQ = ("yh", "yl", "zh", "zm", "zl", "c")
CUBE = ("yl", "zl", "c")
RUN = ("zh", "zm")
ALL = ("dp",) + SEQ
NN = (((1,), (0,)), ((), ()))
NT = (((1,), (1,)), ((), ()))
TN = (((0,), (0,)), ((), ()))


def swap(x, axes, bit, count):
    return lax.ppermute(x, axes, [(i, i ^ bit) for i in range(count)])


def dot(a, b, dims):
    return lax.dot_general(a, b, dims, preferred_element_type=F32)


def together(*xs):
    return lax.optimization_barrier(xs)


def call(body, outs, *operands, flops=0, scratch=()):
    size = sum(o.size * o.dtype.itemsize for o in (*operands, *outs))
    count, total = len(operands), len(operands) + len(outs)

    def kernel(*refs):
        far, near, (sems, *rest) = refs[:total], refs[total : 2 * total], refs[2 * total :]
        loads = [pltpu.make_async_copy(far[i], near[i], sems.at[i]) for i in range(count)]
        stores = [pltpu.make_async_copy(near[i], far[i], sems.at[i]) for i in range(count, total)]
        waited, started = set(), set()

        def ready(*places):
            for i in places or range(count):
                if i not in waited:
                    loads[i].wait()
                    waited.add(i)

        def finish(*places):
            for i in places or range(len(stores)):
                if i not in started:
                    stores[i].start()
                    started.add(i)

        for load in loads:
            load.start()
        body(ready, finish, *near, *rest)
        ready()
        finish()
        for store in stores:
            store.wait()

    return pl.pallas_call(
        kernel,
        out_shape=[pltpu.HBM(o.shape, o.dtype) for o in outs],
        in_specs=[pl.BlockSpec(memory_space=pltpu.HBM)] * count,
        out_specs=[pl.BlockSpec(memory_space=pltpu.HBM)] * len(outs),
        scratch_shapes=[pltpu.VMEM(o.shape, o.dtype) for o in (*operands, *outs)]
        + [pltpu.SemaphoreType.DMA((total,))]
        + list(scratch),
        cost_estimate=pl.CostEstimate(flops=flops, bytes_accessed=size, transcendentals=0),
        compiler_params=pltpu.CompilerParams(vmem_limit_bytes=60 * 2**20),
    )(*operands)


def shape(dims, dtype):
    return jax.ShapeDtypeStruct(dims, dtype)


def slices(weight, tokens, grad):
    depth, d, half = weight.shape[0], HEAD_DIM, weight.shape[0] // 2
    n, width = tokens.shape

    def kernel(weight, tokens, grad, heads_out, half_out, b0, b1, b2, b3, head, half_near, tok, cols, sems):
        me, core = lax.axis_index(CUBE), lax.axis_index("c")
        loads = [(tokens, tok)]
        for k in range(4):
            at = pl.multiple_of(((me // 2) ^ k) * 2 * d, 2 * d)
            loads.append((grad.at[:, pl.ds(at, 2 * d)], cols.at[k]))
        for part in range(3):
            at = pl.multiple_of((part * HEADS + me) * d, d)
            loads.append((weight.at[:, pl.ds(at, d)], head.at[:, pl.ds(part * d, d)]))
        loads.append((weight.at[pl.ds(pl.multiple_of(core * half, half), half), :], half_near))
        loads = [pltpu.make_async_copy(x, y, sems.at[i]) for i, (x, y) in enumerate(loads)]
        stores = []
        for k, block in enumerate((b0, b1, b2, b3)):
            stores.append((tok, block.at[:, pl.ds(0, width)]))
            stores.append((cols.at[k], block.at[:, pl.ds(width, 2 * d)]))
        for j in range(4):
            stores.append((head, heads_out.at[pl.ds(j * depth, depth), :]))
        stores.append((half_near, half_out))
        stores = [pltpu.make_async_copy(x, y, sems.at[i + len(loads)]) for i, (x, y) in enumerate(stores)]
        for copy in loads:
            copy.start()
        for some, then in ((loads[:5], stores[:8]), (loads[5:8], stores[8:12]), (loads[8:], stores[12:])):
            for copy in some:
                copy.wait()
            for copy in then:
                copy.start()
        for copy in stores:
            copy.wait()

    outs = ((4 * depth, 3 * d), (half, weight.shape[1])) + ((n, width + 2 * d),) * 4
    near = ((depth, 3 * d), (half, weight.shape[1]), (n, width), (4, n, 2 * d))
    return pl.pallas_call(
        kernel,
        out_shape=[pltpu.HBM(o, BF) for o in outs],
        in_specs=[pl.BlockSpec(memory_space=pltpu.HBM)] * 3,
        out_specs=[pl.BlockSpec(memory_space=pltpu.HBM)] * len(outs),
        scratch_shapes=[pltpu.VMEM(o, BF) for o in near] + [pltpu.SemaphoreType.DMA((22,))],
        cost_estimate=pl.CostEstimate(flops=0, bytes_accessed=2**21, transcendentals=0),
        compiler_params=pltpu.CompilerParams(vmem_limit_bytes=60 * 2**20),
    )(weight, tokens, grad)


def project(ready, finish, w, *refs):
    pieces, (query, key, value, states, upstream) = refs[:8], refs[8:]
    n, d = pieces[0].shape[0], HEAD_DIM
    width = w.shape[0]
    me = lax.axis_index(CUBE)
    at = pl.multiple_of(width + lax.axis_index("c") * d, d)
    ready(0)
    for k in range(8):
        ready(1 + k)
        got = dot(pieces[k][:, :width], w[...], NN).astype(BF)
        rows = pl.ds(pl.multiple_of((me ^ k) * n, n), n)
        for part, ref in enumerate((query, key, value)):
            ref[rows, :] = got[:, part * d : (part + 1) * d]
        upstream[rows, :] = pieces[k][:, pl.ds(at, d)]
    finish(0, 1, 2, 4)
    half = 4 * n
    for s in range(2):
        rows = pl.ds(s * half, half)
        states[pl.ds(s * d, d), :] = dot(key[rows, :], value[rows, :], TN).astype(BF)


def below(rows):
    return lax.broadcasted_iota(jnp.int32, (rows, rows), 0) >= lax.broadcasted_iota(jnp.int32, (rows, rows), 1)


def inside(ready, finish, query, key, value, scores, intra):
    ready()
    half = query.shape[0] // 2
    keep = below(half)
    for s in range(2):
        rows = pl.ds(s * half, half)
        got = jnp.where(keep, dot(query[rows, :], key[rows, :], NT), 0.0).astype(BF)
        scores[rows, :] = got
        intra[rows, :] = dot(got, value[rows, :], NN)


def combine(ready, finish, mine, a, b, c, out):
    ready()
    d = HEAD_DIM
    total = mine[...].astype(F32) + a[...].astype(F32) + b[...].astype(F32) + c[...].astype(F32)
    out[:d, :] = (total[:d] + total[d : 2 * d]).astype(BF)
    if out.shape[0] > d:
        out[d:, :] = in_parts(jnp.sum(total[2 * d :], axis=0, keepdims=True))


def in_parts(row):
    high = row.astype(BF).astype(F32)
    middle = (row - high).astype(BF).astype(F32)
    low = row - high - middle
    place = lax.broadcasted_iota(jnp.int32, (16, row.shape[1]), 0)
    return jnp.where(place == 0, high, jnp.where(place == 1, middle, jnp.where(place == 2, low, 0.0))).astype(BF)


def states_at(mine, got, far, backward):
    d = HEAD_DIM
    place = lax.axis_index(RUN)
    total = mine[: 2 * d, :].astype(F32)
    near = jnp.zeros_like(total)
    for k, ref in enumerate(got):
        term = ref[: 2 * d, :].astype(F32)
        source = place ^ (k + 1)
        use = (source > place) if backward else (source < place)
        near = near + jnp.where(use, term, 0.0)
        total = total + term
    yh = lax.axis_index("yh")
    cross = jnp.where((yh == 0) if backward else (yh == 1), far[:d, :].astype(F32), 0.0)
    if backward:
        return near[:d] + total[d:] + cross, near[d:] + cross
    return near[:d] + cross, near[d:] + total[:d] + cross


def forward(
    ready, finish, query, intra, mine, a, b, c, far, upstream, gain, attended, mixed_grad, payload, before
):
    ready()
    d = HEAD_DIM
    half = query.shape[0] // 2
    scale = gain[:, pl.ds(pl.multiple_of(lax.axis_index(CUBE) * d, d), d)].astype(F32)
    gain_part = jnp.zeros((1, d), F32)
    for s, state in enumerate(states_at(mine, (a, b, c), far, False)):
        state = state.astype(BF)
        before[pl.ds(s * d, d), :] = state
        rows = pl.ds(s * half, half)
        mixed = intra[rows, :] + dot(query[rows, :], state, NN)
        inverse_rms = lax.rsqrt(jnp.mean(mixed * mixed, axis=-1, keepdims=True) + EPSILON)
        normed = mixed * inverse_rms
        attended[rows, :] = (scale * normed).astype(BF)
        up = upstream[rows, :].astype(F32)
        product = up * normed
        gain_part = gain_part + jnp.sum(product, axis=0, keepdims=True)
        along = jnp.mean(product * scale, axis=-1, keepdims=True)
        grad = (inverse_rms * (up * scale - normed * along)).astype(BF)
        mixed_grad[rows, :] = grad
        payload[pl.ds(s * d, d), :] = dot(query[rows, :], grad, TN).astype(BF)
    payload[2 * d :, :] = in_parts(gain_part)


def backward_inside(
    ready, finish, query, key, value, scores, mixed_grad, before, attended, sent, key_part, value_part
):
    ready()
    d = HEAD_DIM
    half = query.shape[0] // 2
    keep = below(half)
    for s in range(2):
        rows = pl.ds(s * half, half)
        grad = mixed_grad[rows, :]
        got = jnp.where(keep, dot(grad, value[rows, :], NT), 0.0).astype(BF)
        sent[rows, :d] = attended[rows, :]
        sent[rows, d:] = (dot(got, key[rows, :], NN) + dot(grad, before[pl.ds(s * d, d), :], NT)).astype(BF)
        key_part[rows, :] = dot(got, query[rows, :], TN)
        value_part[rows, :] = dot(scores[rows, :], grad, TN)


def backward_rest(ready, finish, key, value, sent, key_part, value_part, mine, a, b, c, far, late, joined):
    ready()
    d = HEAD_DIM
    n = key.shape[0] // 8
    half = 4 * n
    terms = jnp.zeros((16, d), F32)
    for ref in (mine, a, b, c):
        terms = terms + ref[2 * d :, :].astype(F32)
    gain = in_parts(jnp.sum(terms + far[d:, :].astype(F32), axis=0, keepdims=True))
    joined[:, :d] = sent[:, d:]
    for s, state in enumerate(states_at(mine, (a, b, c), far, True)):
        state = state.astype(BF)
        rows = pl.ds(s * half, half)
        key_grad = (key_part[rows, :] + dot(value[rows, :], state, NT)).astype(BF)
        value_grad = (value_part[rows, :] + dot(key[rows, :], state, NN)).astype(BF)
        joined[rows, d : 2 * d] = key_grad
        joined[rows, 2 * d :] = value_grad
        for i in range(4):
            late[s * 4 + i, :n, : 2 * d] = sent[pl.ds(s * half + i * n, n), :]
            late[s * 4 + i, :n, 2 * d : 3 * d] = key_grad[i * n : (i + 1) * n]
            late[s * 4 + i, :n, 3 * d :] = value_grad[i * n : (i + 1) * n]
    for h in range(HEADS):
        late[h, n:, :d] = gain
        late[h, n:, d:] = jnp.zeros((16, 3 * d), BF)


def weigh(ready, finish, joined, *refs):
    pieces, (out, order, turned) = refs[:8], refs[8:]
    n, width = joined.shape[0] // 8, out.shape[0]
    me = lax.axis_index(CUBE)
    ready(0)
    for k in range(8):
        order[k * n : (k + 1) * n, :] = joined[pl.ds(pl.multiple_of((me ^ k) * n, n), n), :]
    for k in range(8):
        ready(1 + k)
        turned[:, k * n : (k + 1) * n] = pieces[k][:, :width].T
    out[...] = dot(turned[...], order[...], NN).astype(BF)


def at_home(ready, finish, late, mine, other, out, attended, gains, joined):
    ready(0)
    n = out.shape[0]
    d = HEAD_DIM
    for h in range(HEADS):
        attended[:, h * d : (h + 1) * d] = late[h, :n, :d]
        joined[h] = late[h, :n, d:]
        terms = jnp.sum(late[h, n:, :d].astype(F32), axis=0, keepdims=True)
        gains[h] = jnp.broadcast_to(terms, (8, d))
    finish(1, 2)
    ready()
    rows = jnp.concatenate(
        [joined[h, :, part * d : (part + 1) * d] for part in range(3) for h in range(HEADS)], axis=1
    )
    first = dot(rows, mine[...], NT).astype(BF)
    second = dot(rows, other[...], NT).astype(BF)
    width = mine.shape[0] // 4
    even = lax.axis_index("c") == 0
    for p in range(4):
        x, y = first[:, p * width : (p + 1) * width], second[:, p * width : (p + 1) * width]
        out[:, 2 * p * width : (2 * p + 1) * width] = jnp.where(even, x, y)
        out[:, (2 * p + 1) * width : (2 * p + 2) * width] = jnp.where(even, y, x)


def add_first(ready, finish, pieces, out):
    ready()
    rows = pieces.shape[0] // 16
    for yl in range(2):
        total = sum(
            pieces[pl.ds(((dp * 2 + yh) * 2 + yl) * rows, rows), :].astype(F32) for dp in range(4) for yh in range(2)
        )
        for j in range(16):
            out[j * 8 + yl * 4 : j * 8 + yl * 4 + 4, :] = total[j * 4 : j * 4 + 4, :]


def add_up(ready, finish, pieces, g0, g1, g2, g3, weight_grad, gain_grad):
    ready()
    d = HEAD_DIM
    for low in range(4):
        total = sum(pieces[pl.ds((run * 4 + low) * 8, 8), :] for run in range(4)) / 4
        for yl in range(2):
            for part in range(3):
                at = (part * HEADS + yl * 4 + low) * d
                weight_grad[:, at : at + d] = total[yl * 4 : yl * 4 + 4, part * d : (part + 1) * d]
    for h in range(HEADS):
        gain_grad[h : h + 1, :] = sum(ref[h, :1, :] for ref in (g0, g1, g2, g3)) / 4


def local(tokens, qkv_weight, out_gain, out_grad):
    replicas = lax.axis_size("dp")
    d = HEAD_DIM
    block = tokens[0]
    n, width = block.shape
    inner = out_gain.shape[0]
    depth = qkv_weight.shape[0]

    w_heads, w_half, *blocks = slices(qkv_weight, block, out_grad[0])
    near = [swap(blocks[bit], ("yl", "zl"), bit, 4) for bit in (1, 2, 3)]
    w_cols = lax.all_to_all(w_heads, "dp", 0, 0, tiled=True)
    mine, _ = together(blocks[0], near[0])
    pieces = [x for side in [mine] + near for x in (side, swap(side, "c", 1, 2))]

    rows = 8 * n
    column, square = shape((rows, d), BF), shape((2 * d, d), BF)
    query, key, value, states, upstream = call(
        project, (column, column, column, square, column), w_cols, *pieces,
        flops=2 * rows * width * 3 * d,
    )
    w_half, _ = together(w_half, states)
    w_mine = lax.all_gather(w_half, "dp", axis=0, tiled=True)
    scores, intra = call(
        inside, (shape((rows, rows // 2), BF), shape((rows, d), F32)), query, key, value, flops=2 * rows * rows * d
    )
    got = [swap(states, RUN, bit, 4) for bit in (1, 2, 3)]
    (both,) = call(combine, (shape((d, d), BF),), states, *got)
    far = swap(both, "yh", 1, 2)
    attended_head, mixed_grad, payload, before = call(
        forward, (column, column, shape((2 * d + 16, d), BF), square),
        query, intra, states, *got, far, upstream, out_gain.reshape(1, inner), flops=4 * rows * d * d,
    )
    grads = [swap(payload, RUN, bit, 4) for bit in (1, 2, 3)]
    (both_grad,) = call(combine, (shape((d + 16, d), BF),), payload, *grads)
    mixed_grad, both_grad = together(mixed_grad, both_grad)
    sent, key_part, value_part = call(
        backward_inside, (shape((rows, 2 * d), BF), shape((rows, d), F32), shape((rows, d), F32)),
        query, key, value, scores, mixed_grad, before, attended_head, flops=4 * rows * rows * d,
    )
    far_grad = swap(both_grad, "yh", 1, 2)
    late, joined = call(
        backward_rest, (shape((HEADS, n + 16, 4 * d), BF), shape((rows, 3 * d), BF)),
        key, value, sent, key_part, value_part, payload, *grads, far_grad, flops=8 * rows * d * d,
    )
    late = lax.all_to_all(late, CUBE, 0, 0, tiled=True)
    (weight_part,) = call(
        weigh, (shape((width, 3 * d), BF),), joined, *pieces,
        flops=2 * rows * width * 3 * d,
        scratch=[pltpu.VMEM((rows, 3 * d), BF), pltpu.VMEM((width, rows), BF)],
    )
    w_mine, _ = together(w_mine, weight_part)
    w_other = swap(w_mine, "c", 1, 2)
    weight_part, _ = together(weight_part, late)
    sums = lax.all_to_all(weight_part, ("dp", "yh", "yl"), 0, 0, tiled=True)
    input_grad, attended, gains = call(
        at_home, (shape((n, width), BF), shape((n, inner), BF), shape((HEADS, 8, d), F32)), late, w_mine, w_other,
        flops=2 * n * width * 3 * inner, scratch=[pltpu.VMEM((HEADS, n, 3 * d), BF)],
    )
    sums, _ = together(sums, gains)
    (sums,) = call(add_first, (shape((rows // 8, 3 * d), F32),), sums)
    sums = lax.all_to_all(sums, ("zh", "zm", "zl", "c"), 0, 0, tiled=True)
    gains = [gains] + [swap(gains, "dp", bit, replicas) for bit in (1, 2, 3)]
    weight_grad, gain_grad = call(
        add_up, (shape((width // 256, 3 * inner), F32), shape((HEADS, d), F32)), sums, *gains
    )
    return (attended[None], input_grad[None], weight_grad, gain_grad.reshape(inner))


def solution(mesh):
    fine = Mesh(mesh.devices.reshape(mesh.devices.shape[0], 2, 2, 2, 2, 2, 2), ALL)
    rows = P("dp", SEQ, None)
    return jax.shard_map(
        local,
        mesh=fine,
        in_specs=(rows, P("dp", None), P(), rows),
        out_specs=(rows, rows, P(ALL, None), P()),
        check_vma=False,
    )
```

time: 724 us -> 162 us (0.22)
  waiting for transfers between devices: 535 us -> 26.8 us
  other arithmetic: 70.6 us -> 0 us
  starting transfers between devices: 0.16 us -> 55.3 us
  blocking collectives: 74.7 us -> 20.2 us
  Pallas kernels: 0 us -> 38.4 us
  matrix products: 21.9 us -> 0 us
    all_gather x3 -> x1, waiting for transfers between devices: 336 us -> 0.02 us  [local(): w_mine = lax.all_gather(w_half, 'dp', axis=0, tiled=True)]
    unnamed x5 -> x1, waiting for transfers between devices: 200 us -> 0.02 us
    psum x1 -> x0, blocking collectives: 74.7 us -> none  [local(): gain_total = lax.psum(gain_local, ('dp', 'seq')) / replicas]
    add x63 -> x0, other arithmetic: 67.4 us -> none  [add_states(): return earlier + later]
    ppermute x0 -> x19, starting transfers between devices: none -> 38.7 us  [swap(): return lax.ppermute(x, axes, [(i, i ^ bit) for i in range(count)])]
    pallas_call x0 -> x12, Pallas kernels: none -> 38.4 us  [the longest x11 35.6 us: call(): pl.pallas_call(kernel, out_shape=[pltpu.HBM(o.shape, o.dtype) for o in ou...]
    dot_general x15 -> x0, matrix products: 21.9 us -> none  [the longest x1 6.27 us: local(): lax.dot_general(inputs, projected_grad, (((0,), (0,)), ((), ())), preferr...]
    all_to_all x0 -> x1, blocking collectives: none -> 20.2 us  [local(): late = lax.all_to_all(late, CUBE, 0, 0, tiled=True)]
  transfers between devices with their start and end apart: 4 -> 23, of which waited for: 4 -> 11; matrix products, arithmetic and copies ran while one was open for 1% -> 0% of each run, Pallas kernels for 0% -> 17%
where the time goes in v2:
time: 162 us; the launch traced here: 161 us
  starting transfers between devices  55.3 us (34%)
  Pallas kernels  38.4 us (24%)
  waiting for transfers between devices  26.8 us (17%)
  blocking collectives  20.2 us (12%)
  between operations  14.3 us (9%)
  local copies, waits for them, and re-layouts  6.13 us (4%)
    ppermute x19, starting transfers between devices, swap(): return lax.ppermute(x, axes, [(i, i ^ bit) for i in range(count)])  38.7 us
    pallas_call x11, Pallas kernels, call(): pl.pallas_call(kernel, out_shape=[pltpu.HBM(o.shape, o.dtype) for o in ou...  35.6 us
    all_to_all x1, blocking collectives, local(): late = lax.all_to_all(late, CUBE, 0, 0, tiled=True)  20.2 us
    ppermute x19, waiting for transfers between devices, swap(): return lax.ppermute(x, axes, [(i, i ^ bit) for i in range(count)])  18 us
    all_to_all x1, starting transfers between devices, local(): sums = lax.all_to_all(sums, ('zh', 'zm', 'zl', 'c'), 0, 0, tiled=True)  7.24 us
    unnamed x46, local copies, waits for them, and re-layouts  5.54 us
    all_to_all x1, starting transfers between devices, local(): sums = lax.all_to_all(weight_part, ('dp', 'yh', 'yl'), 0, 0, tiled=True)  5.36 us
    all_to_all x1, waiting for transfers between devices, local(): sums = lax.all_to_all(weight_part, ('dp', 'yh', 'yl'), 0, 0, tiled=True)  4.88 us
  transfers between devices with their start and end apart: 23, of which 11 were waited for; matrix products, arithmetic and copies ran while one was open for 0% of the time, Pallas kernels for 17%

profile of v2, /device:TPU:1, one launch (start us, length us, event | category | flops | bytes accessed | tf_op | source)
XLA Modules:
  0.0 161.1 jit_solution(11552728401849373192)
XLA Ops:
  7.2 2.8 %shard_map.75 = (bf16[1024,384]{1,0:T(8,128)(2,1)}, bf16[128,3072]{1,0:T(8,128)(2,1)}, bf16[128,1280]{1,0:T(8,128)(2,1)}, bf16[128,1280]{1,0:T(8,128)(2,1)}, bf1...) custom-call(bf16[256,3072]{1,0:T(8,128)(2,1)} %weight.1, bf16[128,1024]{1,0:T(8,128)(2,1)} %bitcast.16, ...), custom_call_target="tpu_custom_call" | custom-call | bytes 2097152 | tf_op jit(solution)/shard_map/pallas_call | solution.py:117
  9.9 2.6 %collective-permute-start = (bf16[128,1280]{1,0:T(8,128)(2,1)}, bf16[128,1280]{1,0:T(8,128)(2,1)S(1)}, u32[]{:S(2)}, u32[]{:S(2)}) collective-permute-start(bf16[128,1280]{1,0:T(8,128)(2,1)} %get-tuple-element.40), channel_id=1, source_target_pairs={{0,2},{2,0},{16,18},{18,16},{1,3},{3,1},{17,19},{19,17},{4,6},{6,4... | collective-permute-start | bytes 983048 | tf_op jit(solution)/shard_map/ppermute | solution.py:24
  13.8 4.0 %all-to-all-start = ((bf16[4,256,384]{2,1,0:T(8,128)(2,1)}), bf16[4,256,384]{2,1,0:T(8,128)(2,1)S(1)}, u32[]{:S(2)}, u32[]{:S(2)}) async-start(bf16[4,256,384]{2,1,0:T(8,128)(2,1)} %bitcast.13), calls=%async_computation | async-start | bytes 1572864 | tf_op jit(solution)/shard_map/all_to_all | solution.py:339
  19.2 4.9 %collective-permute-start.1 = (bf16[128,1280]{1,0:T(8,128)(2,1)S(1)}, bf16[128,1280]{1,0:T(8,128)(2,1)S(1)}, u32[]{:S(2)}, u32[]{:S(2)}) collective-permute-start(bf16[128,1280]{1,0:T(8,128)(2,1)S(1)} %copy-done.2), channel_id=1, source_target_pairs={{0,1},{1,0},{2,3},{3,2},{4,5},{5,4},{6,7},{7,6},{8,9},{9,8},{10,11... | collective-permute-start | bytes 983048 | tf_op jit(solution)/shard_map/ppermute | solution.py:24
  24.2 5.6 %collective-permute-start.4 = (bf16[128,1280]{1,0:T(8,128)(2,1)S(1)}, bf16[128,1280]{1,0:T(8,128)(2,1)S(1)}, u32[]{:S(2)}, u32[]{:S(2)}) collective-permute-start(bf16[128,1280]{1,0:T(8,128)(2,1)S(1)} %collective-permute-done.3.refs_5_), channel_id=1, source_target_pairs={{0,1},{1,0},{2,3},{3,2},{4,5},{5,4},{6,7},{7,6},{8,9},{9,8},{10,11... | collective-permute-start | bytes 983048 | tf_op jit(solution)/shard_map/ppermute | solution.py:24
  32.3 4.7 %shard_map.76 = (bf16[1024,128]{1,0:T(8,128)(2,1)}, bf16[1024,128]{1,0:T(8,128)(2,1)}, bf16[1024,128]{1,0:T(8,128)(2,1)}, bf16[256,128]{1,0:T(8,128)(2,1)}, bf16[1024,128]{1,0:T(8,128)(2,1)}) custom-call(bf16[1024,384]{1,0:T(8,128)(2,1)} %bitcast.12, bf16[128,1280]{1,0:T(8,128)(2,1)} %get-tuple-element.41.refs_1_, bf16[128,1280]{1,0:T(8,128)(2,1)} %copy-done.6, ...), custom_call_target="tpu_custom_call" | custom-call | flops 805306368 | bytes 4521984 | tf_op jit(solution)/shard_map/pallas_call | solution.py:65
  37.1 3.1 %collective-permute-start.7 = (bf16[256,128]{1,0:T(8,128)(2,1)}, bf16[256,128]{1,0:T(8,128)(2,1)S(1)}, u32[]{:S(2)}, u32[]{:S(2)}) collective-permute-start(bf16[256,128]{1,0:T(8,128)(2,1)} %get-tuple-element.49.refs_0_.refs_2_), channel_id=1, source_target_pairs={{0,4},{4,0},{8,12},{12,8},{1,5},{5,1},{9,13},{13,9},{2,6},{6,2},{1... | collective-permute-start | bytes 196616 | tf_op jit(solution)/shard_map/ppermute | solution.py:24
  40.2 4.0 %collective-permute-start.8 = (bf16[256,128]{1,0:T(8,128)(2,1)}, bf16[256,128]{1,0:T(8,128)(2,1)S(1)}, u32[]{:S(2)}, u32[]{:S(2)}) collective-permute-start(bf16[256,128]{1,0:T(8,128)(2,1)} %get-tuple-element.49.refs_0_.refs_2_), channel_id=1, source_target_pairs={{0,8},{4,12},{8,0},{12,4},{1,9},{5,13},{9,1},{13,5},{2,10},{6,14},... | collective-permute-start | bytes 196616 | tf_op jit(solution)/shard_map/ppermute | solution.py:24
  44.2 4.2 %collective-permute-done.8.refs_2_.refs_4_ = bf16[256,128]{1,0:T(8,128)(2,1)S(1)} collective-permute-done((bf16[256,128]{1,0:T(8,128)(2,1)}, bf16[256,128]{1,0:T(8,128)(2,1)S(1)}, u32[]{:S(2)}, u32[]{:S(2)}) %collective-permute-start.8) | collective-permute-done | bytes 65568 | tf_op jit(solution)/shard_map/ppermute | solution.py:24
  50.6 1.7 %shard_map.78 = bf16[128,128]{1,0:T(8,128)(2,1)} custom-call(bf16[256,128]{1,0:T(8,128)(2,1)} %get-tuple-element.49.refs_0_.refs_2_, bf16[256,128]{1,0:T(8,128)(2,1)} %copy-done.14, bf16[256,128]{1,0:T(8,128)(2,1)} %copy-done.15, bf16[256,128]{1,0:T(8,128)(2,1)} %copy-done.16), custom_call_target="tpu_custom_call" | custom-call | bytes 294912 | tf_op jit(solution)/shard_map/pallas_call | solution.py:65
  52.3 2.7 %collective-permute-start.10 = (bf16[128,128]{1,0:T(8,128)(2,1)}, bf16[128,128]{1,0:T(8,128)(2,1)S(1)}, u32[]{:S(2)}, u32[]{:S(2)}) collective-permute-start(bf16[128,128]{1,0:T(8,128)(2,1)} %shard_map.78), channel_id=1, source_target_pairs={{0,32},{32,0},{1,33},{33,1},{2,34},{34,2},{3,35},{35,3},{4,36},{36... | collective-permute-start | bytes 98312 | tf_op jit(solution)/shard_map/ppermute | solution.py:24
  55.6 3.0 %shard_map.77 = (bf16[1024,512]{1,0:T(8,128)(2,1)}, f32[1024,128]{1,0:T(8,128)}) custom-call(bf16[1024,128]{1,0:T(8,128)(2,1)} %get-tuple-element.46.refs_0_, bf16[1024,128]{1,0:T(8,128)(2,1)} %get-tuple-element.44.refs_1_.refs_0_, bf16[1024,128]{1,0:T(8,128)(2,1)} %get-tuple-element.45.refs_2_.refs_1_), custom_call_target="tpu_custom_call" | custom-call | flops 268435456 | bytes 2359296 | tf_op jit(solution)/shard_map/pallas_call | solution.py:65
  59.3 2.8 %shard_map.79 = (bf16[1024,128]{1,0:T(8,128)(2,1)}, bf16[1024,128]{1,0:T(8,128)(2,1)}, bf16[272,128]{1,0:T(8,128)(2,1)}, bf16[256,128]{1,0:T(8,128)(2,1)}) custom-call(bf16[1024,128]{1,0:T(8,128)(2,1)} %get-tuple-element.46.refs_0_, f32[1024,128]{1,0:T(8,128)} %get-tuple-element.48.refs_1_, bf16[256,128]{1,0:T(8,128)(2,1)} %get-tuple-element.49.refs_0_.refs_2_, ...), custom_call_target="tpu_custom_call" | custom-call | flops 67108864 | bytes 2004992 | tf_op jit(solution)/shard_map/pallas_call | solution.py:65
  62.9 5.6 %collective-permute-start.12 = (bf16[272,128]{1,0:T(8,128)(2,1)}, bf16[272,128]{1,0:T(8,128)(2,1)S(1)}, u32[]{:S(2)}, u32[]{:S(2)}) collective-permute-start(bf16[272,128]{1,0:T(8,128)(2,1)} %get-tuple-element.52.refs_0_.refs_5_), channel_id=1, source_target_pairs={{0,8},{4,12},{8,0},{12,4},{1,9},{5,13},{9,1},{13,5},{2,10},{6,14},... | collective-permute-start | bytes 208904 | tf_op jit(solution)/shard_map/ppermute | solution.py:24
  68.6 2.7 %collective-permute-done.12.refs_2_.refs_7_ = bf16[272,128]{1,0:T(8,128)(2,1)S(1)} collective-permute-done((bf16[272,128]{1,0:T(8,128)(2,1)}, bf16[272,128]{1,0:T(8,128)(2,1)S(1)}, u32[]{:S(2)}, u32[]{:S(2)}) %collective-permute-start.12) | collective-permute-done | bytes 69664 | tf_op jit(solution)/shard_map/ppermute | solution.py:24
  71.3 3.9 %collective-permute-done.13.refs_3_.refs_8_ = bf16[272,128]{1,0:T(8,128)(2,1)S(1)} collective-permute-done((bf16[272,128]{1,0:T(8,128)(2,1)}, bf16[272,128]{1,0:T(8,128)(2,1)S(1)}, u32[]{:S(2)}, u32[]{:S(2)}) %collective-permute-start.13) | collective-permute-done | bytes 69664 | tf_op jit(solution)/shard_map/ppermute | solution.py:24
  75.8 1.7 %shard_map.80 = bf16[144,128]{1,0:T(8,128)(2,1)} custom-call(bf16[272,128]{1,0:T(8,128)(2,1)} %get-tuple-element.52.refs_0_.refs_5_, bf16[272,128]{1,0:T(8,128)(2,1)} %copy-done.11, bf16[272,128]{1,0:T(8,128)(2,1)} %copy-done.12, bf16[272,128]{1,0:T(8,128)(2,1)} %copy-done.13), custom_call_target="tpu_custom_call" | custom-call | bytes 315392 | tf_op jit(solution)/shard_map/pallas_call | solution.py:65
  78.5 4.1 %shard_map.81 = (bf16[1024,256]{1,0:T(8,128)(2,1)}, f32[1024,128]{1,0:T(8,128)}, f32[1024,128]{1,0:T(8,128)}) custom-call(bf16[1024,128]{1,0:T(8,128)(2,1)} %get-tuple-element.46.refs_0_, bf16[1024,128]{1,0:T(8,128)(2,1)} %get-tuple-element.44.refs_1_.refs_0_, bf16[1024,128]{1,0:T(8,128)(2,1)} %get-tuple-element.45.refs_2_.refs_1_, ...), custom_call_target="tpu_custom_call" | custom-call | flops 536870912 | bytes 3997696 | tf_op jit(solution)/shard_map/pallas_call | solution.py:65
  83.3 3.4 %shard_map.82 = (bf16[8,144,512]{2,1,0:T(8,128)(2,1)}, bf16[1024,384]{1,0:T(8,128)(2,1)}) custom-call(bf16[1024,128]{1,0:T(8,128)(2,1)} %get-tuple-element.44.refs_1_.refs_0_, bf16[1024,128]{1,0:T(8,128)(2,1)} %get-tuple-element.45.refs_2_.refs_1_, bf16[1024,256]{1,0:T(8,128)(2,1)} %get-tuple-element.56.refs_2_, f32[1024,128]{1,0:T(8,128)} %get-tuple-element.57.refs_3_, ...), custom_call_target="tpu_custom_call" | custom-call | flops 134217728 | bytes 4378624 | tf_op jit(solution)/shard_map/pallas_call | solution.py:65
  86.6 4.4 %shard_map.83 = bf16[1024,384]{1,0:T(8,128)(2,1)} custom-call(bf16[1024,384]{1,0:T(8,128)(2,1)} %get-tuple-element.63.refs_0_, bf16[128,1280]{1,0:T(8,128)(2,1)} %get-tuple-element.41.refs_1_, bf16[128,1280]{1,0:T(8,128)(2,1)} %copy-done.6, bf16[128,1280]{1,0:T(8,128)(2,1)} %copy-done.3, bf16[128,1280]{1,0:T(8,128)(2,1)} %copy-done.7, ...), custom_call_target="tpu_custom_call" | custom-call | flops 805306368 | bytes 4194304 | tf_op jit(solution)/shard_map/pallas_call | solution.py:65
  91.1 2.9 %collective-permute-start.15 = (bf16[512,3072]{1,0:T(8,128)(2,1)}, bf16[512,3072]{1,0:T(8,128)(2,1)S(1)}, u32[]{:S(2)}, u32[]{:S(2)}) collective-permute-start(bf16[512,3072]{1,0:T(8,128)(2,1)} %all-gather.2.cloned.1.call-done.refs_1_), channel_id=1, source_target_pairs={{0,1},{1,0},{2,3},{3,2},{4,5},{5,4},{6,7},{7,6},{8,9},{9,8},{10,11... | collective-permute-start | bytes 9437192 | tf_op jit(solution)/shard_map/ppermute | solution.py:24
  94.0 20.2 %all_to_all.39.refs_0_ = bf16[8,144,512]{2,1,0:T(8,128)(2,1)} all-to-all(bf16[8,144,512]{2,1,0:T(8,128)(2,1)} %get-tuple-element.60), channel_id=1, replica_groups=mesh['dp'=4,'yh'=2,'yl'=2,'zh'=2,'zm'=2,'zl'=2,'c'=2] {'yl','zl','c'}, dimensions={0} | all-to-all | bytes 2359296 | tf_op jit(solution)/shard_map/all_to_all | solution.py:373
  114.2 5.4 %all-to-all-start.2 = ((bf16[16,64,384]{2,1,0:T(8,128)(2,1)}), bf16[16,64,384]{2,1,0:T(8,128)(2,1)}, u32[]{:S(2)}, u32[]{:S(2)}) async-start(bf16[16,64,384]{2,1,0:T(8,128)(2,1)} %bitcast.11), calls=%async_computation.2 | async-start | bytes 1572864 | tf_op jit(solution)/shard_map/all_to_all | solution.py:382
  119.6 1.7 %copy-done = bf16[512,3072]{1,0:T(8,128)(2,1)} copy-done((bf16[512,3072]{1,0:T(8,128)(2,1)}, bf16[512,3072]{1,0:T(8,128)(2,1)S(1)}, u32[]{:S(2)}) %copy-start) | copy-done | bytes 3145752
  121.2 6.3 %shard_map.84 = (bf16[128,1024]{1,0:T(8,128)(2,1)}, bf16[128,1024]{1,0:T(8,128)(2,1)}, f32[8,8,128]{2,1,0:T(8,128)}) custom-call(bf16[8,144,512]{2,1,0:T(8,128)(2,1)} %all_to_all.39.refs_0_, bf16[512,3072]{1,0:T(8,128)(2,1)} %all-gather.2.cloned.1.call-done.refs_1_, bf16[512,3072]{1,0:T(8,128)(2,1)} %copy-done), custom_call_target="tpu_custom_call" | custom-call | flops 805306368 | bytes 8028160 | tf_op jit(solution)/shard_map/pallas_call | solution.py:65
  127.5 4.9 %all-to-all-done.2 = bf16[16,64,384]{2,1,0:T(8,128)(2,1)} async-done(((bf16[16,64,384]{2,1,0:T(8,128)(2,1)}), bf16[16,64,384]{2,1,0:T(8,128)(2,1)}, u32[]{:S(2)}, u32[]{:S(2)}) %all-to-all-start.2) | async-done | bytes 786464 | tf_op jit(solution)/shard_map/all_to_all | solution.py:382
  132.4 1.9 %shard_map.85 = f32[128,384]{1,0:T(8,128)} custom-call(bf16[1024,384]{1,0:T(8,128)(2,1)} %bitcast.7.refs_0_), custom_call_target="tpu_custom_call" | custom-call | bytes 983040 | tf_op jit(solution)/shard_map/pallas_call | solution.py:65
  134.3 7.2 %all-to-all-start.3 = ((f32[16,8,384]{2,1,0:T(8,128)}), f32[16,8,384]{2,1,0:T(8,128)S(1)}, u32[]{:S(2)}, u32[]{:S(2)}) async-start(f32[16,8,384]{2,1,0:T(8,128)} %bitcast.15), calls=%async_computation.3 | async-start | bytes 393216 | tf_op jit(solution)/shard_map/all_to_all | solution.py:389
  141.6 2.0 %collective-permute-start.17 = (f32[8,8,128]{2,1,0:T(8,128)}, f32[8,8,128]{2,1,0:T(8,128)S(1)}, u32[]{:S(2)}, u32[]{:S(2)}) collective-permute-start(f32[8,8,128]{2,1,0:T(8,128)} %get-tuple-element.68.refs_1_), channel_id=1, source_target_pairs={{0,128},{64,192},{128,0},{192,64},{1,129},{65,193},{129,1},{193,65... | collective-permute-start | bytes 98312 | tf_op jit(solution)/shard_map/ppermute | solution.py:24
  143.6 1.9 %collective-permute-start.18 = (f32[8,8,128]{2,1,0:T(8,128)}, f32[8,8,128]{2,1,0:T(8,128)S(1)}, u32[]{:S(2)}, u32[]{:S(2)}) collective-permute-start(f32[8,8,128]{2,1,0:T(8,128)} %get-tuple-element.68.refs_1_), channel_id=1, source_target_pairs={{0,192},{64,128},{128,64},{192,0},{1,193},{65,129},{129,65},{193,1... | collective-permute-start | bytes 98312 | tf_op jit(solution)/shard_map/ppermute | solution.py:24
  146.1 1.9 %collective-permute-done.18.refs_4_ = f32[8,8,128]{2,1,0:T(8,128)S(1)} collective-permute-done((f32[8,8,128]{2,1,0:T(8,128)}, f32[8,8,128]{2,1,0:T(8,128)S(1)}, u32[]{:S(2)}, u32[]{:S(2)}) %collective-permute-start.18) | collective-permute-done | bytes 32800 | tf_op jit(solution)/shard_map/ppermute | solution.py:24
  148.0 3.9 %all-to-all-done.3 = f32[16,8,384]{2,1,0:T(8,128)S(1)} async-done(((f32[16,8,384]{2,1,0:T(8,128)}), f32[16,8,384]{2,1,0:T(8,128)S(1)}, u32[]{:S(2)}, u32[]{:S(2)}) %all-to-all-start.3) | async-done | bytes 196640 | tf_op jit(solution)/shard_map/all_to_all | solution.py:389
  (75 shorter events, 14.8 us)
Async XLA Ops:
  9.9 9.3 %copy-start.2 = (bf16[128,1280]{1,0:T(8,128)(2,1)S(1)}, bf16[128,1280]{1,0:T(8,128)(2,1)}, u32[]{:S(2)}) copy-start(bf16[128,1280]{1,0:T(8,128)(2,1)} %get-tuple-element.41.refs_1_) | copy-start | bytes 983044
  9.9 9.2 %collective-permute-start = (bf16[128,1280]{1,0:T(8,128)(2,1)}, bf16[128,1280]{1,0:T(8,128)(2,1)S(1)}, u32[]{:S(2)}, u32[]{:S(2)}) collective-permute-start(bf16[128,1280]{1,0:T(8,128)(2,1)} %get-tuple-element.40), channel_id=1, source_target_pairs={{0,2},{2,0},{16,18},{18,16},{1,3},{3,1},{17,19},{19,17},{4,6},{6,4... | collective-permute-start | bytes 983048 | tf_op jit(solution)/shard_map/ppermute | solution.py:24
  12.5 11.7 %collective-permute-start.3 = (bf16[128,1280]{1,0:T(8,128)(2,1)}, bf16[128,1280]{1,0:T(8,128)(2,1)S(1)}, u32[]{:S(2)}, u32[]{:S(2)}) collective-permute-start(bf16[128,1280]{1,0:T(8,128)(2,1)} %get-tuple-element.42), channel_id=1, source_target_pairs={{0,16},{2,18},{16,0},{18,2},{1,17},{3,19},{17,1},{19,3},{4,20},{6,... | collective-permute-start | bytes 983048 | tf_op jit(solution)/shard_map/ppermute | solution.py:24
  13.8 16.1 %collective-permute-start.5 = (bf16[128,1280]{1,0:T(8,128)(2,1)}, bf16[128,1280]{1,0:T(8,128)(2,1)S(1)}, u32[]{:S(2)}, u32[]{:S(2)}) collective-permute-start(bf16[128,1280]{1,0:T(8,128)(2,1)} %get-tuple-element.43), channel_id=1, source_target_pairs={{0,18},{2,16},{16,2},{18,0},{1,19},{3,17},{17,3},{19,1},{4,22},{6,... | collective-permute-start | bytes 983048 | tf_op jit(solution)/shard_map/ppermute | solution.py:24
  13.8 16.2 %all-to-all-start = ((bf16[4,256,384]{2,1,0:T(8,128)(2,1)}), bf16[4,256,384]{2,1,0:T(8,128)(2,1)S(1)}, u32[]{:S(2)}, u32[]{:S(2)}) async-start(bf16[4,256,384]{2,1,0:T(8,128)(2,1)} %bitcast.13), calls=%async_computation | async-start | bytes 1572864 | tf_op jit(solution)/shard_map/all_to_all | solution.py:339
  17.8 73.3 %all-gather.2.cloned.1.call-start = ((), (), s32[]{:S(2)}) async-start(), calls=%async_computation.4 | async-start | bytes 3932160 | tf_op jit(solution)/shard_map/all_gather | solution.py:350
  19.2 12.4 %copy-start.3 = (bf16[128,1280]{1,0:T(8,128)(2,1)}, bf16[128,1280]{1,0:T(8,128)(2,1)S(1)}, u32[]{:S(2)}) copy-start(bf16[128,1280]{1,0:T(8,128)(2,1)S(1)} %collective-permute-done.refs_3_) | copy-start | bytes 983044
  19.2 10.8 %collective-permute-start.1 = (bf16[128,1280]{1,0:T(8,128)(2,1)S(1)}, bf16[128,1280]{1,0:T(8,128)(2,1)S(1)}, u32[]{:S(2)}, u32[]{:S(2)}) collective-permute-start(bf16[128,1280]{1,0:T(8,128)(2,1)S(1)} %copy-done.2), channel_id=1, source_target_pairs={{0,1},{1,0},{2,3},{3,2},{4,5},{5,4},{6,7},{7,6},{8,9},{9,8},{10,11... | collective-permute-start | bytes 983048 | tf_op jit(solution)/shard_map/ppermute | solution.py:24
  24.1 5.8 %collective-permute-start.2 = (bf16[128,1280]{1,0:T(8,128)(2,1)S(1)}, bf16[128,1280]{1,0:T(8,128)(2,1)S(1)}, u32[]{:S(2)}, u32[]{:S(2)}) collective-permute-start(bf16[128,1280]{1,0:T(8,128)(2,1)S(1)} %collective-permute-done.refs_3_), channel_id=1, source_target_pairs={{0,1},{1,0},{2,3},{3,2},{4,5},{5,4},{6,7},{7,6},{8,9},{9,8},{10,11... | collective-permute-start | bytes 983048 | tf_op jit(solution)/shard_map/ppermute | solution.py:24
  24.2 7.4 %copy-start.4 = (bf16[128,1280]{1,0:T(8,128)(2,1)}, bf16[128,1280]{1,0:T(8,128)(2,1)S(1)}, u32[]{:S(2)}) copy-start(bf16[128,1280]{1,0:T(8,128)(2,1)S(1)} %collective-permute-done.3.refs_5_) | copy-start | bytes 983044
  24.2 6.9 %collective-permute-start.4 = (bf16[128,1280]{1,0:T(8,128)(2,1)S(1)}, bf16[128,1280]{1,0:T(8,128)(2,1)S(1)}, u32[]{:S(2)}, u32[]{:S(2)}) collective-permute-start(bf16[128,1280]{1,0:T(8,128)(2,1)S(1)} %collective-permute-done.3.refs_5_), channel_id=1, source_target_pairs={{0,1},{1,0},{2,3},{3,2},{4,5},{5,4},{6,7},{7,6},{8,9},{9,8},{10,11... | collective-permute-start | bytes 983048 | tf_op jit(solution)/shard_map/ppermute | solution.py:24
  29.9 1.7 %collective-permute-start.6 = (bf16[128,1280]{1,0:T(8,128)(2,1)S(1)}, bf16[128,1280]{1,0:T(8,128)(2,1)S(1)}, u32[]{:S(2)}, u32[]{:S(2)}) collective-permute-start(bf16[128,1280]{1,0:T(8,128)(2,1)S(1)} %collective-permute-done.5.refs_7_), channel_id=1, source_target_pairs={{0,1},{1,0},{2,3},{3,2},{4,5},{5,4},{6,7},{7,6},{8,9},{9,8},{10,11... | collective-permute-start | bytes 983048 | tf_op jit(solution)/shard_map/ppermute | solution.py:24
  32.3 22.7 %copy-start.22 = (bf16[1024]{0:T(1024)(128)(2,1)S(1)}, bf16[1024]{0:T(1024)(128)(2,1)}, u32[]{:S(2)}) copy-start(bf16[1024]{0:T(1024)(128)(2,1)} %param.6) | copy-start | bytes 6148
  37.1 7.1 %collective-permute-start.7 = (bf16[256,128]{1,0:T(8,128)(2,1)}, bf16[256,128]{1,0:T(8,128)(2,1)S(1)}, u32[]{:S(2)}, u32[]{:S(2)}) collective-permute-start(bf16[256,128]{1,0:T(8,128)(2,1)} %get-tuple-element.49.refs_0_.refs_2_), channel_id=1, source_target_pairs={{0,4},{4,0},{8,12},{12,8},{1,5},{5,1},{9,13},{13,9},{2,6},{6,2},{1... | collective-permute-start | bytes 196616 | tf_op jit(solution)/shard_map/ppermute | solution.py:24
  40.2 8.3 %collective-permute-start.8 = (bf16[256,128]{1,0:T(8,128)(2,1)}, bf16[256,128]{1,0:T(8,128)(2,1)S(1)}, u32[]{:S(2)}, u32[]{:S(2)}) collective-permute-start(bf16[256,128]{1,0:T(8,128)(2,1)} %get-tuple-element.49.refs_0_.refs_2_), channel_id=1, source_target_pairs={{0,8},{4,12},{8,0},{12,4},{1,9},{5,13},{9,1},{13,5},{2,10},{6,14},... | collective-permute-start | bytes 196616 | tf_op jit(solution)/shard_map/ppermute | solution.py:24
  44.2 5.8 %collective-permute-start.9 = (bf16[256,128]{1,0:T(8,128)(2,1)}, bf16[256,128]{1,0:T(8,128)(2,1)S(1)}, u32[]{:S(2)}, u32[]{:S(2)}) collective-permute-start(bf16[256,128]{1,0:T(8,128)(2,1)} %get-tuple-element.49.refs_0_.refs_2_), channel_id=1, source_target_pairs={{0,12},{4,8},{8,4},{12,0},{1,13},{5,9},{9,5},{13,1},{2,14},{6,10},... | collective-permute-start | bytes 196616 | tf_op jit(solution)/shard_map/ppermute | solution.py:24
  44.2 5.8 %copy-start.14 = (bf16[256,128]{1,0:T(8,128)(2,1)}, bf16[256,128]{1,0:T(8,128)(2,1)S(1)}, u32[]{:S(2)}) copy-start(bf16[256,128]{1,0:T(8,128)(2,1)S(1)} %collective-permute-done.7.refs_1_.refs_3_) | copy-start | bytes 196612
  52.3 6.4 %collective-permute-start.10 = (bf16[128,128]{1,0:T(8,128)(2,1)}, bf16[128,128]{1,0:T(8,128)(2,1)S(1)}, u32[]{:S(2)}, u32[]{:S(2)}) collective-permute-start(bf16[128,128]{1,0:T(8,128)(2,1)} %shard_map.78), channel_id=1, source_target_pairs={{0,32},{32,0},{1,33},{33,1},{2,34},{34,2},{3,35},{35,3},{4,36},{36... | collective-permute-start | bytes 98312 | tf_op jit(solution)/shard_map/ppermute | solution.py:24
  62.1 6.5 %collective-permute-start.11 = (bf16[272,128]{1,0:T(8,128)(2,1)}, bf16[272,128]{1,0:T(8,128)(2,1)S(1)}, u32[]{:S(2)}, u32[]{:S(2)}) collective-permute-start(bf16[272,128]{1,0:T(8,128)(2,1)} %get-tuple-element.52.refs_0_.refs_5_), channel_id=1, source_target_pairs={{0,4},{4,0},{8,12},{12,8},{1,5},{5,1},{9,13},{13,9},{2,6},{6,2},{1... | collective-permute-start | bytes 208904 | tf_op jit(solution)/shard_map/ppermute | solution.py:24
  62.9 8.4 %collective-permute-start.12 = (bf16[272,128]{1,0:T(8,128)(2,1)}, bf16[272,128]{1,0:T(8,128)(2,1)S(1)}, u32[]{:S(2)}, u32[]{:S(2)}) collective-permute-start(bf16[272,128]{1,0:T(8,128)(2,1)} %get-tuple-element.52.refs_0_.refs_5_), channel_id=1, source_target_pairs={{0,8},{4,12},{8,0},{12,4},{1,9},{5,13},{9,1},{13,5},{2,10},{6,14},... | collective-permute-start | bytes 208904 | tf_op jit(solution)/shard_map/ppermute | solution.py:24
  68.6 6.6 %collective-permute-start.13 = (bf16[272,128]{1,0:T(8,128)(2,1)}, bf16[272,128]{1,0:T(8,128)(2,1)S(1)}, u32[]{:S(2)}, u32[]{:S(2)}) collective-permute-start(bf16[272,128]{1,0:T(8,128)(2,1)} %get-tuple-element.52.refs_0_.refs_5_), channel_id=1, source_target_pairs={{0,12},{4,8},{8,4},{12,0},{1,13},{5,9},{9,5},{13,1},{2,14},{6,10},... | collective-permute-start | bytes 208904 | tf_op jit(solution)/shard_map/ppermute | solution.py:24
  68.6 6.6 %copy-start.11 = (bf16[272,128]{1,0:T(8,128)(2,1)}, bf16[272,128]{1,0:T(8,128)(2,1)S(1)}, u32[]{:S(2)}) copy-start(bf16[272,128]{1,0:T(8,128)(2,1)S(1)} %collective-permute-done.11.refs_1_.refs_6_) | copy-start | bytes 208900
  71.3 3.9 %copy-start.12 = (bf16[272,128]{1,0:T(8,128)(2,1)}, bf16[272,128]{1,0:T(8,128)(2,1)S(1)}, u32[]{:S(2)}) copy-start(bf16[272,128]{1,0:T(8,128)(2,1)S(1)} %collective-permute-done.12.refs_2_.refs_7_) | copy-start | bytes 208900
  77.5 5.1 %collective-permute-start.14 = (bf16[144,128]{1,0:T(8,128)(2,1)}, bf16[144,128]{1,0:T(8,128)(2,1)S(1)}, u32[]{:S(2)}, u32[]{:S(2)}) collective-permute-start(bf16[144,128]{1,0:T(8,128)(2,1)} %shard_map.80), channel_id=1, source_target_pairs={{0,32},{32,0},{1,33},{33,1},{2,34},{34,2},{3,35},{35,3},{4,36},{36... | collective-permute-start | bytes 110600 | tf_op jit(solution)/shard_map/ppermute | solution.py:24
  91.1 28.5 %collective-permute-start.15 = (bf16[512,3072]{1,0:T(8,128)(2,1)}, bf16[512,3072]{1,0:T(8,128)(2,1)S(1)}, u32[]{:S(2)}, u32[]{:S(2)}) collective-permute-start(bf16[512,3072]{1,0:T(8,128)(2,1)} %all-gather.2.cloned.1.call-done.refs_1_), channel_id=1, source_target_pairs={{0,1},{1,0},{2,3},{3,2},{4,5},{5,4},{6,7},{7,6},{8,9},{9,8},{10,11... | collective-permute-start | bytes 9437192 | tf_op jit(solution)/shard_map/ppermute | solution.py:24
  114.2 18.2 %all-to-all-start.2 = ((bf16[16,64,384]{2,1,0:T(8,128)(2,1)}), bf16[16,64,384]{2,1,0:T(8,128)(2,1)}, u32[]{:S(2)}, u32[]{:S(2)}) async-start(bf16[16,64,384]{2,1,0:T(8,128)(2,1)} %bitcast.11), calls=%async_computation.2 | async-start | bytes 1572864 | tf_op jit(solution)/shard_map/all_to_all | solution.py:382
  134.3 17.6 %all-to-all-start.3 = ((f32[16,8,384]{2,1,0:T(8,128)}), f32[16,8,384]{2,1,0:T(8,128)S(1)}, u32[]{:S(2)}, u32[]{:S(2)}) async-start(f32[16,8,384]{2,1,0:T(8,128)} %bitcast.15), calls=%async_computation.3 | async-start | bytes 393216 | tf_op jit(solution)/shard_map/all_to_all | solution.py:389
  141.6 3.9 %collective-permute-start.16 = (f32[8,8,128]{2,1,0:T(8,128)}, f32[8,8,128]{2,1,0:T(8,128)S(1)}, u32[]{:S(2)}, u32[]{:S(2)}) collective-permute-start(f32[8,8,128]{2,1,0:T(8,128)} %get-tuple-element.68.refs_1_), channel_id=1, source_target_pairs={{0,64},{64,0},{128,192},{192,128},{1,65},{65,1},{129,193},{193,129... | collective-permute-start | bytes 98312 | tf_op jit(solution)/shard_map/ppermute | solution.py:24
  141.6 4.6 %collective-permute-start.17 = (f32[8,8,128]{2,1,0:T(8,128)}, f32[8,8,128]{2,1,0:T(8,128)S(1)}, u32[]{:S(2)}, u32[]{:S(2)}) collective-permute-start(f32[8,8,128]{2,1,0:T(8,128)} %get-tuple-element.68.refs_1_), channel_id=1, source_target_pairs={{0,128},{64,192},{128,0},{192,64},{1,129},{65,193},{129,1},{193,65... | collective-permute-start | bytes 98312 | tf_op jit(solution)/shard_map/ppermute | solution.py:24
  143.6 4.5 %collective-permute-start.18 = (f32[8,8,128]{2,1,0:T(8,128)}, f32[8,8,128]{2,1,0:T(8,128)S(1)}, u32[]{:S(2)}, u32[]{:S(2)}) collective-permute-start(f32[8,8,128]{2,1,0:T(8,128)} %get-tuple-element.68.refs_1_), channel_id=1, source_target_pairs={{0,192},{64,128},{128,64},{192,0},{1,193},{65,129},{129,65},{193,1... | collective-permute-start | bytes 98312 | tf_op jit(solution)/shard_map/ppermute | solution.py:24
  145.4 6.5 %copy-start.18 = (f32[8,8,128]{2,1,0:T(8,128)}, f32[8,8,128]{2,1,0:T(8,128)S(1)}, u32[]{:S(2)}) copy-start(f32[8,8,128]{2,1,0:T(8,128)S(1)} %collective-permute-done.16.refs_2_) | copy-start | bytes 98308
  146.1 5.8 %copy-start.19 = (f32[8,8,128]{2,1,0:T(8,128)}, f32[8,8,128]{2,1,0:T(8,128)S(1)}, u32[]{:S(2)}) copy-start(f32[8,8,128]{2,1,0:T(8,128)S(1)} %collective-permute-done.17.refs_3_) | copy-start | bytes 98308
  (14 other events, 18.3 us)
Sparse Core Ops, SparseCore 0:
  37.2 43.6 all-gather.1

commit v3 on v2

v3 whole, which is shorter than its diff:
```python
import jax
import jax.numpy as jnp
from jax import lax
from jax.experimental import pallas as pl
from jax.experimental.pallas import tpu as pltpu
from jax.sharding import Mesh, PartitionSpec as P

HEADS = 8
HEAD_DIM = 128
EPSILON = 1e-05
BF = jnp.bfloat16
F32 = jnp.float32

SEQ = ("yh", "yl", "zh", "zm", "zl", "c")
CUBE = ("yl", "zl", "c")
RUN = ("zh", "zm")
ALL = ("dp",) + SEQ
NN = (((1,), (0,)), ((), ()))
NT = (((1,), (1,)), ((), ()))
TN = (((0,), (0,)), ((), ()))


def swap(x, axes, bit, count):
    return lax.ppermute(x, axes, [(i, i ^ bit) for i in range(count)])


def dot(a, b, dims):
    return lax.dot_general(a, b, dims, preferred_element_type=F32)


def together(*xs):
    return lax.optimization_barrier(xs)


def call(body, outs, *operands, flops=0, scratch=(), near_in=False, near_out=False, limit=60, views=None):
    size = sum(o.size * o.dtype.itemsize for o in (*operands, *outs))
    count, total = len(operands), len(operands) + len(outs)
    moved = ([] if near_in else list(range(count))) + ([] if near_out else list(range(count, total)))
    arrays = (*operands, *outs)
    views = views or {}
    dims = [views[i][0] if i in views else x.shape for i, x in enumerate(arrays)]

    def kernel(*refs):
        given, (*copies, sems), rest = refs[:total], refs[total : total + len(moved) + 1], refs[total + len(moved) + 1 :]
        near = list(given)
        for slot, i in enumerate(moved):
            near[i] = copies[slot]
        given = [views[i][1](ref) if i in views else ref for i, ref in enumerate(given)]
        loads = {i: pltpu.make_async_copy(given[i], near[i], sems.at[i]) for i in moved if i < count}
        stores = {i - count: pltpu.make_async_copy(near[i], given[i], sems.at[i]) for i in moved if i >= count}
        waited, started = set(), set()

        def ready(*places):
            for i in places or range(count):
                if i in loads and i not in waited:
                    loads[i].wait()
                    waited.add(i)

        def finish(*places):
            for i in places or range(len(outs)):
                if i in stores and i not in started:
                    stores[i].start()
                    started.add(i)

        for load in loads.values():
            load.start()
        body(ready, finish, *near, *rest)
        ready()
        finish()
        for store in stores.values():
            store.wait()

    inside, outside = pl.BlockSpec(memory_space=pltpu.VMEM), pl.BlockSpec(memory_space=pltpu.HBM)
    return pl.pallas_call(
        kernel,
        out_shape=[o if near_out else pltpu.HBM(o.shape, o.dtype) for o in outs],
        in_specs=[inside if near_in else outside] * count,
        out_specs=[inside if near_out else outside] * len(outs),
        scratch_shapes=[pltpu.VMEM(dims[i], arrays[i].dtype) for i in moved]
        + [pltpu.SemaphoreType.DMA((total,))]
        + list(scratch),
        cost_estimate=pl.CostEstimate(flops=flops, bytes_accessed=size, transcendentals=0),
        compiler_params=pltpu.CompilerParams(vmem_limit_bytes=limit * 2**20),
    )(*operands)


def shape(dims, dtype):
    return jax.ShapeDtypeStruct(dims, dtype)


def slices(weight, tokens, grad):
    depth, d, half = weight.shape[0], HEAD_DIM, weight.shape[0] // 2
    n, width = tokens.shape

    def kernel(weight, tokens, grad, heads_out, half_out, b0, b1, b2, b3, head, half_near, tok, cols, sems):
        me, core = lax.axis_index(CUBE), lax.axis_index("c")
        loads = [(tokens, tok)]
        for k in range(4):
            at = pl.multiple_of(((me // 2) ^ k) * 2 * d, 2 * d)
            loads.append((grad.at[:, pl.ds(at, 2 * d)], cols.at[k]))
        for part in range(3):
            at = pl.multiple_of((part * HEADS + me) * d, d)
            loads.append((weight.at[:, pl.ds(at, d)], head.at[:, pl.ds(part * d, d)]))
        loads.append((weight.at[pl.ds(pl.multiple_of(core * half, half), half), :], half_near))
        loads = [pltpu.make_async_copy(x, y, sems.at[i]) for i, (x, y) in enumerate(loads)]
        stores = []
        for k, block in enumerate((b0, b1, b2, b3)):
            stores.append((tok, block.at[:, pl.ds(0, width)]))
            stores.append((cols.at[k], block.at[:, pl.ds(width, 2 * d)]))
        for j in range(4):
            stores.append((head, heads_out.at[pl.ds(j * depth, depth), :]))
        stores.append((half_near, half_out))
        stores = [pltpu.make_async_copy(x, y, sems.at[i + len(loads)]) for i, (x, y) in enumerate(stores)]
        for copy in loads:
            copy.start()
        for some, then in ((loads[:5], stores[:8]), (loads[5:8], stores[8:12]), (loads[8:], stores[12:])):
            for copy in some:
                copy.wait()
            for copy in then:
                copy.start()
        for copy in stores:
            copy.wait()

    outs = ((4 * depth, 3 * d), (half, weight.shape[1])) + ((n, width + 2 * d),) * 4
    near = ((depth, 3 * d), (half, weight.shape[1]), (n, width), (4, n, 2 * d))
    return pl.pallas_call(
        kernel,
        out_shape=[pltpu.HBM(o, BF) for o in outs],
        in_specs=[pl.BlockSpec(memory_space=pltpu.HBM)] * 3,
        out_specs=[pl.BlockSpec(memory_space=pltpu.HBM)] * len(outs),
        scratch_shapes=[pltpu.VMEM(o, BF) for o in near] + [pltpu.SemaphoreType.DMA((22,))],
        cost_estimate=pl.CostEstimate(flops=0, bytes_accessed=2**21, transcendentals=0),
        compiler_params=pltpu.CompilerParams(vmem_limit_bytes=60 * 2**20),
    )(weight, tokens, grad)


def load_rows(pieces, rows, width, sems):
    n = pieces[0].shape[0]
    me = lax.axis_index(CUBE)
    copies = []
    for k in range(8):
        place = pl.ds(pl.multiple_of((me ^ k) * n, n), n)
        copies.append(pltpu.make_async_copy(pieces[k].at[:, pl.ds(0, width)], rows.at[place, :], sems.at[k]))
        copies[-1].start()
    return copies


def project(w_cols, pieces):
    d, n = HEAD_DIM, pieces[0].shape[0]
    width, rows = w_cols.shape[0], 8 * n

    def kernel(w_far, *refs):
        pieces, (query, key, value, states, upstream, w, tokens, sems) = refs[:8], refs[8:]
        me = lax.axis_index(CUBE)
        at = pl.multiple_of(width + lax.axis_index("c") * d, d)
        first = pltpu.make_async_copy(w_far, w, sems.at[16])
        first.start()
        loads = load_rows(pieces, tokens, width, sems)
        ups = []
        for k in range(8):
            place = pl.ds(pl.multiple_of((me ^ k) * n, n), n)
            ups.append(pltpu.make_async_copy(pieces[k].at[:, pl.ds(at, d)], upstream.at[place, :], sems.at[8 + k]))
            ups[-1].start()
        first.wait()
        for p in range(4):
            loads[2 * p].wait()
            loads[2 * p + 1].wait()
            place = pl.ds(pl.multiple_of(((me // 2) ^ p) * 2 * n, 2 * n), 2 * n)
            got = dot(tokens[place, :], w[...], NN).astype(BF)
            for part, ref in enumerate((query, key, value)):
                ref[place, :] = got[:, part * d : (part + 1) * d]
        half = 4 * n
        for s in range(2):
            place = pl.ds(s * half, half)
            states[pl.ds(s * d, d), :] = dot(key[place, :], value[place, :], TN).astype(BF)
        for copy in ups:
            copy.wait()

    column = shape((rows, d), BF)
    return pl.pallas_call(
        kernel,
        out_shape=[column, column, column, shape((2 * d, d), BF), column],
        in_specs=[pl.BlockSpec(memory_space=pltpu.HBM)] * 9,
        out_specs=[pl.BlockSpec(memory_space=pltpu.VMEM)] * 5,
        scratch_shapes=[
            pltpu.VMEM(w_cols.shape, BF), pltpu.VMEM((rows, width), BF), pltpu.SemaphoreType.DMA((17,))
        ],
        cost_estimate=pl.CostEstimate(flops=2 * rows * width * 3 * d, bytes_accessed=2**22, transcendentals=0),
        compiler_params=pltpu.CompilerParams(vmem_limit_bytes=58 * 2**20),
    )(w_cols, *pieces)


def below(rows):
    return lax.broadcasted_iota(jnp.int32, (rows, rows), 0) >= lax.broadcasted_iota(jnp.int32, (rows, rows), 1)


def inside(ready, finish, query, key, value, upstream, states, scores, intra, *copies):
    for source, copy in zip((query, key, value, upstream, states), copies):
        copy[...] = source[...]
    half = query.shape[0] // 2
    keep = below(half)
    for s in range(2):
        rows = pl.ds(s * half, half)
        got = jnp.where(keep, dot(query[rows, :], key[rows, :], NT), 0.0).astype(BF)
        scores[rows, :] = got
        intra[rows, :] = dot(got, value[rows, :], NN)


def combine(ready, finish, mine, a, b, c, out):
    ready()
    d = HEAD_DIM
    total = mine[...].astype(F32) + a[...].astype(F32) + b[...].astype(F32) + c[...].astype(F32)
    out[...] = (total[:d] + total[d:]).astype(BF)


def in_parts(row):
    high = row.astype(BF).astype(F32)
    middle = (row - high).astype(BF).astype(F32)
    wide = jnp.concatenate([high, middle, row - high - middle], axis=1)
    place = lax.broadcasted_iota(jnp.int32, (16, wide.shape[1]), 0)
    return jnp.where(place == 0, wide, 0.0).astype(BF)


def states_at(mine, got, far, backward):
    d = HEAD_DIM
    place = lax.axis_index(RUN)
    total = mine[: 2 * d, :].astype(F32)
    near = jnp.zeros_like(total)
    for k, ref in enumerate(got):
        term = ref[: 2 * d, :].astype(F32)
        source = place ^ (k + 1)
        use = (source > place) if backward else (source < place)
        near = near + jnp.where(use, term, 0.0)
        total = total + term
    yh = lax.axis_index("yh")
    cross = jnp.where((yh == 0) if backward else (yh == 1), far[:d, :].astype(F32), 0.0)
    if backward:
        return near[:d] + total[d:] + cross, near[d:] + cross
    return near[:d] + cross, near[d:] + total[:d] + cross


def forward(
    ready, finish, query, intra, mine, a, b, c, far, upstream, gain, attended, mixed_grad, payload, before, gain_sum
):
    ready()
    d = HEAD_DIM
    half = query.shape[0] // 2
    scale = gain[:, pl.ds(pl.multiple_of(lax.axis_index(CUBE) * d, d), d)].astype(F32)
    gain_part = jnp.zeros((1, d), F32)
    for s, state in enumerate(states_at(mine, (a, b, c), far, False)):
        state = state.astype(BF)
        before[pl.ds(s * d, d), :] = state
        rows = pl.ds(s * half, half)
        mixed = intra[rows, :] + dot(query[rows, :], state, NN)
        inverse_rms = lax.rsqrt(jnp.mean(mixed * mixed, axis=-1, keepdims=True) + EPSILON)
        normed = mixed * inverse_rms
        attended[rows, :] = (scale * normed).astype(BF)
        up = upstream[rows, :].astype(F32)
        product = up * normed
        gain_part = gain_part + jnp.sum(product, axis=0, keepdims=True)
        along = jnp.mean(product * scale, axis=-1, keepdims=True)
        grad = (inverse_rms * (up * scale - normed * along)).astype(BF)
        mixed_grad[rows, :] = grad
        payload[pl.ds(s * d, d), :] = dot(query[rows, :], grad, TN).astype(BF)
    gain_sum[...] = jnp.broadcast_to(gain_part, gain_sum.shape)


def backward_inside(
    ready, finish, query, key, value, scores, mixed_grad, before, attended, sent, key_part, value_part
):
    ready()
    d = HEAD_DIM
    half = query.shape[0] // 2
    keep = below(half)
    for s in range(2):
        rows = pl.ds(s * half, half)
        grad = mixed_grad[rows, :]
        got = jnp.where(keep, dot(grad, value[rows, :], NT), 0.0).astype(BF)
        sent[rows, :d] = attended[rows, :]
        sent[rows, d:] = (dot(got, key[rows, :], NN) + dot(grad, before[pl.ds(s * d, d), :], NT)).astype(BF)
        key_part[rows, :] = dot(got, query[rows, :], TN)
        value_part[rows, :] = dot(scores[rows, :], grad, TN)


def backward_rest(ready, finish, key, value, sent, key_part, value_part, mine, a, b, c, far, joined, *refs):
    late, blocks = refs[:4], refs[4]
    ready()
    d = HEAD_DIM
    n = key.shape[0] // 8
    half = 4 * n
    joined[:, :d] = sent[:, d:]
    for s, state in enumerate(states_at(mine, (a, b, c), far, True)):
        state = state.astype(BF)
        rows = pl.ds(s * half, half)
        key_grad = (key_part[rows, :] + dot(value[rows, :], state, NT)).astype(BF)
        value_grad = (value_part[rows, :] + dot(key[rows, :], state, NN)).astype(BF)
        joined[rows, d : 2 * d] = key_grad
        joined[rows, 2 * d :] = value_grad
        for i in range(4):
            blocks[s * 4 + i, :, : 2 * d] = sent[pl.ds(s * half + i * n, n), :]
            blocks[s * 4 + i, :, 2 * d : 3 * d] = key_grad[i * n : (i + 1) * n]
            blocks[s * 4 + i, :, 3 * d :] = value_grad[i * n : (i + 1) * n]
    finish(0)
    chip = lax.axis_index(CUBE) // 2
    for k in range(4):
        for core in range(2):
            late[k][core] = blocks[(chip ^ k) * 2 + core]
        finish(1 + k)


def weigh(joined, gain_sum, pieces, width):
    n, d = pieces[0].shape[0], HEAD_DIM
    rows = 8 * n

    def kernel(joined_far, gain_far, *refs):
        pieces, (out_far, joined, gain, tokens, out, sems) = refs[:8], refs[8:]
        first = pltpu.make_async_copy(joined_far, joined, sems.at[8])
        second = pltpu.make_async_copy(gain_far, gain, sems.at[10])
        first.start()
        second.start()
        loads = load_rows(pieces, tokens, width, sems)
        first.wait()
        for load in loads:
            load.wait()
        second.wait()
        terms = in_parts(gain[:1, :])
        step, share = 256, width // 16
        for j in range(width // step):
            got = dot(tokens[:, j * step : (j + 1) * step].T, joined[...], NN).astype(BF)
            for i in range(step // share):
                at = (j * (step // share) + i) * (share + 16)
                out[at : at + share, :] = got[i * share : (i + 1) * share]
                out[at + share : at + share + 16, :] = terms
        last = pltpu.make_async_copy(out, out_far, sems.at[9])
        last.start()
        last.wait()

    return pl.pallas_call(
        kernel,
        out_shape=pltpu.HBM((width + 256, 3 * d), BF),
        in_specs=[pl.BlockSpec(memory_space=pltpu.HBM)] * 10,
        out_specs=pl.BlockSpec(memory_space=pltpu.HBM),
        scratch_shapes=[
            pltpu.VMEM((rows, 3 * d), BF), pltpu.VMEM((8, d), F32), pltpu.VMEM((rows, width), BF),
            pltpu.VMEM((width + 256, 3 * d), BF), pltpu.SemaphoreType.DMA((11,)),
        ],
        cost_estimate=pl.CostEstimate(flops=2 * rows * width * 3 * d, bytes_accessed=2**22, transcendentals=0),
        compiler_params=pltpu.CompilerParams(vmem_limit_bytes=60 * 2**20),
    )(joined, gain_sum, *pieces)


def at_home(ready, finish, mine, *refs):
    late, (keep, send, attended, blocks) = refs[:8], refs[8:]
    ready(*range(1, 9))
    d = HEAD_DIM
    n = attended.shape[0]
    me, core = lax.axis_index(CUBE), lax.axis_index("c")
    for k in range(HEADS):
        blocks[me ^ k, :n, :] = late[k][core]
        blocks[me ^ k, n:, :] = late[k][1 - core]
    for h in range(HEADS):
        attended[:, h * d : (h + 1) * d] = blocks[h, :n, :d]
    finish(2)
    rows = jnp.concatenate(
        [blocks[h, :, (1 + part) * d : (2 + part) * d] for part in range(3) for h in range(HEADS)], axis=1
    )
    ready(0)
    got = dot(rows, mine[...], NT).astype(BF)
    keep[...] = got[:n]
    send[...] = got[n:]


def add_first(ready, finish, pieces, out):
    ready()
    d = HEAD_DIM
    whole, width = pieces.shape[0] // 16, pieces.shape[1]
    rows = whole - 16
    for yl in range(2):
        total = sum(
            pieces[pl.ds(((dp * 2 + yh) * 2 + yl) * whole, whole), :].astype(F32) for dp in range(4) for yh in range(2)
        )
        gain = total[rows : rows + 1]
        gain = jnp.broadcast_to(gain[:, :d] + gain[:, d : 2 * d] + gain[:, 2 * d :], (4, d))
        for j in range(16):
            place = pl.ds(j * 8 + yl * 4, 4)
            out[place, :width] = total[j * 4 : j * 4 + 4, :]
            out[place, width:] = gain


def add_up(ready, finish, pieces, keep, got, weight_grad, gain_grad, input_grad):
    ready()
    d = HEAD_DIM
    for low in range(4):
        total = sum(pieces[pl.ds((run * 4 + low) * 8, 8), :] for run in range(4)) / 4
        for yl in range(2):
            h = yl * 4 + low
            for part in range(3):
                at = (part * HEADS + h) * d
                weight_grad[:, at : at + d] = total[yl * 4 : yl * 4 + 4, part * d : (part + 1) * d]
            gain_grad[h : h + 1, :] = total[yl * 4 : yl * 4 + 1, 3 * d :]
    width = keep.shape[1] // 4
    even = lax.axis_index("c") == 0
    for p in range(4):
        x, y = keep[:, p * width : (p + 1) * width], got[:, p * width : (p + 1) * width]
        input_grad[:, 2 * p * width : (2 * p + 1) * width] = jnp.where(even, x, y)
        input_grad[:, (2 * p + 1) * width : (2 * p + 2) * width] = jnp.where(even, y, x)


def local(tokens, qkv_weight, out_gain, out_grad):
    replicas = lax.axis_size("dp")
    d = HEAD_DIM
    block = tokens[0]
    n, width = block.shape
    inner = out_gain.shape[0]
    depth = qkv_weight.shape[0]

    w_heads, w_half, *blocks = slices(qkv_weight, block, out_grad[0])
    near = [swap(blocks[bit], ("yl", "zl"), bit, 4) for bit in (1, 2, 3)]
    w_cols = lax.all_to_all(w_heads, "dp", 0, 0, tiled=True)
    mine, _ = together(blocks[0], near[0])
    pieces = [x for side in [mine] + near for x in (side, swap(side, "c", 1, 2))]

    rows = 8 * n
    column, square = shape((rows, d), BF), shape((2 * d, d), BF)
    query, key, value, states, upstream = project(w_cols, pieces)
    w_half, _ = together(w_half, states)
    w_mine = lax.all_gather(w_half, "dp", axis=0, tiled=True)
    got = [swap(states, RUN, bit, 4) for bit in (1, 2, 3)]
    scores, intra, query, key, value, upstream, states = call(
        inside, (shape((rows, rows // 2), BF), shape((rows, d), F32), column, column, column, column, square),
        query, key, value, upstream, states, flops=2 * rows * rows * d, near_in=True, near_out=True, limit=12,
    )
    scores, *got = together(scores, *got)
    (both,) = call(combine, (shape((d, d), BF),), states, *got, near_in=True, near_out=True, limit=12)
    far = swap(both, "yh", 1, 2)
    attended_head, mixed_grad, payload, before, gain_sum = call(
        forward, (column, column, square, square, shape((8, d), F32)),
        query, intra, states, *got, far, upstream, out_gain.reshape(1, inner), flops=4 * rows * d * d, near_in=True, near_out=True, limit=12,
    )
    grads = [swap(payload, RUN, bit, 4) for bit in (1, 2, 3)]
    (both_grad,) = call(combine, (shape((d, d), BF),), payload, *grads, near_in=True, near_out=True, limit=12)
    mixed_grad, both_grad = together(mixed_grad, both_grad)
    sent, key_part, value_part = call(
        backward_inside, (shape((rows, 2 * d), BF), shape((rows, d), F32), shape((rows, d), F32)),
        query, key, value, scores, mixed_grad, before, attended_head, flops=4 * rows * rows * d, near_in=True, near_out=True, limit=12,
    )
    far_grad = swap(both_grad, "yh", 1, 2)
    joined, *late = call(
        backward_rest, (shape((rows, 3 * d), BF),) + (shape((2, n, 4 * d), BF),) * 4,
        key, value, sent, key_part, value_part, payload, *grads, far_grad, flops=8 * rows * d * d,
        near_in=True, limit=16, scratch=[pltpu.VMEM((HEADS, n, 4 * d), BF)],
    )
    late = [late[0]] + [swap(late[bit], ("yl", "zl"), bit, 4) for bit in (1, 2, 3)]
    weight_part = weigh(joined, gain_sum, pieces, width)
    sums = lax.all_to_all(weight_part, ("dp", "yh", "yl"), 0, 0, tiled=True)
    (sums,) = call(add_first, (shape((rows // 8, 4 * d), F32),), sums)
    *late, _ = together(*late, sums)
    late = [x for side in late for x in (side, swap(side, "c", 1, 2))]
    sums = lax.all_to_all(sums, ("zh", "zm", "zl", "c"), 0, 0, tiled=True)
    half = shape((n, width // 2), BF)
    keep, send, attended = call(
        at_home, (half, half, shape((n, inner), BF)), w_mine, *late,
        flops=2 * n * width * 3 * inner, scratch=[pltpu.VMEM((HEADS, 2 * n, 4 * d), BF)],
    )
    got = swap(send, "c", 1, 2)
    sums, got = together(sums, got)
    weight_grad, gain_grad, input_grad = call(
        add_up, (shape((width // 256, 3 * inner), F32), shape((HEADS, d), F32), shape((n, width), BF)), sums, keep, got
    )
    return (attended[None], input_grad[None], weight_grad, gain_grad.reshape(inner))


def solution(mesh):
    fine = Mesh(mesh.devices.reshape(mesh.devices.shape[0], 2, 2, 2, 2, 2, 2), ALL)
    rows = P("dp", SEQ, None)
    return jax.shard_map(
        local,
        mesh=fine,
        in_specs=(rows, P("dp", None), P(), rows),
        out_specs=(rows, rows, P(ALL, None), P()),
        check_vma=False,
    )
```

time: 162 us -> 135 us (0.83)
  blocking collectives: 20.2 us -> 0 us
  Pallas kernels: 38.4 us -> 25.2 us
  starting transfers between devices: 55.3 us -> 61.1 us
  local copies, waits for them, and re-layouts: 6.13 us -> 7.81 us
    all_to_all x1 -> x0, blocking collectives: 20.2 us -> none  [local(): late = lax.all_to_all(late, CUBE, 0, 0, tiled=True)]
    pallas_call x11, Pallas kernels: 35.6 us -> 22.4 us  [the longest x9 13.8 us: call(): pl.pallas_call(kernel, out_shape=[o if near_out else pltpu.HBM(o.shape, o...]
    all_to_all x1, waiting for transfers between devices: 4.88 us -> 10.3 us  [local(): sums = lax.all_to_all(weight_part, ('dp', 'yh', 'yl'), 0, 0, tiled=True)]
    all_to_all x1, starting transfers between devices: 7.24 us -> 12.6 us  [local(): sums = lax.all_to_all(sums, ('zh', 'zm', 'zl', 'c'), 0, 0, tiled=True)]
    ppermute x19 -> x23, waiting for transfers between devices: 18 us -> 12.9 us  [swap(): return lax.ppermute(x, axes, [(i, i ^ bit) for i in range(count)])]
    unnamed x46 -> x58, local copies, waits for them, and re-layouts: 5.54 us -> 7.8 us
    ppermute x19 -> x23, starting transfers between devices: 38.7 us -> 38 us  [swap(): return lax.ppermute(x, axes, [(i, i ^ bit) for i in range(count)])]
  transfers between devices with their start and end apart: 23 -> 27, of which waited for: 11 -> 14; matrix products, arithmetic and copies ran while one was open for 0% -> 0% of each run, Pallas kernels for 17% -> 12%
where the time goes in v3:
time: 135 us
  starting transfers between devices  61.1 us (45%)
  waiting for transfers between devices  26.5 us (20%)
  Pallas kernels  25.2 us (19%)
  between operations  14.4 us (11%)
  local copies, waits for them, and re-layouts  7.81 us (6%)
    ppermute x23, starting transfers between devices, swap(): return lax.ppermute(x, axes, [(i, i ^ bit) for i in range(count)])  38 us
    pallas_call x9, Pallas kernels, call(): pl.pallas_call(kernel, out_shape=[o if near_out else pltpu.HBM(o.shape, o...  13.8 us
    ppermute x23, waiting for transfers between devices, swap(): return lax.ppermute(x, axes, [(i, i ^ bit) for i in range(count)])  12.9 us
    all_to_all x1, starting transfers between devices, local(): sums = lax.all_to_all(sums, ('zh', 'zm', 'zl', 'c'), 0, 0, tiled=True)  12.6 us
    all_to_all x1, waiting for transfers between devices, local(): sums = lax.all_to_all(weight_part, ('dp', 'yh', 'yl'), 0, 0, tiled=True)  10.3 us
    unnamed x58, local copies, waits for them, and re-layouts  7.8 us
    all_to_all x1, starting transfers between devices, local(): sums = lax.all_to_all(weight_part, ('dp', 'yh', 'yl'), 0, 0, tiled=True)  6.45 us
    pallas_call x1, Pallas kernels, project(): pl.pallas_call(kernel, out_shape=[column, column, column, shape((2 * d, d...  4.44 us
  transfers between devices with their start and end apart: 27, of which 14 were waited for; matrix products, arithmetic and copies ran while one was open for 0% of the time, Pallas kernels for 12%

profile of v3, /device:TPU:1, one launch (start us, length us, event | category | flops | bytes accessed | tf_op | source)
XLA Modules:
  0.0 134.9 jit_solution(3569636852761459839)
XLA Ops:
  7.2 2.7 %shard_map.75 = (bf16[1024,384]{1,0:T(8,128)(2,1)}, bf16[128,3072]{1,0:T(8,128)(2,1)}, bf16[128,1280]{1,0:T(8,128)(2,1)}, bf16[128,1280]{1,0:T(8,128)(2,1)}, bf1...) custom-call(bf16[256,3072]{1,0:T(8,128)(2,1)} %weight.1, bf16[128,1024]{1,0:T(8,128)(2,1)} %bitcast.17, ...), custom_call_target="tpu_custom_call" | custom-call | bytes 2097152 | tf_op jit(solution)/shard_map/pallas_call | solution.py:126
  9.9 2.6 %collective-permute-start = (bf16[128,1280]{1,0:T(8,128)(2,1)}, bf16[128,1280]{1,0:T(8,128)(2,1)S(1)}, u32[]{:S(2)}, u32[]{:S(2)}) collective-permute-start(bf16[128,1280]{1,0:T(8,128)(2,1)} %get-tuple-element.58), channel_id=1, source_target_pairs={{0,2},{2,0},{16,18},{18,16},{1,3},{3,1},{17,19},{19,17},{4,6},{6,4... | collective-permute-start | bytes 983048 | tf_op jit(solution)/shard_map/ppermute | solution.py:24
  12.5 1.3 collective-permute-start.3
  13.8 4.0 %all-to-all-start = ((bf16[4,256,384]{2,1,0:T(8,128)(2,1)}), bf16[4,256,384]{2,1,0:T(8,128)(2,1)S(1)}, u32[]{:S(2)}, u32[]{:S(2)}) async-start(bf16[4,256,384]{2,1,0:T(8,128)(2,1)} %bitcast.16), calls=%async_computation | async-start | bytes 1572864 | tf_op jit(solution)/shard_map/all_to_all | solution.py:419
  17.8 1.4 %collective-permute-done.refs_2_ = bf16[128,1280]{1,0:T(8,128)(2,1)S(1)} collective-permute-done((bf16[128,1280]{1,0:T(8,128)(2,1)}, bf16[128,1280]{1,0:T(8,128)(2,1)S(1)}, u32[]{:S(2)}, u32[]{:S(2)}) %collective-permute-start) | collective-permute-done | bytes 327712 | tf_op jit(solution)/shard_map/ppermute | solution.py:24
  19.2 4.9 %collective-permute-start.1 = (bf16[128,1280]{1,0:T(8,128)(2,1)}, bf16[128,1280]{1,0:T(8,128)(2,1)S(1)}, u32[]{:S(2)}, u32[]{:S(2)}) collective-permute-start(bf16[128,1280]{1,0:T(8,128)(2,1)} %get-tuple-element.59.refs_0_), channel_id=1, source_target_pairs={{0,1},{1,0},{2,3},{3,2},{4,5},{5,4},{6,7},{7,6},{8,9},{9,8},{10,11... | collective-permute-start | bytes 983048 | tf_op jit(solution)/shard_map/ppermute | solution.py:24
  24.1 5.7 %collective-permute-start.4 = (bf16[128,1280]{1,0:T(8,128)(2,1)S(1)}, bf16[128,1280]{1,0:T(8,128)(2,1)S(1)}, u32[]{:S(2)}, u32[]{:S(2)}) collective-permute-start(bf16[128,1280]{1,0:T(8,128)(2,1)S(1)} %collective-permute-done.3.refs_4_), channel_id=1, source_target_pairs={{0,1},{1,0},{2,3},{3,2},{4,5},{5,4},{6,7},{7,6},{8,9},{9,8},{10,11... | collective-permute-start | bytes 983048 | tf_op jit(solution)/shard_map/ppermute | solution.py:24
  30.0 1.1 collective-permute-done.4.refs_5_
  32.3 4.4 %shard_map.76 = (bf16[1024,128]{1,0:T(8,128)(2,1)}, bf16[1024,128]{1,0:T(8,128)(2,1)}, bf16[1024,128]{1,0:T(8,128)(2,1)}, bf16[256,128]{1,0:T(8,128)(2,1)}, bf16[1024,128]{1,0:T(8,128)(2,1)}) custom-call(bf16[1024,384]{1,0:T(8,128)(2,1)} %bitcast.13, bf16[128,1280]{1,0:T(8,128)(2,1)} %get-tuple-element.59.refs_0_, bf16[128,1280]{1,0:T(8,128)(2,1)} %copy-done.11, ...), custom_call_target="tpu_custom_call" | custom-call | flops 805306368 | bytes 4194304 | tf_op jit(solution)/shard_map/pallas_call | solution.py:180
  36.8 3.1 %collective-permute-start.7 = (bf16[256,128]{1,0:T(8,128)(2,1)}, bf16[256,128]{1,0:T(8,128)(2,1)S(1)}, u32[]{:S(2)}, u32[]{:S(2)}) collective-permute-start(bf16[256,128]{1,0:T(8,128)(2,1)} %get-tuple-element.62.refs_4_), channel_id=1, source_target_pairs={{0,4},{4,0},{8,12},{12,8},{1,5},{5,1},{9,13},{13,9},{2,6},{6,2},{1... | collective-permute-start | bytes 196616 | tf_op jit(solution)/shard_map/ppermute | solution.py:24
  39.9 4.0 %collective-permute-start.8 = (bf16[256,128]{1,0:T(8,128)(2,1)}, bf16[256,128]{1,0:T(8,128)(2,1)S(1)}, u32[]{:S(2)}, u32[]{:S(2)}) collective-permute-start(bf16[256,128]{1,0:T(8,128)(2,1)} %get-tuple-element.62.refs_4_), channel_id=1, source_target_pairs={{0,8},{4,12},{8,0},{12,4},{1,9},{5,13},{9,1},{13,5},{2,10},{6,14},... | collective-permute-start | bytes 196616 | tf_op jit(solution)/shard_map/ppermute | solution.py:24
  43.9 0.9 copy-done
  48.5 1.0 shard_map.77
  49.8 2.8 %collective-permute-start.10 = (bf16[128,128]{1,0:T(8,128)(2,1)S(1)}, bf16[128,128]{1,0:T(8,128)(2,1)S(1)}, u32[]{:S(2)}, u32[]{:S(2)}) collective-permute-start(bf16[128,128]{1,0:T(8,128)(2,1)S(1)} %shard_map.78), channel_id=1, source_target_pairs={{0,32},{32,0},{1,33},{33,1},{2,34},{34,2},{3,35},{35,3},{4,36},{36... | collective-permute-start | bytes 98312 | tf_op jit(solution)/shard_map/ppermute | solution.py:24
  52.6 1.6 %collective-permute-done.10.refs_6_ = bf16[128,128]{1,0:T(8,128)(2,1)S(1)} collective-permute-done((bf16[128,128]{1,0:T(8,128)(2,1)S(1)}, bf16[128,128]{1,0:T(8,128)(2,1)S(1)}, u32[]{:S(2)}, u32[]{:S(2)}) %collective-permute-start.10) | collective-permute-done | bytes 32800 | tf_op jit(solution)/shard_map/ppermute | solution.py:24
  55.0 1.6 %collective-permute-start.11 = (bf16[256,128]{1,0:T(8,128)(2,1)S(1)}, bf16[256,128]{1,0:T(8,128)(2,1)S(1)}, u32[]{:S(2)}, u32[]{:S(2)}) collective-permute-start(bf16[256,128]{1,0:T(8,128)(2,1)S(1)} %get-tuple-element.80.refs_0_.refs_5_), channel_id=1, source_target_pairs={{0,4},{4,0},{8,12},{12,8},{1,5},{5,1},{9,13},{13,9},{2,6},{6,2},{1... | collective-permute-start | bytes 196616 | tf_op jit(solution)/shard_map/ppermute | solution.py:24
  56.6 4.9 %collective-permute-start.12 = (bf16[256,128]{1,0:T(8,128)(2,1)S(1)}, bf16[256,128]{1,0:T(8,128)(2,1)S(1)}, u32[]{:S(2)}, u32[]{:S(2)}) collective-permute-start(bf16[256,128]{1,0:T(8,128)(2,1)S(1)} %get-tuple-element.80.refs_0_.refs_5_), channel_id=1, source_target_pairs={{0,8},{4,12},{8,0},{12,4},{1,9},{5,13},{9,1},{13,5},{2,10},{6,14},... | collective-permute-start | bytes 196616 | tf_op jit(solution)/shard_map/ppermute | solution.py:24
  61.5 2.3 %collective-permute-done.12.refs_2_.refs_7_ = bf16[256,128]{1,0:T(8,128)(2,1)S(1)} collective-permute-done((bf16[256,128]{1,0:T(8,128)(2,1)S(1)}, bf16[256,128]{1,0:T(8,128)(2,1)S(1)}, u32[]{:S(2)}, u32[]{:S(2)}) %collective-permute-start.12) | collective-permute-done | bytes 65568 | tf_op jit(solution)/shard_map/ppermute | solution.py:24
  63.9 3.8 %collective-permute-done.13.refs_3_.refs_8_ = bf16[256,128]{1,0:T(8,128)(2,1)S(1)} collective-permute-done((bf16[256,128]{1,0:T(8,128)(2,1)S(1)}, bf16[256,128]{1,0:T(8,128)(2,1)S(1)}, u32[]{:S(2)}, u32[]{:S(2)}) %collective-permute-start.13) | collective-permute-done | bytes 65568 | tf_op jit(solution)/shard_map/ppermute | solution.py:24
  67.7 2.7 %collective-permute-start.14 = (bf16[128,128]{1,0:T(8,128)(2,1)S(1)}, bf16[128,128]{1,0:T(8,128)(2,1)S(1)}, u32[]{:S(2)}, u32[]{:S(2)}) collective-permute-start(bf16[128,128]{1,0:T(8,128)(2,1)S(1)} %shard_map.80), channel_id=1, source_target_pairs={{0,32},{32,0},{1,33},{33,1},{2,34},{34,2},{3,35},{35,3},{4,36},{36... | collective-permute-start | bytes 98312 | tf_op jit(solution)/shard_map/ppermute | solution.py:24
  70.4 1.4 %shard_map.81 = (bf16[1024,256]{1,0:T(8,128)(2,1)S(1)}, f32[1024,128]{1,0:T(8,128)S(1)}, f32[1024,128]{1,0:T(8,128)S(1)}) custom-call(bf16[1024,128]{1,0:T(8,128)(2,1)S(1)} %get-tuple-element.70.refs_0_, bf16[1024,128]{1,0:T(8,128)(2,1)S(1)} %get-tuple-element.68.refs_1_.refs_0_, bf16[1024,128]{1,0:T(8,128)(2,1)S(1)} %get-tuple-element.69.refs_2_.refs_1_, ...), custom_call_target="tpu_custom_call" | custom-call | flops 536870912 | bytes 3997696 | tf_op jit(solution)/shard_map/pallas_call | solution.py:74
  72.3 1.8 %shard_map.82 = (bf16[1024,384]{1,0:T(8,128)(2,1)}, bf16[2,128,512]{2,1,0:T(8,128)(2,1)}, bf16[2,128,512]{2,1,0:T(8,128)(2,1)}, bf16[2,128,512]{2,1,0:T(8,128)(2,1)}, bf16[2,128,512]{2,1,0:T(8,128)(2,1)}) custom-call(bf16[1024,128]{1,0:T(8,128)(2,1)S(1)} %get-tuple-element.68.refs_1_.refs_0_, bf16[1024,128]{1,0:T(8,128)(2,1)S(1)} %get-tuple-element.69.refs_2_.refs_1_, ...), custom_call_target="tpu_custom_call" | custom-call | flops 134217728 | bytes 4227072 | tf_op jit(solution)/shard_map/pallas_call | solution.py:74
  74.1 4.2 %shard_map.83 = bf16[1280,384]{1,0:T(8,128)(2,1)} custom-call(bf16[1024,384]{1,0:T(8,128)(2,1)} %get-tuple-element.92.joined_far, f32[8,128]{1,0:T(8,128)} %copy-done.5, bf16[128,1280]{1,0:T(8,128)(2,1)} %get-tuple-element.59.refs_0_, bf16[128,1280]{1,0:T(8,128)(2,1)} %copy-done.11, bf16[128,1280]{1,0:T(8,128)(2,1)} %copy-done.8, ...), custom_call_target="tpu_custom_call" | custom-call | flops 805306368 | bytes 4194304 | tf_op jit(solution)/shard_map/pallas_call | solution.py:338
  78.3 6.5 %all-to-all-start.1 = ((bf16[16,80,384]{2,1,0:T(8,128)(2,1)}), bf16[16,80,384]{2,1,0:T(8,128)(2,1)S(1)}, u32[]{:S(2)}, u32[]{:S(2)}) async-start(bf16[16,80,384]{2,1,0:T(8,128)(2,1)} %bitcast.11), calls=%async_computation.1 | async-start | bytes 1966080 | tf_op jit(solution)/shard_map/all_to_all | solution.py:455
  84.8 1.6 %collective-permute-start.15 = (bf16[2,128,512]{2,1,0:T(8,128)(2,1)S(1)}, bf16[2,128,512]{2,1,0:T(8,128)(2,1)S(1)}, u32[]{:S(2)}, u32[]{:S(2)}) collective-permute-start(bf16[2,128,512]{2,1,0:T(8,128)(2,1)S(1)} %copy-done.28), channel_id=1, source_target_pairs={{0,2},{2,0},{16,18},{18,16},{1,3},{3,1},{17,19},{19,17},{4,6},{6,4... | collective-permute-start | bytes 786440 | tf_op jit(solution)/shard_map/ppermute | solution.py:24
  86.4 1.4 %collective-permute-start.16 = (bf16[2,128,512]{2,1,0:T(8,128)(2,1)S(1)}, bf16[2,128,512]{2,1,0:T(8,128)(2,1)S(1)}, u32[]{:S(2)}, u32[]{:S(2)}) collective-permute-start(bf16[2,128,512]{2,1,0:T(8,128)(2,1)S(1)} %copy-done.27), channel_id=1, source_target_pairs={{0,16},{2,18},{16,0},{18,2},{1,17},{3,19},{17,1},{19,3},{4,20},{6,... | collective-permute-start | bytes 786440 | tf_op jit(solution)/shard_map/ppermute | solution.py:24
  87.8 10.3 %all-to-all-done.1 = bf16[16,80,384]{2,1,0:T(8,128)(2,1)S(1)} async-done(((bf16[16,80,384]{2,1,0:T(8,128)(2,1)}), bf16[16,80,384]{2,1,0:T(8,128)(2,1)S(1)}, u32[]{:S(2)}, u32[]{:S(2)}) %all-to-all-start.1) | async-done | bytes 983072 | tf_op jit(solution)/shard_map/all_to_all | solution.py:455
  99.0 2.1 %shard_map.84 = f32[128,512]{1,0:T(8,128)} custom-call(bf16[1280,384]{1,0:T(8,128)(2,1)} %bitcast.12), custom_call_target="tpu_custom_call" | custom-call | bytes 1245184 | tf_op jit(solution)/shard_map/pallas_call | solution.py:74
  101.1 12.6 %all-to-all-start.2 = ((f32[16,8,512]{2,1,0:T(8,128)}), f32[16,8,512]{2,1,0:T(8,128)S(1)}, u32[]{:S(2)}, u32[]{:S(2)}) async-start(f32[16,8,512]{2,1,0:T(8,128)} %bitcast.14), calls=%async_computation.2 | async-start | bytes 524288 | tf_op jit(solution)/shard_map/all_to_all | solution.py:459
  117.2 4.7 %shard_map.85 = (bf16[128,512]{1,0:T(8,128)(2,1)}, bf16[128,512]{1,0:T(8,128)(2,1)}, bf16[128,1024]{1,0:T(8,128)(2,1)}) custom-call(bf16[512,3072]{1,0:T(8,128)(2,1)} %all-gather.2.cloned.1.call-done.refs_0_, bf16[2,128,512]{2,1,0:T(8,128)(2,1)} %get-tuple-element.94.refs_1_, bf16[2,128,512]{2,1,0:T(8,128)(2,1)} %copy-done.20, ...), custom_call_target="tpu_custom_call" | custom-call | flops 805306368 | bytes 5767168 | tf_op jit(solution)/shard_map/pallas_call | solution.py:74
  122.1 3.3 %all-to-all-done.2 = f32[16,8,512]{2,1,0:T(8,128)S(1)} async-done(((f32[16,8,512]{2,1,0:T(8,128)}), f32[16,8,512]{2,1,0:T(8,128)S(1)}, u32[]{:S(2)}, u32[]{:S(2)}) %all-to-all-start.2) | async-done | bytes 262176 | tf_op jit(solution)/shard_map/all_to_all | solution.py:459
  126.2 1.9 %shard_map.86 = (f32[4,3072]{1,0:T(4,128)}, f32[8,128]{1,0:T(8,128)}, bf16[128,1024]{1,0:T(8,128)(2,1)}) custom-call(f32[128,512]{1,0:T(8,128)} %bitcast.15, bf16[128,512]{1,0:T(8,128)(2,1)} %get-tuple-element.101.refs_1_, bf16[128,512]{1,0:T(8,128)(2,1)} %copy-done.24), custom_call_target="tpu_custom_call" | custom-call | bytes 839680 | tf_op jit(solution)/shard_map/pallas_call | solution.py:74
  (94 shorter events, 12.1 us)
Async XLA Ops:
  9.9 9.2 %collective-permute-start = (bf16[128,1280]{1,0:T(8,128)(2,1)}, bf16[128,1280]{1,0:T(8,128)(2,1)S(1)}, u32[]{:S(2)}, u32[]{:S(2)}) collective-permute-start(bf16[128,1280]{1,0:T(8,128)(2,1)} %get-tuple-element.58), channel_id=1, source_target_pairs={{0,2},{2,0},{16,18},{18,16},{1,3},{3,1},{17,19},{19,17},{4,6},{6,4... | collective-permute-start | bytes 983048 | tf_op jit(solution)/shard_map/ppermute | solution.py:24
  12.5 11.6 %collective-permute-start.3 = (bf16[128,1280]{1,0:T(8,128)(2,1)}, bf16[128,1280]{1,0:T(8,128)(2,1)S(1)}, u32[]{:S(2)}, u32[]{:S(2)}) collective-permute-start(bf16[128,1280]{1,0:T(8,128)(2,1)} %get-tuple-element.60), channel_id=1, source_target_pairs={{0,16},{2,18},{16,0},{18,2},{1,17},{3,19},{17,1},{19,3},{4,20},{6,... | collective-permute-start | bytes 983048 | tf_op jit(solution)/shard_map/ppermute | solution.py:24
  13.8 16.1 %collective-permute-start.5 = (bf16[128,1280]{1,0:T(8,128)(2,1)}, bf16[128,1280]{1,0:T(8,128)(2,1)S(1)}, u32[]{:S(2)}, u32[]{:S(2)}) collective-permute-start(bf16[128,1280]{1,0:T(8,128)(2,1)} %get-tuple-element.61), channel_id=1, source_target_pairs={{0,18},{2,16},{16,2},{18,0},{1,19},{3,17},{17,3},{19,1},{4,22},{6,... | collective-permute-start | bytes 983048 | tf_op jit(solution)/shard_map/ppermute | solution.py:24
  13.8 16.2 %all-to-all-start = ((bf16[4,256,384]{2,1,0:T(8,128)(2,1)}), bf16[4,256,384]{2,1,0:T(8,128)(2,1)S(1)}, u32[]{:S(2)}, u32[]{:S(2)}) async-start(bf16[4,256,384]{2,1,0:T(8,128)(2,1)} %bitcast.16), calls=%async_computation | async-start | bytes 1572864 | tf_op jit(solution)/shard_map/all_to_all | solution.py:419
  17.8 34.8 %copy-start.25 = (bf16[1024]{0:T(1024)(128)(2,1)S(1)}, bf16[1024]{0:T(1024)(128)(2,1)}, u32[]{:S(2)}) copy-start(bf16[1024]{0:T(1024)(128)(2,1)} %param.6) | copy-start | bytes 6148
  17.8 98.7 %all-gather.2.cloned.1.call-start = ((), (), s32[]{:S(2)}) async-start(), calls=%async_computation.3 | async-start | bytes 3932160 | tf_op jit(solution)/shard_map/all_gather | solution.py:427
  19.2 12.4 %copy-start.8 = (bf16[128,1280]{1,0:T(8,128)(2,1)}, bf16[128,1280]{1,0:T(8,128)(2,1)S(1)}, u32[]{:S(2)}) copy-start(bf16[128,1280]{1,0:T(8,128)(2,1)S(1)} %collective-permute-done.refs_2_) | copy-start | bytes 983044
  19.2 10.8 %collective-permute-start.1 = (bf16[128,1280]{1,0:T(8,128)(2,1)}, bf16[128,1280]{1,0:T(8,128)(2,1)S(1)}, u32[]{:S(2)}, u32[]{:S(2)}) collective-permute-start(bf16[128,1280]{1,0:T(8,128)(2,1)} %get-tuple-element.59.refs_0_), channel_id=1, source_target_pairs={{0,1},{1,0},{2,3},{3,2},{4,5},{5,4},{6,7},{7,6},{8,9},{9,8},{10,11... | collective-permute-start | bytes 983048 | tf_op jit(solution)/shard_map/ppermute | solution.py:24
  24.1 5.9 %collective-permute-start.2 = (bf16[128,1280]{1,0:T(8,128)(2,1)S(1)}, bf16[128,1280]{1,0:T(8,128)(2,1)S(1)}, u32[]{:S(2)}, u32[]{:S(2)}) collective-permute-start(bf16[128,1280]{1,0:T(8,128)(2,1)S(1)} %collective-permute-done.refs_2_), channel_id=1, source_target_pairs={{0,1},{1,0},{2,3},{3,2},{4,5},{5,4},{6,7},{7,6},{8,9},{9,8},{10,11... | collective-permute-start | bytes 983048 | tf_op jit(solution)/shard_map/ppermute | solution.py:24
  24.1 7.0 %collective-permute-start.4 = (bf16[128,1280]{1,0:T(8,128)(2,1)S(1)}, bf16[128,1280]{1,0:T(8,128)(2,1)S(1)}, u32[]{:S(2)}, u32[]{:S(2)}) collective-permute-start(bf16[128,1280]{1,0:T(8,128)(2,1)S(1)} %collective-permute-done.3.refs_4_), channel_id=1, source_target_pairs={{0,1},{1,0},{2,3},{3,2},{4,5},{5,4},{6,7},{7,6},{8,9},{9,8},{10,11... | collective-permute-start | bytes 983048 | tf_op jit(solution)/shard_map/ppermute | solution.py:24
  29.8 1.7 %collective-permute-start.6 = (bf16[128,1280]{1,0:T(8,128)(2,1)S(1)}, bf16[128,1280]{1,0:T(8,128)(2,1)S(1)}, u32[]{:S(2)}, u32[]{:S(2)}) collective-permute-start(bf16[128,1280]{1,0:T(8,128)(2,1)S(1)} %collective-permute-done.5.refs_6_), channel_id=1, source_target_pairs={{0,1},{1,0},{2,3},{3,2},{4,5},{5,4},{6,7},{7,6},{8,9},{9,8},{10,11... | collective-permute-start | bytes 983048 | tf_op jit(solution)/shard_map/ppermute | solution.py:24
  36.8 12.7 %collective-permute-start.7 = (bf16[256,128]{1,0:T(8,128)(2,1)}, bf16[256,128]{1,0:T(8,128)(2,1)S(1)}, u32[]{:S(2)}, u32[]{:S(2)}) collective-permute-start(bf16[256,128]{1,0:T(8,128)(2,1)} %get-tuple-element.62.refs_4_), channel_id=1, source_target_pairs={{0,4},{4,0},{8,12},{12,8},{1,5},{5,1},{9,13},{13,9},{2,6},{6,2},{1... | collective-permute-start | bytes 196616 | tf_op jit(solution)/shard_map/ppermute | solution.py:24
  39.9 9.6 %collective-permute-start.8 = (bf16[256,128]{1,0:T(8,128)(2,1)}, bf16[256,128]{1,0:T(8,128)(2,1)S(1)}, u32[]{:S(2)}, u32[]{:S(2)}) collective-permute-start(bf16[256,128]{1,0:T(8,128)(2,1)} %get-tuple-element.62.refs_4_), channel_id=1, source_target_pairs={{0,8},{4,12},{8,0},{12,4},{1,9},{5,13},{9,1},{13,5},{2,10},{6,14},... | collective-permute-start | bytes 196616 | tf_op jit(solution)/shard_map/ppermute | solution.py:24
  43.9 5.8 %collective-permute-start.9 = (bf16[256,128]{1,0:T(8,128)(2,1)}, bf16[256,128]{1,0:T(8,128)(2,1)S(1)}, u32[]{:S(2)}, u32[]{:S(2)}) collective-permute-start(bf16[256,128]{1,0:T(8,128)(2,1)} %get-tuple-element.62.refs_4_), channel_id=1, source_target_pairs={{0,12},{4,8},{8,4},{12,0},{1,13},{5,9},{9,5},{13,1},{2,14},{6,10},... | collective-permute-start | bytes 196616 | tf_op jit(solution)/shard_map/ppermute | solution.py:24
  49.8 4.4 %collective-permute-start.10 = (bf16[128,128]{1,0:T(8,128)(2,1)S(1)}, bf16[128,128]{1,0:T(8,128)(2,1)S(1)}, u32[]{:S(2)}, u32[]{:S(2)}) collective-permute-start(bf16[128,128]{1,0:T(8,128)(2,1)S(1)} %shard_map.78), channel_id=1, source_target_pairs={{0,32},{32,0},{1,33},{33,1},{2,34},{34,2},{3,35},{35,3},{4,36},{36... | collective-permute-start | bytes 98312 | tf_op jit(solution)/shard_map/ppermute | solution.py:24
  55.0 17.3 %copy-start.5 = (f32[8,128]{1,0:T(8,128)}, f32[8,128]{1,0:T(8,128)S(1)}, u32[]{:S(2)}) copy-start(f32[8,128]{1,0:T(8,128)S(1)} %get-tuple-element.93.gain_far) | copy-start | bytes 12292
  55.0 6.5 %collective-permute-start.11 = (bf16[256,128]{1,0:T(8,128)(2,1)S(1)}, bf16[256,128]{1,0:T(8,128)(2,1)S(1)}, u32[]{:S(2)}, u32[]{:S(2)}) collective-permute-start(bf16[256,128]{1,0:T(8,128)(2,1)S(1)} %get-tuple-element.80.refs_0_.refs_5_), channel_id=1, source_target_pairs={{0,4},{4,0},{8,12},{12,8},{1,5},{5,1},{9,13},{13,9},{2,6},{6,2},{1... | collective-permute-start | bytes 196616 | tf_op jit(solution)/shard_map/ppermute | solution.py:24
  56.6 7.2 %collective-permute-start.12 = (bf16[256,128]{1,0:T(8,128)(2,1)S(1)}, bf16[256,128]{1,0:T(8,128)(2,1)S(1)}, u32[]{:S(2)}, u32[]{:S(2)}) collective-permute-start(bf16[256,128]{1,0:T(8,128)(2,1)S(1)} %get-tuple-element.80.refs_0_.refs_5_), channel_id=1, source_target_pairs={{0,8},{4,12},{8,0},{12,4},{1,9},{5,13},{9,1},{13,5},{2,10},{6,14},... | collective-permute-start | bytes 196616 | tf_op jit(solution)/shard_map/ppermute | solution.py:24
  61.5 6.1 %collective-permute-start.13 = (bf16[256,128]{1,0:T(8,128)(2,1)S(1)}, bf16[256,128]{1,0:T(8,128)(2,1)S(1)}, u32[]{:S(2)}, u32[]{:S(2)}) collective-permute-start(bf16[256,128]{1,0:T(8,128)(2,1)S(1)} %get-tuple-element.80.refs_0_.refs_5_), channel_id=1, source_target_pairs={{0,12},{4,8},{8,4},{12,0},{1,13},{5,9},{9,5},{13,1},{2,14},{6,10},... | collective-permute-start | bytes 196616 | tf_op jit(solution)/shard_map/ppermute | solution.py:24
  67.7 4.6 %collective-permute-start.14 = (bf16[128,128]{1,0:T(8,128)(2,1)S(1)}, bf16[128,128]{1,0:T(8,128)(2,1)S(1)}, u32[]{:S(2)}, u32[]{:S(2)}) collective-permute-start(bf16[128,128]{1,0:T(8,128)(2,1)S(1)} %shard_map.80), channel_id=1, source_target_pairs={{0,32},{32,0},{1,33},{33,1},{2,34},{34,2},{3,35},{35,3},{4,36},{36... | collective-permute-start | bytes 98312 | tf_op jit(solution)/shard_map/ppermute | solution.py:24
  74.1 13.7 %copy-start.26 = (bf16[2,128,512]{2,1,0:T(8,128)(2,1)S(1)}, bf16[2,128,512]{2,1,0:T(8,128)(2,1)}, u32[]{:S(2)}) copy-start(bf16[2,128,512]{2,1,0:T(8,128)(2,1)} %get-tuple-element.91) | copy-start | bytes 786436
  74.1 39.6 %copy-start.16 = (bf16[2,128,512]{2,1,0:T(8,128)(2,1)S(1)}, bf16[2,128,512]{2,1,0:T(8,128)(2,1)}, u32[]{:S(2)}) copy-start(bf16[2,128,512]{2,1,0:T(8,128)(2,1)} %get-tuple-element.94.refs_1_) | copy-start | bytes 786436
  78.3 19.8 %all-to-all-start.1 = ((bf16[16,80,384]{2,1,0:T(8,128)(2,1)}), bf16[16,80,384]{2,1,0:T(8,128)(2,1)S(1)}, u32[]{:S(2)}, u32[]{:S(2)}) async-start(bf16[16,80,384]{2,1,0:T(8,128)(2,1)} %bitcast.11), calls=%async_computation.1 | async-start | bytes 1966080 | tf_op jit(solution)/shard_map/all_to_all | solution.py:455
  84.8 28.9 %collective-permute-start.15 = (bf16[2,128,512]{2,1,0:T(8,128)(2,1)S(1)}, bf16[2,128,512]{2,1,0:T(8,128)(2,1)S(1)}, u32[]{:S(2)}, u32[]{:S(2)}) collective-permute-start(bf16[2,128,512]{2,1,0:T(8,128)(2,1)S(1)} %copy-done.28), channel_id=1, source_target_pairs={{0,2},{2,0},{16,18},{18,16},{1,3},{3,1},{17,19},{19,17},{4,6},{6,4... | collective-permute-start | bytes 786440 | tf_op jit(solution)/shard_map/ppermute | solution.py:24
  86.4 27.3 %collective-permute-start.16 = (bf16[2,128,512]{2,1,0:T(8,128)(2,1)S(1)}, bf16[2,128,512]{2,1,0:T(8,128)(2,1)S(1)}, u32[]{:S(2)}, u32[]{:S(2)}) collective-permute-start(bf16[2,128,512]{2,1,0:T(8,128)(2,1)S(1)} %copy-done.27), channel_id=1, source_target_pairs={{0,16},{2,18},{16,0},{18,2},{1,17},{3,19},{17,1},{19,3},{4,20},{6,... | collective-permute-start | bytes 786440 | tf_op jit(solution)/shard_map/ppermute | solution.py:24
  87.8 26.0 %collective-permute-start.17 = (bf16[2,128,512]{2,1,0:T(8,128)(2,1)S(1)}, bf16[2,128,512]{2,1,0:T(8,128)(2,1)S(1)}, u32[]{:S(2)}, u32[]{:S(2)}) collective-permute-start(bf16[2,128,512]{2,1,0:T(8,128)(2,1)S(1)} %copy-done.26), channel_id=1, source_target_pairs={{0,18},{2,16},{16,2},{18,0},{1,19},{3,17},{17,3},{19,1},{4,22},{6,... | collective-permute-start | bytes 786440 | tf_op jit(solution)/shard_map/ppermute | solution.py:24
  101.1 24.3 %all-to-all-start.2 = ((f32[16,8,512]{2,1,0:T(8,128)}), f32[16,8,512]{2,1,0:T(8,128)S(1)}, u32[]{:S(2)}, u32[]{:S(2)}) async-start(f32[16,8,512]{2,1,0:T(8,128)} %bitcast.14), calls=%async_computation.2 | async-start | bytes 524288 | tf_op jit(solution)/shard_map/all_to_all | solution.py:459
  113.8 1.6 %collective-permute-start.18 = (bf16[2,128,512]{2,1,0:T(8,128)(2,1)S(1)}, bf16[2,128,512]{2,1,0:T(8,128)(2,1)S(1)}, u32[]{:S(2)}, u32[]{:S(2)}) collective-permute-start(bf16[2,128,512]{2,1,0:T(8,128)(2,1)S(1)} %copy-done.16), channel_id=1, source_target_pairs={{0,1},{1,0},{2,3},{3,2},{4,5},{5,4},{6,7},{7,6},{8,9},{9,8},{10,11... | collective-permute-start | bytes 786440 | tf_op jit(solution)/shard_map/ppermute | solution.py:24
  114.0 1.8 %collective-permute-start.19 = (bf16[2,128,512]{2,1,0:T(8,128)(2,1)S(1)}, bf16[2,128,512]{2,1,0:T(8,128)(2,1)S(1)}, u32[]{:S(2)}, u32[]{:S(2)}) collective-permute-start(bf16[2,128,512]{2,1,0:T(8,128)(2,1)S(1)} %collective-permute-done.15.refs_3_), channel_id=1, source_target_pairs={{0,1},{1,0},{2,3},{3,2},{4,5},{5,4},{6,7},{7,6},{8,9},{9,8},{10,11... | collective-permute-start | bytes 786440 | tf_op jit(solution)/shard_map/ppermute | solution.py:24
  114.4 1.8 %collective-permute-start.20 = (bf16[2,128,512]{2,1,0:T(8,128)(2,1)S(1)}, bf16[2,128,512]{2,1,0:T(8,128)(2,1)S(1)}, u32[]{:S(2)}, u32[]{:S(2)}) collective-permute-start(bf16[2,128,512]{2,1,0:T(8,128)(2,1)S(1)} %collective-permute-done.16.refs_5_), channel_id=1, source_target_pairs={{0,1},{1,0},{2,3},{3,2},{4,5},{5,4},{6,7},{7,6},{8,9},{9,8},{10,11... | collective-permute-start | bytes 786440 | tf_op jit(solution)/shard_map/ppermute | solution.py:24
  114.5 2.0 %collective-permute-start.21 = (bf16[2,128,512]{2,1,0:T(8,128)(2,1)S(1)}, bf16[2,128,512]{2,1,0:T(8,128)(2,1)S(1)}, u32[]{:S(2)}, u32[]{:S(2)}) collective-permute-start(bf16[2,128,512]{2,1,0:T(8,128)(2,1)S(1)} %collective-permute-done.17.refs_7_), channel_id=1, source_target_pairs={{0,1},{1,0},{2,3},{3,2},{4,5},{5,4},{6,7},{7,6},{8,9},{9,8},{10,11... | collective-permute-start | bytes 786440 | tf_op jit(solution)/shard_map/ppermute | solution.py:24
  121.9 3.5 %collective-permute-start.22 = (bf16[128,512]{1,0:T(8,128)(2,1)}, bf16[128,512]{1,0:T(8,128)(2,1)S(1)}, u32[]{:S(2)}, u32[]{:S(2)}) collective-permute-start(bf16[128,512]{1,0:T(8,128)(2,1)} %get-tuple-element.99), channel_id=1, source_target_pairs={{0,1},{1,0},{2,3},{3,2},{4,5},{5,4},{6,7},{7,6},{8,9},{9,8},{10,11... | collective-permute-start | bytes 393224 | tf_op jit(solution)/shard_map/ppermute | solution.py:24
  (24 other events, 57.4 us)
Sparse Core Ops, SparseCore 0:
  36.9 43.6 all-gather.1

commit v4 on v3

--- a/solution.py
+++ b/solution.py
@@ -41,13 +41,15 @@
     dims = [views[i][0] if i in views else x.shape for i, x in enumerate(arrays)]
 
     def kernel(*refs):
-        given, (*copies, sems), rest = refs[:total], refs[total : total + len(moved) + 1], refs[total + len(moved) + 1 :]
+        given, copies, rest = refs[:total], refs[total : total + len(moved)], refs[total + len(moved) :]
+        sems, rest = (rest[0], rest[1:]) if moved else (None, rest)
+        slots = {i: slot for slot, i in enumerate(moved)}
         near = list(given)
         for slot, i in enumerate(moved):
             near[i] = copies[slot]
         given = [views[i][1](ref) if i in views else ref for i, ref in enumerate(given)]
-        loads = {i: pltpu.make_async_copy(given[i], near[i], sems.at[i]) for i in moved if i < count}
-        stores = {i - count: pltpu.make_async_copy(near[i], given[i], sems.at[i]) for i in moved if i >= count}
+        loads = {i: pltpu.make_async_copy(given[i], near[i], sems.at[slots[i]]) for i in moved if i < count}
+        stores = {i - count: pltpu.make_async_copy(near[i], given[i], sems.at[slots[i]]) for i in moved if i >= count}
         waited, started = set(), set()
 
         def ready(*places):
@@ -77,7 +79,7 @@
         in_specs=[inside if near_in else outside] * count,
         out_specs=[inside if near_out else outside] * len(outs),
         scratch_shapes=[pltpu.VMEM(dims[i], arrays[i].dtype) for i in moved]
-        + [pltpu.SemaphoreType.DMA((total,))]
+        + ([pltpu.SemaphoreType.DMA((len(moved),))] if moved else [])
         + list(scratch),
         cost_estimate=pl.CostEstimate(flops=flops, bytes_accessed=size, transcendentals=0),
         compiler_params=pltpu.CompilerParams(vmem_limit_bytes=limit * 2**20),
@@ -89,11 +91,11 @@
 
 
 def slices(weight, tokens, grad):
-    depth, d, half = weight.shape[0], HEAD_DIM, weight.shape[0] // 2
+    depth, d = weight.shape[0], HEAD_DIM
     n, width = tokens.shape
 
-    def kernel(weight, tokens, grad, heads_out, half_out, b0, b1, b2, b3, head, half_near, tok, cols, sems):
-        me, core = lax.axis_index(CUBE), lax.axis_index("c")
+    def kernel(weight, tokens, grad, heads_out, b0, b1, b2, b3, head, tok, cols, sems):
+        me = lax.axis_index(CUBE)
         loads = [(tokens, tok)]
         for k in range(4):
             at = pl.multiple_of(((me // 2) ^ k) * 2 * d, 2 * d)
@@ -101,7 +103,6 @@
         for part in range(3):
             at = pl.multiple_of((part * HEADS + me) * d, d)
             loads.append((weight.at[:, pl.ds(at, d)], head.at[:, pl.ds(part * d, d)]))
-        loads.append((weight.at[pl.ds(pl.multiple_of(core * half, half), half), :], half_near))
         loads = [pltpu.make_async_copy(x, y, sems.at[i]) for i, (x, y) in enumerate(loads)]
         stores = []
         for k, block in enumerate((b0, b1, b2, b3)):
@@ -109,11 +110,10 @@
             stores.append((cols.at[k], block.at[:, pl.ds(width, 2 * d)]))
         for j in range(4):
             stores.append((head, heads_out.at[pl.ds(j * depth, depth), :]))
-        stores.append((half_near, half_out))
         stores = [pltpu.make_async_copy(x, y, sems.at[i + len(loads)]) for i, (x, y) in enumerate(stores)]
         for copy in loads:
             copy.start()
-        for some, then in ((loads[:5], stores[:8]), (loads[5:8], stores[8:12]), (loads[8:], stores[12:])):
+        for some, then in ((loads[:5], stores[:8]), (loads[5:], stores[8:])):
             for copy in some:
                 copy.wait()
             for copy in then:
@@ -121,17 +121,40 @@
         for copy in stores:
             copy.wait()
 
-    outs = ((4 * depth, 3 * d), (half, weight.shape[1])) + ((n, width + 2 * d),) * 4
-    near = ((depth, 3 * d), (half, weight.shape[1]), (n, width), (4, n, 2 * d))
+    outs = ((4 * depth, 3 * d),) + ((n, width + 2 * d),) * 4
+    near = ((depth, 3 * d), (n, width), (4, n, 2 * d))
     return pl.pallas_call(
         kernel,
         out_shape=[pltpu.HBM(o, BF) for o in outs],
         in_specs=[pl.BlockSpec(memory_space=pltpu.HBM)] * 3,
         out_specs=[pl.BlockSpec(memory_space=pltpu.HBM)] * len(outs),
-        scratch_shapes=[pltpu.VMEM(o, BF) for o in near] + [pltpu.SemaphoreType.DMA((22,))],
+        scratch_shapes=[pltpu.VMEM(o, BF) for o in near] + [pltpu.SemaphoreType.DMA((20,))],
         cost_estimate=pl.CostEstimate(flops=0, bytes_accessed=2**21, transcendentals=0),
         compiler_params=pltpu.CompilerParams(vmem_limit_bytes=60 * 2**20),
     )(weight, tokens, grad)
+
+
+def half_rows(weight):
+    half = weight.shape[0] // 2
+
+    def kernel(weight, out, near, sems):
+        at = pl.multiple_of(lax.axis_index("c") * half, half)
+        load = pltpu.make_async_copy(weight.at[pl.ds(at, half), :], near, sems.at[0])
+        load.start()
+        load.wait()
+        store = pltpu.make_async_copy(near, out, sems.at[1])
+        store.start()
+        store.wait()
+
+    return pl.pallas_call(
+        kernel,
+        out_shape=pltpu.HBM((half, weight.shape[1]), BF),
+        in_specs=[pl.BlockSpec(memory_space=pltpu.HBM)],
+        out_specs=pl.BlockSpec(memory_space=pltpu.HBM),
+        scratch_shapes=[pltpu.VMEM((half, weight.shape[1]), BF), pltpu.SemaphoreType.DMA((2,))],
+        cost_estimate=pl.CostEstimate(flops=0, bytes_accessed=2**21, transcendentals=0),
+        compiler_params=pltpu.CompilerParams(vmem_limit_bytes=60 * 2**20),
+    )(weight)
 
 
 def load_rows(pieces, rows, width, sems):
@@ -151,8 +174,8 @@
 
     def kernel(w_far, *refs):
         pieces, (query, key, value, states, upstream, w, tokens, sems) = refs[:8], refs[8:]
+        at = pl.multiple_of(width + lax.axis_index("c") * d, d)
         me = lax.axis_index(CUBE)
-        at = pl.multiple_of(width + lax.axis_index("c") * d, d)
         first = pltpu.make_async_copy(w_far, w, sems.at[16])
         first.start()
         loads = load_rows(pieces, tokens, width, sems)
@@ -162,13 +185,11 @@
             ups.append(pltpu.make_async_copy(pieces[k].at[:, pl.ds(at, d)], upstream.at[place, :], sems.at[8 + k]))
             ups[-1].start()
         first.wait()
-        for p in range(4):
-            loads[2 * p].wait()
-            loads[2 * p + 1].wait()
-            place = pl.ds(pl.multiple_of(((me // 2) ^ p) * 2 * n, 2 * n), 2 * n)
-            got = dot(tokens[place, :], w[...], NN).astype(BF)
-            for part, ref in enumerate((query, key, value)):
-                ref[place, :] = got[:, part * d : (part + 1) * d]
+        for load in loads:
+            load.wait()
+        got = dot(tokens[...], w[...], NN).astype(BF)
+        for part, ref in enumerate((query, key, value)):
+            ref[...] = got[:, part * d : (part + 1) * d]
         half = 4 * n
         for s in range(2):
             place = pl.ds(s * half, half)
@@ -324,7 +345,7 @@
             load.wait()
         second.wait()
         terms = in_parts(gain[:1, :])
-        step, share = 256, width // 16
+        step, share = 256, width // 4
         for j in range(width // step):
             got = dot(tokens[:, j * step : (j + 1) * step].T, joined[...], NN).astype(BF)
             for i in range(step // share):
@@ -337,12 +358,12 @@
 
     return pl.pallas_call(
         kernel,
-        out_shape=pltpu.HBM((width + 256, 3 * d), BF),
+        out_shape=pltpu.HBM((width + 64, 3 * d), BF),
         in_specs=[pl.BlockSpec(memory_space=pltpu.HBM)] * 10,
         out_specs=pl.BlockSpec(memory_space=pltpu.HBM),
         scratch_shapes=[
             pltpu.VMEM((rows, 3 * d), BF), pltpu.VMEM((8, d), F32), pltpu.VMEM((rows, width), BF),
-            pltpu.VMEM((width + 256, 3 * d), BF), pltpu.SemaphoreType.DMA((11,)),
+            pltpu.VMEM((width + 64, 3 * d), BF), pltpu.SemaphoreType.DMA((11,)),
         ],
         cost_estimate=pl.CostEstimate(flops=2 * rows * width * 3 * d, bytes_accessed=2**22, transcendentals=0),
         compiler_params=pltpu.CompilerParams(vmem_limit_bytes=60 * 2**20),
@@ -373,31 +394,31 @@
 def add_first(ready, finish, pieces, out):
     ready()
     d = HEAD_DIM
-    whole, width = pieces.shape[0] // 16, pieces.shape[1]
+    whole = pieces.shape[0] // 4
     rows = whole - 16
-    for yl in range(2):
-        total = sum(
-            pieces[pl.ds(((dp * 2 + yh) * 2 + yl) * whole, whole), :].astype(F32) for dp in range(4) for yh in range(2)
-        )
-        gain = total[rows : rows + 1]
-        gain = jnp.broadcast_to(gain[:, :d] + gain[:, d : 2 * d] + gain[:, 2 * d :], (4, d))
-        for j in range(16):
-            place = pl.ds(j * 8 + yl * 4, 4)
-            out[place, :width] = total[j * 4 : j * 4 + 4, :]
-            out[place, width:] = gain
+    total = sum(pieces[pl.ds(dp * whole, whole), :].astype(F32) for dp in range(4))
+    gain = total[rows : rows + 1]
+    gain = in_parts(gain[:, :d] + gain[:, d : 2 * d] + gain[:, 2 * d :])[:1, :].astype(F32)
+    place = lax.broadcasted_iota(jnp.int32, (4, d), 0)
+    parts = jnp.where(place == 0, gain[:, :d], jnp.where(place == 1, gain[:, d : 2 * d], gain[:, 2 * d :]))
+    parts = jnp.where(place == 3, 0.0, parts)
+    for j in range(rows // 4):
+        four = total[j * 4 : j * 4 + 4]
+        message = jnp.concatenate([four[:, :d], four[:, d : 2 * d], four[:, 2 * d :], parts], axis=0)
+        out[j * 16 : j * 16 + 16, :] = message.astype(BF)
 
 
 def add_up(ready, finish, pieces, keep, got, weight_grad, gain_grad, input_grad):
     ready()
     d = HEAD_DIM
-    for low in range(4):
-        total = sum(pieces[pl.ds((run * 4 + low) * 8, 8), :] for run in range(4)) / 4
-        for yl in range(2):
-            h = yl * 4 + low
-            for part in range(3):
-                at = (part * HEADS + h) * d
-                weight_grad[:, at : at + d] = total[yl * 4 : yl * 4 + 4, part * d : (part + 1) * d]
-            gain_grad[h : h + 1, :] = total[yl * 4 : yl * 4 + 1, 3 * d :]
+    for h in range(HEADS):
+        yl, low = h // 4, h % 4
+        places = [((yh * 2 + yl) * 4 + run) * 4 + low for yh in range(2) for run in range(4)]
+        total = sum(pieces[i * 16 : i * 16 + 16, :].astype(F32) for i in places) / 4
+        for part in range(3):
+            at = (part * HEADS + h) * d
+            weight_grad[:, at : at + d] = total[part * 4 : part * 4 + 4]
+        gain_grad[h : h + 1, :] = jnp.sum(total[12:], axis=0, keepdims=True)
     width = keep.shape[1] // 4
     even = lax.axis_index("c") == 0
     for p in range(4):
@@ -414,10 +435,11 @@
     inner = out_gain.shape[0]
     depth = qkv_weight.shape[0]
 
-    w_heads, w_half, *blocks = slices(qkv_weight, block, out_grad[0])
+    w_heads, *blocks = slices(qkv_weight, block, out_grad[0])
     near = [swap(blocks[bit], ("yl", "zl"), bit, 4) for bit in (1, 2, 3)]
     w_cols = lax.all_to_all(w_heads, "dp", 0, 0, tiled=True)
-    mine, _ = together(blocks[0], near[0])
+    w_half = half_rows(qkv_weight)
+    mine, *_ = together(blocks[0], near[0], w_half)
     pieces = [x for side in [mine] + near for x in (side, swap(side, "c", 1, 2))]
 
     rows = 8 * n
@@ -452,11 +474,11 @@
     )
     late = [late[0]] + [swap(late[bit], ("yl", "zl"), bit, 4) for bit in (1, 2, 3)]
     weight_part = weigh(joined, gain_sum, pieces, width)
-    sums = lax.all_to_all(weight_part, ("dp", "yh", "yl"), 0, 0, tiled=True)
-    (sums,) = call(add_first, (shape((rows // 8, 4 * d), F32),), sums)
+    sums = lax.all_to_all(weight_part, "dp", 0, 0, tiled=True)
+    (sums,) = call(add_first, (shape((width, d), BF),), sums, near_in=True, limit=12)
     *late, _ = together(*late, sums)
     late = [x for side in late for x in (side, swap(side, "c", 1, 2))]
-    sums = lax.all_to_all(sums, ("zh", "zm", "zl", "c"), 0, 0, tiled=True)
+    sums = lax.all_to_all(sums, SEQ, 0, 0, tiled=True)
     half = shape((n, width // 2), BF)
     keep, send, attended = call(
         at_home, (half, half, shape((n, inner), BF)), w_mine, *late,
@@ -465,7 +487,8 @@
     got = swap(send, "c", 1, 2)
     sums, got = together(sums, got)
     weight_grad, gain_grad, input_grad = call(
-        add_up, (shape((width // 256, 3 * inner), F32), shape((HEADS, d), F32), shape((n, width), BF)), sums, keep, got
+        add_up, (shape((width // 256, 3 * inner), F32), shape((HEADS, d), F32), shape((n, width), BF)), sums, keep, got,
+        near_in=True, limit=12,
     )
     return (attended[None], input_grad[None], weight_grad, gain_grad.reshape(inner))
 

time: 135 us -> 125 us (0.926)
  waiting for transfers between devices: 26.5 us -> 19 us
    all_to_all x2, waiting for transfers between devices: 13.6 us -> 7.8 us  [the longest x1 4.51 us: local(): sums = lax.all_to_all(weight_part, 'dp', 0, 0, tiled=True)]
    pallas_call x9, Pallas kernels: 13.8 us -> 11 us  [call(): pl.pallas_call(kernel, out_shape=[o if near_out else pltpu.HBM(o.shape, o...]
    all_to_all x2, starting transfers between devices: 19.1 us -> 16.9 us  [the longest x1 13.3 us: local(): sums = lax.all_to_all(sums, SEQ, 0, 0, tiled=True)]
    pallas_call x1 -> x2, Pallas kernels: 4.18 us -> 6.18 us  [the longest x1 4.13 us: weigh(): pl.pallas_call(kernel, out_shape=pltpu.HBM((width + 64, 3 * d), BF), in_s...]
    ppermute x23, waiting for transfers between devices: 12.9 us -> 11.2 us  [swap(): return lax.ppermute(x, axes, [(i, i ^ bit) for i in range(count)])]
    unnamed x58 -> x56, local copies, waits for them, and re-layouts: 7.8 us -> 7 us
  transfers between devices with their start and end apart: 27 -> 27, of which waited for: 14 -> 13; matrix products, arithmetic and copies ran while one was open for 0% -> 0% of each run, Pallas kernels for 12% -> 13%
where the time goes in v4:
time: 125 us; the launch traced here: 124 us
  starting transfers between devices  59.8 us (48%)
  Pallas kernels  24.1 us (19%)
  waiting for transfers between devices  19 us (15%)
  between operations  14.4 us (12%)
  local copies, waits for them, and re-layouts  7.01 us (6%)
    ppermute x23, starting transfers between devices, swap(): return lax.ppermute(x, axes, [(i, i ^ bit) for i in range(count)])  38.9 us
    all_to_all x1, starting transfers between devices, local(): sums = lax.all_to_all(sums, SEQ, 0, 0, tiled=True)  13.3 us
    ppermute x23, waiting for transfers between devices, swap(): return lax.ppermute(x, axes, [(i, i ^ bit) for i in range(count)])  11.2 us
    pallas_call x9, Pallas kernels, call(): pl.pallas_call(kernel, out_shape=[o if near_out else pltpu.HBM(o.shape, o...  11 us
    unnamed x56, local copies, waits for them, and re-layouts  7 us
    all_to_all x1, waiting for transfers between devices, local(): sums = lax.all_to_all(weight_part, 'dp', 0, 0, tiled=True)  4.51 us
    pallas_call x1, Pallas kernels, project(): pl.pallas_call(kernel, out_shape=[column, column, column, shape((2 * d, d...  4.4 us
    pallas_call x1, Pallas kernels, weigh(): pl.pallas_call(kernel, out_shape=pltpu.HBM((width + 64, 3 * d), BF), in_s...  4.13 us
  transfers between devices with their start and end apart: 27, of which 13 were waited for; matrix products, arithmetic and copies ran while one was open for 0% of the time, Pallas kernels for 13%

profile of v4, /device:TPU:1, one launch (start us, length us, event | category | flops | bytes accessed | tf_op | source)
XLA Modules:
  0.0 124.3 jit_solution(3179766684874547608)
XLA Ops:
  7.2 2.5 %shard_map.76 = (bf16[1024,384]{1,0:T(8,128)(2,1)}, bf16[128,1280]{1,0:T(8,128)(2,1)}, bf16[128,1280]{1,0:T(8,128)(2,1)}, bf16[128,1280]{1,0:T(8,128)(2,1)}, bf16[128,1280]{1,0:T(8,128)(2,1)}) custom-call(bf16[256,3072]{1,0:T(8,128)(2,1)} %weight.3, bf16[128,1024]{1,0:T(8,128)(2,1)} %bitcast.17, bf16[128,1024]{1,0:T(8,128)(2,1)} %bitcast.18), custom_call_target="tpu_custom_call" | custom-call | bytes 2097152 | tf_op jit(solution)/shard_map/pallas_call | solution.py:126
  9.7 2.6 %collective-permute-start = (bf16[128,1280]{1,0:T(8,128)(2,1)}, bf16[128,1280]{1,0:T(8,128)(2,1)S(1)}, u32[]{:S(2)}, u32[]{:S(2)}) collective-permute-start(bf16[128,1280]{1,0:T(8,128)(2,1)} %get-tuple-element.56), channel_id=1, source_target_pairs={{0,2},{2,0},{16,18},{18,16},{1,3},{3,1},{17,19},{19,17},{4,6},{6,4... | collective-permute-start | bytes 983048 | tf_op jit(solution)/shard_map/ppermute | solution.py:24
  12.2 1.3 %collective-permute-start.3 = (bf16[128,1280]{1,0:T(8,128)(2,1)}, bf16[128,1280]{1,0:T(8,128)(2,1)S(1)}, u32[]{:S(2)}, u32[]{:S(2)}) collective-permute-start(bf16[128,1280]{1,0:T(8,128)(2,1)} %get-tuple-element.58), channel_id=1, source_target_pairs={{0,16},{2,18},{16,0},{18,2},{1,17},{3,19},{17,1},{19,3},{4,20},{6,... | collective-permute-start | bytes 983048 | tf_op jit(solution)/shard_map/ppermute | solution.py:24
  13.5 4.0 %all-to-all-start = ((bf16[4,256,384]{2,1,0:T(8,128)(2,1)}), bf16[4,256,384]{2,1,0:T(8,128)(2,1)S(1)}, u32[]{:S(2)}, u32[]{:S(2)}) async-start(bf16[4,256,384]{2,1,0:T(8,128)(2,1)} %bitcast.16), calls=%async_computation | async-start | bytes 1572864 | tf_op jit(solution)/shard_map/all_to_all | solution.py:440
  17.6 2.0 %shard_map.75 = bf16[128,3072]{1,0:T(8,128)(2,1)} custom-call(bf16[256,3072]{1,0:T(8,128)(2,1)} %weight.3), custom_call_target="tpu_custom_call" | custom-call | bytes 2097152 | tf_op jit(solution)/shard_map/pallas_call | solution.py:149
  19.7 4.2 %collective-permute-start.1 = (bf16[128,1280]{1,0:T(8,128)(2,1)S(1)}, bf16[128,1280]{1,0:T(8,128)(2,1)S(1)}, u32[]{:S(2)}, u32[]{:S(2)}) collective-permute-start(bf16[128,1280]{1,0:T(8,128)(2,1)S(1)} %copy-done.8), channel_id=1, source_target_pairs={{0,1},{1,0},{2,3},{3,2},{4,5},{5,4},{6,7},{7,6},{8,9},{9,8},{10,11... | collective-permute-start | bytes 983048 | tf_op jit(solution)/shard_map/ppermute | solution.py:24
  24.0 5.6 %collective-permute-start.4 = (bf16[128,1280]{1,0:T(8,128)(2,1)S(1)}, bf16[128,1280]{1,0:T(8,128)(2,1)S(1)}, u32[]{:S(2)}, u32[]{:S(2)}) collective-permute-start(bf16[128,1280]{1,0:T(8,128)(2,1)S(1)} %collective-permute-done.3.refs_4_), channel_id=1, source_target_pairs={{0,1},{1,0},{2,3},{3,2},{4,5},{5,4},{6,7},{7,6},{8,9},{9,8},{10,11... | collective-permute-start | bytes 983048 | tf_op jit(solution)/shard_map/ppermute | solution.py:24
  29.8 1.1 collective-permute-done.4.refs_5_
  32.1 4.4 %shard_map.77 = (bf16[1024,128]{1,0:T(8,128)(2,1)}, bf16[1024,128]{1,0:T(8,128)(2,1)}, bf16[1024,128]{1,0:T(8,128)(2,1)}, bf16[256,128]{1,0:T(8,128)(2,1)}, bf16[1024,128]{1,0:T(8,128)(2,1)}) custom-call(bf16[1024,384]{1,0:T(8,128)(2,1)} %bitcast.14, bf16[128,1280]{1,0:T(8,128)(2,1)} %get-tuple-element.57.refs_0_, bf16[128,1280]{1,0:T(8,128)(2,1)} %copy-done.12, ...), custom_call_target="tpu_custom_call" | custom-call | flops 805306368 | bytes 4194304 | tf_op jit(solution)/shard_map/pallas_call | solution.py:201
  36.5 3.1 %collective-permute-start.7 = (bf16[256,128]{1,0:T(8,128)(2,1)}, bf16[256,128]{1,0:T(8,128)(2,1)S(1)}, u32[]{:S(2)}, u32[]{:S(2)}) collective-permute-start(bf16[256,128]{1,0:T(8,128)(2,1)} %get-tuple-element.60.refs_4_), channel_id=1, source_target_pairs={{0,4},{4,0},{8,12},{12,8},{1,5},{5,1},{9,13},{13,9},{2,6},{6,2},{1... | collective-permute-start | bytes 196616 | tf_op jit(solution)/shard_map/ppermute | solution.py:24
  39.6 4.0 %collective-permute-start.8 = (bf16[256,128]{1,0:T(8,128)(2,1)}, bf16[256,128]{1,0:T(8,128)(2,1)S(1)}, u32[]{:S(2)}, u32[]{:S(2)}) collective-permute-start(bf16[256,128]{1,0:T(8,128)(2,1)} %get-tuple-element.60.refs_4_), channel_id=1, source_target_pairs={{0,8},{4,12},{8,0},{12,4},{1,9},{5,13},{9,1},{13,5},{2,10},{6,14},... | collective-permute-start | bytes 196616 | tf_op jit(solution)/shard_map/ppermute | solution.py:24
  43.6 0.9 copy-done
  45.5 0.9 copy-done.2
  46.5 0.9 copy-done.3
  49.5 2.8 %collective-permute-start.10 = (bf16[128,128]{1,0:T(8,128)(2,1)S(1)}, bf16[128,128]{1,0:T(8,128)(2,1)S(1)}, u32[]{:S(2)}, u32[]{:S(2)}) collective-permute-start(bf16[128,128]{1,0:T(8,128)(2,1)S(1)} %shard_map.79), channel_id=1, source_target_pairs={{0,32},{32,0},{1,33},{33,1},{2,34},{34,2},{3,35},{35,3},{4,36},{36... | collective-permute-start | bytes 98312 | tf_op jit(solution)/shard_map/ppermute | solution.py:24
  52.3 1.6 %collective-permute-done.10.refs_6_ = bf16[128,128]{1,0:T(8,128)(2,1)S(1)} collective-permute-done((bf16[128,128]{1,0:T(8,128)(2,1)S(1)}, bf16[128,128]{1,0:T(8,128)(2,1)S(1)}, u32[]{:S(2)}, u32[]{:S(2)}) %collective-permute-start.10) | collective-permute-done | bytes 32800 | tf_op jit(solution)/shard_map/ppermute | solution.py:24
  54.6 1.4 %collective-permute-start.11 = (bf16[256,128]{1,0:T(8,128)(2,1)S(1)}, bf16[256,128]{1,0:T(8,128)(2,1)S(1)}, u32[]{:S(2)}, u32[]{:S(2)}) collective-permute-start(bf16[256,128]{1,0:T(8,128)(2,1)S(1)} %get-tuple-element.78.refs_0_.refs_5_), channel_id=1, source_target_pairs={{0,4},{4,0},{8,12},{12,8},{1,5},{5,1},{9,13},{13,9},{2,6},{6,2},{1... | collective-permute-start | bytes 196616 | tf_op jit(solution)/shard_map/ppermute | solution.py:24
  56.0 5.0 %collective-permute-start.12 = (bf16[256,128]{1,0:T(8,128)(2,1)S(1)}, bf16[256,128]{1,0:T(8,128)(2,1)S(1)}, u32[]{:S(2)}, u32[]{:S(2)}) collective-permute-start(bf16[256,128]{1,0:T(8,128)(2,1)S(1)} %get-tuple-element.78.refs_0_.refs_5_), channel_id=1, source_target_pairs={{0,8},{4,12},{8,0},{12,4},{1,9},{5,13},{9,1},{13,5},{2,10},{6,14},... | collective-permute-start | bytes 196616 | tf_op jit(solution)/shard_map/ppermute | solution.py:24
  61.1 2.3 %collective-permute-done.12.refs_2_.refs_7_ = bf16[256,128]{1,0:T(8,128)(2,1)S(1)} collective-permute-done((bf16[256,128]{1,0:T(8,128)(2,1)S(1)}, bf16[256,128]{1,0:T(8,128)(2,1)S(1)}, u32[]{:S(2)}, u32[]{:S(2)}) %collective-permute-start.12) | collective-permute-done | bytes 65568 | tf_op jit(solution)/shard_map/ppermute | solution.py:24
  63.4 3.5 %collective-permute-done.13.refs_3_.refs_8_ = bf16[256,128]{1,0:T(8,128)(2,1)S(1)} collective-permute-done((bf16[256,128]{1,0:T(8,128)(2,1)S(1)}, bf16[256,128]{1,0:T(8,128)(2,1)S(1)}, u32[]{:S(2)}, u32[]{:S(2)}) %collective-permute-start.13) | collective-permute-done | bytes 65568 | tf_op jit(solution)/shard_map/ppermute | solution.py:24
  66.9 3.0 %collective-permute-start.14 = (bf16[128,128]{1,0:T(8,128)(2,1)S(1)}, bf16[128,128]{1,0:T(8,128)(2,1)S(1)}, u32[]{:S(2)}, u32[]{:S(2)}) collective-permute-start(bf16[128,128]{1,0:T(8,128)(2,1)S(1)} %shard_map.81), channel_id=1, source_target_pairs={{0,32},{32,0},{1,33},{33,1},{2,34},{34,2},{3,35},{35,3},{4,36},{36... | collective-permute-start | bytes 98312 | tf_op jit(solution)/shard_map/ppermute | solution.py:24
  69.9 1.3 %shard_map.82 = (bf16[1024,256]{1,0:T(8,128)(2,1)S(1)}, f32[1024,128]{1,0:T(8,128)S(1)}, f32[1024,128]{1,0:T(8,128)S(1)}) custom-call(bf16[1024,128]{1,0:T(8,128)(2,1)S(1)} %get-tuple-element.68.refs_0_, bf16[1024,128]{1,0:T(8,128)(2,1)S(1)} %get-tuple-element.66.refs_1_.refs_0_, bf16[1024,128]{1,0:T(8,128)(2,1)S(1)} %get-tuple-element.67.refs_2_.refs_1_, ...), custom_call_target="tpu_custom_call" | custom-call | flops 536870912 | bytes 3997696 | tf_op jit(solution)/shard_map/pallas_call | solution.py:76
  71.5 1.6 %shard_map.83 = (bf16[1024,384]{1,0:T(8,128)(2,1)}, bf16[2,128,512]{2,1,0:T(8,128)(2,1)}, bf16[2,128,512]{2,1,0:T(8,128)(2,1)}, bf16[2,128,512]{2,1,0:T(8,128)(2,1)}, bf16[2,128,512]{2,1,0:T(8,128)(2,1)}) custom-call(bf16[1024,128]{1,0:T(8,128)(2,1)S(1)} %get-tuple-element.66.refs_1_.refs_0_, bf16[1024,128]{1,0:T(8,128)(2,1)S(1)} %get-tuple-element.67.refs_2_.refs_1_, ...), custom_call_target="tpu_custom_call" | custom-call | flops 134217728 | bytes 4227072 | tf_op jit(solution)/shard_map/pallas_call | solution.py:76
  73.2 4.1 %shard_map.84 = bf16[1088,384]{1,0:T(8,128)(2,1)} custom-call(bf16[1024,384]{1,0:T(8,128)(2,1)} %get-tuple-element.90.joined_far, f32[8,128]{1,0:T(8,128)} %copy-done.6, bf16[128,1280]{1,0:T(8,128)(2,1)} %get-tuple-element.57.refs_0_, bf16[128,1280]{1,0:T(8,128)(2,1)} %copy-done.12, bf16[128,1280]{1,0:T(8,128)(2,1)} %copy-done.9, ...), custom_call_target="tpu_custom_call" | custom-call | flops 805306368 | bytes 4194304 | tf_op jit(solution)/shard_map/pallas_call | solution.py:359
  77.3 3.6 %all-to-all-start.1 = ((bf16[4,272,384]{2,1,0:T(8,128)(2,1)}), bf16[4,272,384]{2,1,0:T(8,128)(2,1)S(1)}, u32[]{:S(2)}, u32[]{:S(2)}) async-start(bf16[4,272,384]{2,1,0:T(8,128)(2,1)} %bitcast.13), calls=%async_computation.1 | async-start | bytes 1671168 | tf_op jit(solution)/shard_map/all_to_all | solution.py:477
  81.0 1.5 %collective-permute-start.15 = (bf16[2,128,512]{2,1,0:T(8,128)(2,1)S(1)}, bf16[2,128,512]{2,1,0:T(8,128)(2,1)S(1)}, u32[]{:S(2)}, u32[]{:S(2)}) collective-permute-start(bf16[2,128,512]{2,1,0:T(8,128)(2,1)S(1)} %copy-done.27), channel_id=1, source_target_pairs={{0,2},{2,0},{16,18},{18,16},{1,3},{3,1},{17,19},{19,17},{4,6},{6,4... | collective-permute-start | bytes 786440 | tf_op jit(solution)/shard_map/ppermute | solution.py:24
  82.5 1.4 %collective-permute-start.16 = (bf16[2,128,512]{2,1,0:T(8,128)(2,1)S(1)}, bf16[2,128,512]{2,1,0:T(8,128)(2,1)S(1)}, u32[]{:S(2)}, u32[]{:S(2)}) collective-permute-start(bf16[2,128,512]{2,1,0:T(8,128)(2,1)S(1)} %copy-done.26), channel_id=1, source_target_pairs={{0,16},{2,18},{16,0},{18,2},{1,17},{3,19},{17,1},{19,3},{4,20},{6,... | collective-permute-start | bytes 786440 | tf_op jit(solution)/shard_map/ppermute | solution.py:24
  83.9 1.2 collective-permute-start.17
  85.1 4.5 %all-to-all-done.1 = bf16[4,272,384]{2,1,0:T(8,128)(2,1)S(1)} async-done(((bf16[4,272,384]{2,1,0:T(8,128)(2,1)}), bf16[4,272,384]{2,1,0:T(8,128)(2,1)S(1)}, u32[]{:S(2)}, u32[]{:S(2)}) %all-to-all-start.1) | async-done | bytes 835616 | tf_op jit(solution)/shard_map/all_to_all | solution.py:477
  90.4 13.3 %all-to-all-start.2 = ((bf16[64,16,128]{2,1,0:T(8,128)(2,1)}), bf16[64,16,128]{2,1,0:T(8,128)(2,1)S(1)}, u32[]{:S(2)}, u32[]{:S(2)}) async-start(bf16[64,16,128]{2,1,0:T(8,128)(2,1)} %bitcast.15), calls=%async_computation.2 | async-start | bytes 524288 | tf_op jit(solution)/shard_map/all_to_all | solution.py:481
  107.3 4.6 %shard_map.86 = (bf16[128,512]{1,0:T(8,128)(2,1)}, bf16[128,512]{1,0:T(8,128)(2,1)}, bf16[128,1024]{1,0:T(8,128)(2,1)}) custom-call(bf16[512,3072]{1,0:T(8,128)(2,1)} %all-gather.2.cloned.1.call-done.refs_0_, bf16[2,128,512]{2,1,0:T(8,128)(2,1)} %get-tuple-element.92.refs_1_, bf16[2,128,512]{2,1,0:T(8,128)(2,1)} %copy-done.20, ...), custom_call_target="tpu_custom_call" | custom-call | flops 805306368 | bytes 5767168 | tf_op jit(solution)/shard_map/pallas_call | solution.py:76
  112.4 3.3 %all-to-all-done.2 = bf16[64,16,128]{2,1,0:T(8,128)(2,1)S(1)} async-done(((bf16[64,16,128]{2,1,0:T(8,128)(2,1)}), bf16[64,16,128]{2,1,0:T(8,128)(2,1)S(1)}, u32[]{:S(2)}, u32[]{:S(2)}) %all-to-all-start.2) | async-done | bytes 262176 | tf_op jit(solution)/shard_map/all_to_all | solution.py:481
  (93 shorter events, 12.1 us)
Async XLA Ops:
  9.7 9.9 %collective-permute-start = (bf16[128,1280]{1,0:T(8,128)(2,1)}, bf16[128,1280]{1,0:T(8,128)(2,1)S(1)}, u32[]{:S(2)}, u32[]{:S(2)}) collective-permute-start(bf16[128,1280]{1,0:T(8,128)(2,1)} %get-tuple-element.56), channel_id=1, source_target_pairs={{0,2},{2,0},{16,18},{18,16},{1,3},{3,1},{17,19},{19,17},{4,6},{6,4... | collective-permute-start | bytes 983048 | tf_op jit(solution)/shard_map/ppermute | solution.py:24
  12.2 11.7 %collective-permute-start.3 = (bf16[128,1280]{1,0:T(8,128)(2,1)}, bf16[128,1280]{1,0:T(8,128)(2,1)S(1)}, u32[]{:S(2)}, u32[]{:S(2)}) collective-permute-start(bf16[128,1280]{1,0:T(8,128)(2,1)} %get-tuple-element.58), channel_id=1, source_target_pairs={{0,16},{2,18},{16,0},{18,2},{1,17},{3,19},{17,1},{19,3},{4,20},{6,... | collective-permute-start | bytes 983048 | tf_op jit(solution)/shard_map/ppermute | solution.py:24
  13.5 16.1 %collective-permute-start.5 = (bf16[128,1280]{1,0:T(8,128)(2,1)}, bf16[128,1280]{1,0:T(8,128)(2,1)S(1)}, u32[]{:S(2)}, u32[]{:S(2)}) collective-permute-start(bf16[128,1280]{1,0:T(8,128)(2,1)} %get-tuple-element.59), channel_id=1, source_target_pairs={{0,18},{2,16},{16,2},{18,0},{1,19},{3,17},{17,3},{19,1},{4,22},{6,... | collective-permute-start | bytes 983048 | tf_op jit(solution)/shard_map/ppermute | solution.py:24
  13.5 16.2 %all-to-all-start = ((bf16[4,256,384]{2,1,0:T(8,128)(2,1)}), bf16[4,256,384]{2,1,0:T(8,128)(2,1)S(1)}, u32[]{:S(2)}, u32[]{:S(2)}) async-start(bf16[4,256,384]{2,1,0:T(8,128)(2,1)} %bitcast.16), calls=%async_computation | async-start | bytes 1572864 | tf_op jit(solution)/shard_map/all_to_all | solution.py:440
  17.6 89.0 %all-gather.2.cloned.1.call-start = ((), (), s32[]{:S(2)}) async-start(), calls=%async_computation.3 | async-start | bytes 3932160 | tf_op jit(solution)/shard_map/all_gather | solution.py:449
  19.6 32.6 %copy-start.24 = (bf16[1024]{0:T(1024)(128)(2,1)S(1)}, bf16[1024]{0:T(1024)(128)(2,1)}, u32[]{:S(2)}) copy-start(bf16[1024]{0:T(1024)(128)(2,1)} %param.6) | copy-start | bytes 6148
  19.6 11.7 %copy-start.9 = (bf16[128,1280]{1,0:T(8,128)(2,1)}, bf16[128,1280]{1,0:T(8,128)(2,1)S(1)}, u32[]{:S(2)}) copy-start(bf16[128,1280]{1,0:T(8,128)(2,1)S(1)} %collective-permute-done.refs_2_) | copy-start | bytes 983044
  19.7 10.1 %collective-permute-start.1 = (bf16[128,1280]{1,0:T(8,128)(2,1)S(1)}, bf16[128,1280]{1,0:T(8,128)(2,1)S(1)}, u32[]{:S(2)}, u32[]{:S(2)}) collective-permute-start(bf16[128,1280]{1,0:T(8,128)(2,1)S(1)} %copy-done.8), channel_id=1, source_target_pairs={{0,1},{1,0},{2,3},{3,2},{4,5},{5,4},{6,7},{7,6},{8,9},{9,8},{10,11... | collective-permute-start | bytes 983048 | tf_op jit(solution)/shard_map/ppermute | solution.py:24
  23.9 5.8 %collective-permute-start.2 = (bf16[128,1280]{1,0:T(8,128)(2,1)S(1)}, bf16[128,1280]{1,0:T(8,128)(2,1)S(1)}, u32[]{:S(2)}, u32[]{:S(2)}) collective-permute-start(bf16[128,1280]{1,0:T(8,128)(2,1)S(1)} %collective-permute-done.refs_2_), channel_id=1, source_target_pairs={{0,1},{1,0},{2,3},{3,2},{4,5},{5,4},{6,7},{7,6},{8,9},{9,8},{10,11... | collective-permute-start | bytes 983048 | tf_op jit(solution)/shard_map/ppermute | solution.py:24
  24.0 6.9 %collective-permute-start.4 = (bf16[128,1280]{1,0:T(8,128)(2,1)S(1)}, bf16[128,1280]{1,0:T(8,128)(2,1)S(1)}, u32[]{:S(2)}, u32[]{:S(2)}) collective-permute-start(bf16[128,1280]{1,0:T(8,128)(2,1)S(1)} %collective-permute-done.3.refs_4_), channel_id=1, source_target_pairs={{0,1},{1,0},{2,3},{3,2},{4,5},{5,4},{6,7},{7,6},{8,9},{9,8},{10,11... | collective-permute-start | bytes 983048 | tf_op jit(solution)/shard_map/ppermute | solution.py:24
  29.6 1.7 %collective-permute-start.6 = (bf16[128,1280]{1,0:T(8,128)(2,1)S(1)}, bf16[128,1280]{1,0:T(8,128)(2,1)S(1)}, u32[]{:S(2)}, u32[]{:S(2)}) collective-permute-start(bf16[128,1280]{1,0:T(8,128)(2,1)S(1)} %collective-permute-done.5.refs_6_), channel_id=1, source_target_pairs={{0,1},{1,0},{2,3},{3,2},{4,5},{5,4},{6,7},{7,6},{8,9},{9,8},{10,11... | collective-permute-start | bytes 983048 | tf_op jit(solution)/shard_map/ppermute | solution.py:24
  36.5 12.6 %collective-permute-start.7 = (bf16[256,128]{1,0:T(8,128)(2,1)}, bf16[256,128]{1,0:T(8,128)(2,1)S(1)}, u32[]{:S(2)}, u32[]{:S(2)}) collective-permute-start(bf16[256,128]{1,0:T(8,128)(2,1)} %get-tuple-element.60.refs_4_), channel_id=1, source_target_pairs={{0,4},{4,0},{8,12},{12,8},{1,5},{5,1},{9,13},{13,9},{2,6},{6,2},{1... | collective-permute-start | bytes 196616 | tf_op jit(solution)/shard_map/ppermute | solution.py:24
  39.6 9.5 %collective-permute-start.8 = (bf16[256,128]{1,0:T(8,128)(2,1)}, bf16[256,128]{1,0:T(8,128)(2,1)S(1)}, u32[]{:S(2)}, u32[]{:S(2)}) collective-permute-start(bf16[256,128]{1,0:T(8,128)(2,1)} %get-tuple-element.60.refs_4_), channel_id=1, source_target_pairs={{0,8},{4,12},{8,0},{12,4},{1,9},{5,13},{9,1},{13,5},{2,10},{6,14},... | collective-permute-start | bytes 196616 | tf_op jit(solution)/shard_map/ppermute | solution.py:24
  43.6 5.8 %collective-permute-start.9 = (bf16[256,128]{1,0:T(8,128)(2,1)}, bf16[256,128]{1,0:T(8,128)(2,1)S(1)}, u32[]{:S(2)}, u32[]{:S(2)}) collective-permute-start(bf16[256,128]{1,0:T(8,128)(2,1)} %get-tuple-element.60.refs_4_), channel_id=1, source_target_pairs={{0,12},{4,8},{8,4},{12,0},{1,13},{5,9},{9,5},{13,1},{2,14},{6,10},... | collective-permute-start | bytes 196616 | tf_op jit(solution)/shard_map/ppermute | solution.py:24
  49.5 4.4 %collective-permute-start.10 = (bf16[128,128]{1,0:T(8,128)(2,1)S(1)}, bf16[128,128]{1,0:T(8,128)(2,1)S(1)}, u32[]{:S(2)}, u32[]{:S(2)}) collective-permute-start(bf16[128,128]{1,0:T(8,128)(2,1)S(1)} %shard_map.79), channel_id=1, source_target_pairs={{0,32},{32,0},{1,33},{33,1},{2,34},{34,2},{3,35},{35,3},{4,36},{36... | collective-permute-start | bytes 98312 | tf_op jit(solution)/shard_map/ppermute | solution.py:24
  54.6 16.9 %copy-start.6 = (f32[8,128]{1,0:T(8,128)}, f32[8,128]{1,0:T(8,128)S(1)}, u32[]{:S(2)}) copy-start(f32[8,128]{1,0:T(8,128)S(1)} %get-tuple-element.91.gain_far) | copy-start | bytes 12292
  54.6 6.5 %collective-permute-start.11 = (bf16[256,128]{1,0:T(8,128)(2,1)S(1)}, bf16[256,128]{1,0:T(8,128)(2,1)S(1)}, u32[]{:S(2)}, u32[]{:S(2)}) collective-permute-start(bf16[256,128]{1,0:T(8,128)(2,1)S(1)} %get-tuple-element.78.refs_0_.refs_5_), channel_id=1, source_target_pairs={{0,4},{4,0},{8,12},{12,8},{1,5},{5,1},{9,13},{13,9},{2,6},{6,2},{1... | collective-permute-start | bytes 196616 | tf_op jit(solution)/shard_map/ppermute | solution.py:24
  56.0 7.4 %collective-permute-start.12 = (bf16[256,128]{1,0:T(8,128)(2,1)S(1)}, bf16[256,128]{1,0:T(8,128)(2,1)S(1)}, u32[]{:S(2)}, u32[]{:S(2)}) collective-permute-start(bf16[256,128]{1,0:T(8,128)(2,1)S(1)} %get-tuple-element.78.refs_0_.refs_5_), channel_id=1, source_target_pairs={{0,8},{4,12},{8,0},{12,4},{1,9},{5,13},{9,1},{13,5},{2,10},{6,14},... | collective-permute-start | bytes 196616 | tf_op jit(solution)/shard_map/ppermute | solution.py:24
  61.1 5.8 %collective-permute-start.13 = (bf16[256,128]{1,0:T(8,128)(2,1)S(1)}, bf16[256,128]{1,0:T(8,128)(2,1)S(1)}, u32[]{:S(2)}, u32[]{:S(2)}) collective-permute-start(bf16[256,128]{1,0:T(8,128)(2,1)S(1)} %get-tuple-element.78.refs_0_.refs_5_), channel_id=1, source_target_pairs={{0,12},{4,8},{8,4},{12,0},{1,13},{5,9},{9,5},{13,1},{2,14},{6,10},... | collective-permute-start | bytes 196616 | tf_op jit(solution)/shard_map/ppermute | solution.py:24
  66.9 4.6 %collective-permute-start.14 = (bf16[128,128]{1,0:T(8,128)(2,1)S(1)}, bf16[128,128]{1,0:T(8,128)(2,1)S(1)}, u32[]{:S(2)}, u32[]{:S(2)}) collective-permute-start(bf16[128,128]{1,0:T(8,128)(2,1)S(1)} %shard_map.81), channel_id=1, source_target_pairs={{0,32},{32,0},{1,33},{33,1},{2,34},{34,2},{3,35},{35,3},{4,36},{36... | collective-permute-start | bytes 98312 | tf_op jit(solution)/shard_map/ppermute | solution.py:24
  73.2 10.7 %copy-start.25 = (bf16[2,128,512]{2,1,0:T(8,128)(2,1)S(1)}, bf16[2,128,512]{2,1,0:T(8,128)(2,1)}, u32[]{:S(2)}) copy-start(bf16[2,128,512]{2,1,0:T(8,128)(2,1)} %get-tuple-element.89) | copy-start | bytes 786436
  73.2 30.6 %copy-start.16 = (bf16[2,128,512]{2,1,0:T(8,128)(2,1)S(1)}, bf16[2,128,512]{2,1,0:T(8,128)(2,1)}, u32[]{:S(2)}) copy-start(bf16[2,128,512]{2,1,0:T(8,128)(2,1)} %get-tuple-element.92.refs_1_) | copy-start | bytes 786436
  77.3 12.2 %all-to-all-start.1 = ((bf16[4,272,384]{2,1,0:T(8,128)(2,1)}), bf16[4,272,384]{2,1,0:T(8,128)(2,1)S(1)}, u32[]{:S(2)}, u32[]{:S(2)}) async-start(bf16[4,272,384]{2,1,0:T(8,128)(2,1)} %bitcast.13), calls=%async_computation.1 | async-start | bytes 1671168 | tf_op jit(solution)/shard_map/all_to_all | solution.py:477
  81.0 22.7 %collective-permute-start.15 = (bf16[2,128,512]{2,1,0:T(8,128)(2,1)S(1)}, bf16[2,128,512]{2,1,0:T(8,128)(2,1)S(1)}, u32[]{:S(2)}, u32[]{:S(2)}) collective-permute-start(bf16[2,128,512]{2,1,0:T(8,128)(2,1)S(1)} %copy-done.27), channel_id=1, source_target_pairs={{0,2},{2,0},{16,18},{18,16},{1,3},{3,1},{17,19},{19,17},{4,6},{6,4... | collective-permute-start | bytes 786440 | tf_op jit(solution)/shard_map/ppermute | solution.py:24
  82.5 21.2 %collective-permute-start.16 = (bf16[2,128,512]{2,1,0:T(8,128)(2,1)S(1)}, bf16[2,128,512]{2,1,0:T(8,128)(2,1)S(1)}, u32[]{:S(2)}, u32[]{:S(2)}) collective-permute-start(bf16[2,128,512]{2,1,0:T(8,128)(2,1)S(1)} %copy-done.26), channel_id=1, source_target_pairs={{0,16},{2,18},{16,0},{18,2},{1,17},{3,19},{17,1},{19,3},{4,20},{6,... | collective-permute-start | bytes 786440 | tf_op jit(solution)/shard_map/ppermute | solution.py:24
  83.9 19.8 %collective-permute-start.17 = (bf16[2,128,512]{2,1,0:T(8,128)(2,1)S(1)}, bf16[2,128,512]{2,1,0:T(8,128)(2,1)S(1)}, u32[]{:S(2)}, u32[]{:S(2)}) collective-permute-start(bf16[2,128,512]{2,1,0:T(8,128)(2,1)S(1)} %copy-done.25), channel_id=1, source_target_pairs={{0,18},{2,16},{16,2},{18,0},{1,19},{3,17},{17,3},{19,1},{4,22},{6,... | collective-permute-start | bytes 786440 | tf_op jit(solution)/shard_map/ppermute | solution.py:24
  90.4 25.3 %all-to-all-start.2 = ((bf16[64,16,128]{2,1,0:T(8,128)(2,1)}), bf16[64,16,128]{2,1,0:T(8,128)(2,1)S(1)}, u32[]{:S(2)}, u32[]{:S(2)}) async-start(bf16[64,16,128]{2,1,0:T(8,128)(2,1)} %bitcast.15), calls=%async_computation.2 | async-start | bytes 524288 | tf_op jit(solution)/shard_map/all_to_all | solution.py:481
  103.8 1.7 %collective-permute-start.18 = (bf16[2,128,512]{2,1,0:T(8,128)(2,1)S(1)}, bf16[2,128,512]{2,1,0:T(8,128)(2,1)S(1)}, u32[]{:S(2)}, u32[]{:S(2)}) collective-permute-start(bf16[2,128,512]{2,1,0:T(8,128)(2,1)S(1)} %copy-done.16), channel_id=1, source_target_pairs={{0,1},{1,0},{2,3},{3,2},{4,5},{5,4},{6,7},{7,6},{8,9},{9,8},{10,11... | collective-permute-start | bytes 786440 | tf_op jit(solution)/shard_map/ppermute | solution.py:24
  104.3 1.5 %collective-permute-start.19 = (bf16[2,128,512]{2,1,0:T(8,128)(2,1)S(1)}, bf16[2,128,512]{2,1,0:T(8,128)(2,1)S(1)}, u32[]{:S(2)}, u32[]{:S(2)}) collective-permute-start(bf16[2,128,512]{2,1,0:T(8,128)(2,1)S(1)} %collective-permute-done.15.refs_3_), channel_id=1, source_target_pairs={{0,1},{1,0},{2,3},{3,2},{4,5},{5,4},{6,7},{7,6},{8,9},{9,8},{10,11... | collective-permute-start | bytes 786440 | tf_op jit(solution)/shard_map/ppermute | solution.py:24
  104.4 1.8 %collective-permute-start.20 = (bf16[2,128,512]{2,1,0:T(8,128)(2,1)S(1)}, bf16[2,128,512]{2,1,0:T(8,128)(2,1)S(1)}, u32[]{:S(2)}, u32[]{:S(2)}) collective-permute-start(bf16[2,128,512]{2,1,0:T(8,128)(2,1)S(1)} %collective-permute-done.16.refs_5_), channel_id=1, source_target_pairs={{0,1},{1,0},{2,3},{3,2},{4,5},{5,4},{6,7},{7,6},{8,9},{9,8},{10,11... | collective-permute-start | bytes 786440 | tf_op jit(solution)/shard_map/ppermute | solution.py:24
  104.8 1.8 %collective-permute-start.21 = (bf16[2,128,512]{2,1,0:T(8,128)(2,1)S(1)}, bf16[2,128,512]{2,1,0:T(8,128)(2,1)S(1)}, u32[]{:S(2)}, u32[]{:S(2)}) collective-permute-start(bf16[2,128,512]{2,1,0:T(8,128)(2,1)S(1)} %collective-permute-done.17.refs_7_), channel_id=1, source_target_pairs={{0,1},{1,0},{2,3},{3,2},{4,5},{5,4},{6,7},{7,6},{8,9},{9,8},{10,11... | collective-permute-start | bytes 786440 | tf_op jit(solution)/shard_map/ppermute | solution.py:24
  111.9 3.8 %collective-permute-start.22 = (bf16[128,512]{1,0:T(8,128)(2,1)}, bf16[128,512]{1,0:T(8,128)(2,1)S(1)}, u32[]{:S(2)}, u32[]{:S(2)}) collective-permute-start(bf16[128,512]{1,0:T(8,128)(2,1)} %get-tuple-element.97), channel_id=1, source_target_pairs={{0,1},{1,0},{2,3},{3,2},{4,5},{5,4},{6,7},{7,6},{8,9},{9,8},{10,11... | collective-permute-start | bytes 393224 | tf_op jit(solution)/shard_map/ppermute | solution.py:24
  (23 other events, 60.1 us)
Sparse Core Ops, SparseCore 0:
  36.6 43.6 all-gather.1

commit v5 on v4

--- a/solution.py
+++ b/solution.py
@@ -157,13 +157,13 @@
     )(weight)
 
 
-def load_rows(pieces, rows, width, sems):
+def load_rows(pieces, rows, sems):
     n = pieces[0].shape[0]
     me = lax.axis_index(CUBE)
     copies = []
     for k in range(8):
         place = pl.ds(pl.multiple_of((me ^ k) * n, n), n)
-        copies.append(pltpu.make_async_copy(pieces[k].at[:, pl.ds(0, width)], rows.at[place, :], sems.at[k]))
+        copies.append(pltpu.make_async_copy(pieces[k], rows.at[place, :], sems.at[k]))
         copies[-1].start()
     return copies
 
@@ -173,38 +173,31 @@
     width, rows = w_cols.shape[0], 8 * n
 
     def kernel(w_far, *refs):
-        pieces, (query, key, value, states, upstream, w, tokens, sems) = refs[:8], refs[8:]
+        pieces, (packed, states, w, tokens, sems) = refs[:8], refs[8:]
         at = pl.multiple_of(width + lax.axis_index("c") * d, d)
-        me = lax.axis_index(CUBE)
-        first = pltpu.make_async_copy(w_far, w, sems.at[16])
+        first = pltpu.make_async_copy(w_far, w, sems.at[8])
         first.start()
-        loads = load_rows(pieces, tokens, width, sems)
-        ups = []
-        for k in range(8):
-            place = pl.ds(pl.multiple_of((me ^ k) * n, n), n)
-            ups.append(pltpu.make_async_copy(pieces[k].at[:, pl.ds(at, d)], upstream.at[place, :], sems.at[8 + k]))
-            ups[-1].start()
+        loads = load_rows(pieces, tokens, sems)
         first.wait()
         for load in loads:
             load.wait()
-        got = dot(tokens[...], w[...], NN).astype(BF)
-        for part, ref in enumerate((query, key, value)):
-            ref[...] = got[:, part * d : (part + 1) * d]
+        packed[3 * rows : 4 * rows, :] = tokens[:, pl.ds(at, d)]
+        got = dot(tokens[:, :width], w[...], NN).astype(BF)
+        for part in range(3):
+            packed[part * rows : (part + 1) * rows, :] = got[:, part * d : (part + 1) * d]
         half = 4 * n
         for s in range(2):
-            place = pl.ds(s * half, half)
-            states[pl.ds(s * d, d), :] = dot(key[place, :], value[place, :], TN).astype(BF)
-        for copy in ups:
-            copy.wait()
-
-    column = shape((rows, d), BF)
+            key, value = packed[pl.ds(rows + s * half, half), :], packed[pl.ds(2 * rows + s * half, half), :]
+            states[pl.ds(s * d, d), :] = dot(key, value, TN).astype(BF)
+        packed[4 * rows :, :] = states[...]
+
     return pl.pallas_call(
         kernel,
-        out_shape=[column, column, column, shape((2 * d, d), BF), column],
+        out_shape=[shape((4 * rows + 2 * d, d), BF), shape((2 * d, d), BF)],
         in_specs=[pl.BlockSpec(memory_space=pltpu.HBM)] * 9,
-        out_specs=[pl.BlockSpec(memory_space=pltpu.VMEM)] * 5,
+        out_specs=[pl.BlockSpec(memory_space=pltpu.VMEM)] * 2,
         scratch_shapes=[
-            pltpu.VMEM(w_cols.shape, BF), pltpu.VMEM((rows, width), BF), pltpu.SemaphoreType.DMA((17,))
+            pltpu.VMEM(w_cols.shape, BF), pltpu.VMEM((rows, pieces[0].shape[1]), BF), pltpu.SemaphoreType.DMA((9,))
         ],
         cost_estimate=pl.CostEstimate(flops=2 * rows * width * 3 * d, bytes_accessed=2**22, transcendentals=0),
         compiler_params=pltpu.CompilerParams(vmem_limit_bytes=58 * 2**20),
@@ -215,16 +208,17 @@
     return lax.broadcasted_iota(jnp.int32, (rows, rows), 0) >= lax.broadcasted_iota(jnp.int32, (rows, rows), 1)
 
 
-def inside(ready, finish, query, key, value, upstream, states, scores, intra, *copies):
-    for source, copy in zip((query, key, value, upstream, states), copies):
-        copy[...] = source[...]
-    half = query.shape[0] // 2
+def inside(ready, finish, packed, scores, intra, query, key, value, upstream, states):
+    rows = query.shape[0]
+    for i, copy in enumerate((query, key, value, upstream, states)):
+        copy[...] = packed[i * rows : i * rows + copy.shape[0], :]
+    half = rows // 2
     keep = below(half)
     for s in range(2):
-        rows = pl.ds(s * half, half)
-        got = jnp.where(keep, dot(query[rows, :], key[rows, :], NT), 0.0).astype(BF)
-        scores[rows, :] = got
-        intra[rows, :] = dot(got, value[rows, :], NN)
+        place = pl.ds(s * half, half)
+        got = jnp.where(keep, dot(query[place, :], key[place, :], NT), 0.0).astype(BF)
+        scores[place, :] = got
+        intra[place, :] = dot(got, value[place, :], NN)
 
 
 def combine(ready, finish, mine, a, b, c, out):
@@ -329,45 +323,78 @@
         finish(1 + k)
 
 
-def weigh(joined, gain_sum, pieces, width):
-    n, d = pieces[0].shape[0], HEAD_DIM
-    rows = 8 * n
-
-    def kernel(joined_far, gain_far, *refs):
-        pieces, (out_far, joined, gain, tokens, out, sems) = refs[:8], refs[8:]
-        first = pltpu.make_async_copy(joined_far, joined, sems.at[8])
-        second = pltpu.make_async_copy(gain_far, gain, sems.at[10])
+def turn(pieces, width):
+    n = pieces[0].shape[0]
+    rows, step = 8 * n, 256
+
+    def kernel(*refs):
+        pieces, (out_far, tokens, out, sems) = refs[:8], refs[8:]
+        for load in load_rows(pieces, tokens, sems):
+            load.wait()
+        stores = []
+        for j in range(width // step):
+            part = pl.ds(j * step, step)
+            out[part, :] = tokens[:, j * step : (j + 1) * step].T
+            stores.append(pltpu.make_async_copy(out.at[part, :], out_far.at[part, :], sems.at[8 + j]))
+            stores[-1].start()
+        for store in stores:
+            store.wait()
+
+    return pl.pallas_call(
+        kernel,
+        out_shape=pltpu.HBM((width, rows), BF),
+        in_specs=[pl.BlockSpec(memory_space=pltpu.HBM)] * 8,
+        out_specs=pl.BlockSpec(memory_space=pltpu.HBM),
+        scratch_shapes=[
+            pltpu.VMEM((rows, pieces[0].shape[1]), BF), pltpu.VMEM((width, rows), BF),
+            pltpu.SemaphoreType.DMA((8 + width // step,)),
+        ],
+        cost_estimate=pl.CostEstimate(flops=0, bytes_accessed=2**22, transcendentals=0),
+        compiler_params=pltpu.CompilerParams(vmem_limit_bytes=58 * 2**20),
+    )(*pieces)
+
+
+def weigh(joined, gain_sum, turned):
+    width, rows = turned.shape
+    d = HEAD_DIM
+    step, share = 256, width // 4
+
+    def kernel(joined_far, gain_far, turned_far, out_far, joined, gain, turned, out, sems):
+        first = pltpu.make_async_copy(joined_far, joined, sems.at[0])
+        second = pltpu.make_async_copy(gain_far, gain, sems.at[1])
         first.start()
         second.start()
-        loads = load_rows(pieces, tokens, width, sems)
+        loads, stores = [], []
+        for j in range(width // step):
+            part = pl.ds(j * step, step)
+            loads.append(pltpu.make_async_copy(turned_far.at[part, :], turned.at[part, :], sems.at[2 + j]))
+            loads[-1].start()
         first.wait()
-        for load in loads:
-            load.wait()
         second.wait()
         terms = in_parts(gain[:1, :])
-        step, share = 256, width // 4
         for j in range(width // step):
-            got = dot(tokens[:, j * step : (j + 1) * step].T, joined[...], NN).astype(BF)
-            for i in range(step // share):
-                at = (j * (step // share) + i) * (share + 16)
-                out[at : at + share, :] = got[i * share : (i + 1) * share]
-                out[at + share : at + share + 16, :] = terms
-        last = pltpu.make_async_copy(out, out_far, sems.at[9])
-        last.start()
-        last.wait()
+            loads[j].wait()
+            at = j * (share + 16)
+            out[at : at + share, :] = dot(turned[j * step : (j + 1) * step, :], joined[...], NN).astype(BF)
+            out[at + share : at + share + 16, :] = terms
+            part = pl.ds(at, share + 16)
+            stores.append(pltpu.make_async_copy(out.at[part, :], out_far.at[part, :], sems.at[6 + j]))
+            stores[-1].start()
+        for store in stores:
+            store.wait()
 
     return pl.pallas_call(
         kernel,
         out_shape=pltpu.HBM((width + 64, 3 * d), BF),
-        in_specs=[pl.BlockSpec(memory_space=pltpu.HBM)] * 10,
+        in_specs=[pl.BlockSpec(memory_space=pltpu.HBM)] * 3,
         out_specs=pl.BlockSpec(memory_space=pltpu.HBM),
         scratch_shapes=[
-            pltpu.VMEM((rows, 3 * d), BF), pltpu.VMEM((8, d), F32), pltpu.VMEM((rows, width), BF),
-            pltpu.VMEM((width + 64, 3 * d), BF), pltpu.SemaphoreType.DMA((11,)),
+            pltpu.VMEM((rows, 3 * d), BF), pltpu.VMEM((8, d), F32), pltpu.VMEM((width, rows), BF),
+            pltpu.VMEM((width + 64, 3 * d), BF), pltpu.SemaphoreType.DMA((10,)),
         ],
         cost_estimate=pl.CostEstimate(flops=2 * rows * width * 3 * d, bytes_accessed=2**22, transcendentals=0),
         compiler_params=pltpu.CompilerParams(vmem_limit_bytes=60 * 2**20),
-    )(joined, gain_sum, *pieces)
+    )(joined, gain_sum, turned)
 
 
 def at_home(ready, finish, mine, *refs):
@@ -444,22 +471,25 @@
 
     rows = 8 * n
     column, square = shape((rows, d), BF), shape((2 * d, d), BF)
-    query, key, value, states, upstream = project(w_cols, pieces)
+    packed, states = project(w_cols, pieces)
     w_half, _ = together(w_half, states)
     w_mine = lax.all_gather(w_half, "dp", axis=0, tiled=True)
-    got = [swap(states, RUN, bit, 4) for bit in (1, 2, 3)]
+    got = [swap(states, RUN, bit, 4) for bit in (2, 1, 3)]
+    got = [got[1], got[0], got[2]]
     scores, intra, query, key, value, upstream, states = call(
         inside, (shape((rows, rows // 2), BF), shape((rows, d), F32), column, column, column, column, square),
-        query, key, value, upstream, states, flops=2 * rows * rows * d, near_in=True, near_out=True, limit=12,
-    )
-    scores, *got = together(scores, *got)
+        packed, flops=2 * rows * rows * d, near_in=True, near_out=True, limit=12,
+    )
+    turned = turn(pieces, width)
+    scores, turned, *got = together(scores, turned, *got)
     (both,) = call(combine, (shape((d, d), BF),), states, *got, near_in=True, near_out=True, limit=12)
     far = swap(both, "yh", 1, 2)
     attended_head, mixed_grad, payload, before, gain_sum = call(
         forward, (column, column, square, square, shape((8, d), F32)),
         query, intra, states, *got, far, upstream, out_gain.reshape(1, inner), flops=4 * rows * d * d, near_in=True, near_out=True, limit=12,
     )
-    grads = [swap(payload, RUN, bit, 4) for bit in (1, 2, 3)]
+    grads = [swap(payload, RUN, bit, 4) for bit in (2, 1, 3)]
+    grads = [grads[1], grads[0], grads[2]]
     (both_grad,) = call(combine, (shape((d, d), BF),), payload, *grads, near_in=True, near_out=True, limit=12)
     mixed_grad, both_grad = together(mixed_grad, both_grad)
     sent, key_part, value_part = call(
@@ -473,11 +503,12 @@
         near_in=True, limit=16, scratch=[pltpu.VMEM((HEADS, n, 4 * d), BF)],
     )
     late = [late[0]] + [swap(late[bit], ("yl", "zl"), bit, 4) for bit in (1, 2, 3)]
-    weight_part = weigh(joined, gain_sum, pieces, width)
+    weight_part = weigh(joined, gain_sum, turned)
     sums = lax.all_to_all(weight_part, "dp", 0, 0, tiled=True)
     (sums,) = call(add_first, (shape((width, d), BF),), sums, near_in=True, limit=12)
-    *late, _ = together(*late, sums)
-    late = [x for side in late for x in (side, swap(side, "c", 1, 2))]
+    first = [late[0], swap(late[0], "c", 1, 2)]
+    *rest, _ = together(*late[1:], sums)
+    late = first + [x for side in rest for x in (side, swap(side, "c", 1, 2))]
     sums = lax.all_to_all(sums, SEQ, 0, 0, tiled=True)
     half = shape((n, width // 2), BF)
     keep, send, attended = call(

time: 125 us -> 125 us (level)
  local copies, waits for them, and re-layouts: 7.01 us -> 2.36 us
  Pallas kernels: 24.1 us -> 27.4 us
    unnamed x56 -> x48, local copies, waits for them, and re-layouts: 7 us -> 2.36 us
    pallas_call x1 -> x2, Pallas kernels: 4.4 us -> 7.87 us  [the longest x1 4.57 us: project(): pl.pallas_call(kernel, out_shape=[shape((4 * rows + 2 * d, d), BF), shape...]
  transfers between devices with their start and end apart: 27 -> 27, of which waited for: 13 -> 14; matrix products, arithmetic and copies ran while one was open for 0% -> 0% of each run, Pallas kernels for 13% -> 16%
where the time goes in v5:
time: 125 us; the launch traced here: 124 us
  starting transfers between devices  60.3 us (48%)
  Pallas kernels  27.4 us (22%)
  waiting for transfers between devices  20 us (16%)
  between operations  14.4 us (12%)
  local copies, waits for them, and re-layouts  2.36 us (2%)
    ppermute x23, starting transfers between devices, swap(): return lax.ppermute(x, axes, [(i, i ^ bit) for i in range(count)])  39.2 us
    all_to_all x1, starting transfers between devices, local(): sums = lax.all_to_all(sums, SEQ, 0, 0, tiled=True)  13.3 us
    ppermute x23, waiting for transfers between devices, swap(): return lax.ppermute(x, axes, [(i, i ^ bit) for i in range(count)])  12.1 us
    pallas_call x9, Pallas kernels, call(): pl.pallas_call(kernel, out_shape=[o if near_out else pltpu.HBM(o.shape, o...  11 us
    all_to_all x1, waiting for transfers between devices, local(): sums = lax.all_to_all(weight_part, 'dp', 0, 0, tiled=True)  4.58 us
    pallas_call x1, Pallas kernels, project(): pl.pallas_call(kernel, out_shape=[shape((4 * rows + 2 * d, d), BF), shape...  4.57 us
    all_to_all x1, starting transfers between devices, local(): w_cols = lax.all_to_all(w_heads, 'dp', 0, 0, tiled=True)  4.01 us
    pallas_call x1, Pallas kernels, weigh(): pl.pallas_call(kernel, out_shape=pltpu.HBM((width + 64, 3 * d), BF), in_s...  3.92 us
  transfers between devices with their start and end apart: 27, of which 14 were waited for; matrix products, arithmetic and copies ran while one was open for 0% of the time, Pallas kernels for 16%

profile of v5, /device:TPU:1, one launch (start us, length us, event | category | flops | bytes accessed | tf_op | source)
XLA Modules:
  0.0 124.4 jit_solution(6004897161217531141)
XLA Ops:
  7.2 2.5 %shard_map.76 = (bf16[1024,384]{1,0:T(8,128)(2,1)}, bf16[128,1280]{1,0:T(8,128)(2,1)}, bf16[128,1280]{1,0:T(8,128)(2,1)}, bf16[128,1280]{1,0:T(8,128)(2,1)}, bf16[128,1280]{1,0:T(8,128)(2,1)}) custom-call(bf16[256,3072]{1,0:T(8,128)(2,1)} %weight.3, bf16[128,1024]{1,0:T(8,128)(2,1)} %bitcast.17, bf16[128,1024]{1,0:T(8,128)(2,1)} %bitcast.18), custom_call_target="tpu_custom_call" | custom-call | bytes 2097152 | tf_op jit(solution)/shard_map/pallas_call | solution.py:126
  9.7 2.6 %collective-permute-start = (bf16[128,1280]{1,0:T(8,128)(2,1)}, bf16[128,1280]{1,0:T(8,128)(2,1)S(1)}, u32[]{:S(2)}, u32[]{:S(2)}) collective-permute-start(bf16[128,1280]{1,0:T(8,128)(2,1)} %get-tuple-element.53), channel_id=1, source_target_pairs={{0,2},{2,0},{16,18},{18,16},{1,3},{3,1},{17,19},{19,17},{4,6},{6,4... | collective-permute-start | bytes 983048 | tf_op jit(solution)/shard_map/ppermute | solution.py:24
  12.3 1.3 %collective-permute-start.3 = (bf16[128,1280]{1,0:T(8,128)(2,1)}, bf16[128,1280]{1,0:T(8,128)(2,1)S(1)}, u32[]{:S(2)}, u32[]{:S(2)}) collective-permute-start(bf16[128,1280]{1,0:T(8,128)(2,1)} %get-tuple-element.55), channel_id=1, source_target_pairs={{0,16},{2,18},{16,0},{18,2},{1,17},{3,19},{17,1},{19,3},{4,20},{6,... | collective-permute-start | bytes 983048 | tf_op jit(solution)/shard_map/ppermute | solution.py:24
  13.6 4.0 %all-to-all-start = ((bf16[4,256,384]{2,1,0:T(8,128)(2,1)}), bf16[4,256,384]{2,1,0:T(8,128)(2,1)S(1)}, u32[]{:S(2)}, u32[]{:S(2)}) async-start(bf16[4,256,384]{2,1,0:T(8,128)(2,1)} %bitcast.16), calls=%async_computation | async-start | bytes 1572864 | tf_op jit(solution)/shard_map/all_to_all | solution.py:467
  17.6 2.0 %shard_map.75 = bf16[128,3072]{1,0:T(8,128)(2,1)} custom-call(bf16[256,3072]{1,0:T(8,128)(2,1)} %weight.3), custom_call_target="tpu_custom_call" | custom-call | bytes 2097152 | tf_op jit(solution)/shard_map/pallas_call | solution.py:149
  19.7 4.3 %collective-permute-start.1 = (bf16[128,1280]{1,0:T(8,128)(2,1)S(1)}, bf16[128,1280]{1,0:T(8,128)(2,1)S(1)}, u32[]{:S(2)}, u32[]{:S(2)}) collective-permute-start(bf16[128,1280]{1,0:T(8,128)(2,1)S(1)} %copy-done.4), channel_id=1, source_target_pairs={{0,1},{1,0},{2,3},{3,2},{4,5},{5,4},{6,7},{7,6},{8,9},{9,8},{10,11... | collective-permute-start | bytes 983048 | tf_op jit(solution)/shard_map/ppermute | solution.py:24
  24.0 5.6 %collective-permute-start.4 = (bf16[128,1280]{1,0:T(8,128)(2,1)S(1)}, bf16[128,1280]{1,0:T(8,128)(2,1)S(1)}, u32[]{:S(2)}, u32[]{:S(2)}) collective-permute-start(bf16[128,1280]{1,0:T(8,128)(2,1)S(1)} %collective-permute-done.3.refs_4_), channel_id=1, source_target_pairs={{0,1},{1,0},{2,3},{3,2},{4,5},{5,4},{6,7},{7,6},{8,9},{9,8},{10,11... | collective-permute-start | bytes 983048 | tf_op jit(solution)/shard_map/ppermute | solution.py:24
  29.8 1.1 collective-permute-done.4.refs_5_
  32.1 4.6 %shard_map.77 = (bf16[4352,128]{1,0:T(8,128)(2,1)}, bf16[256,128]{1,0:T(8,128)(2,1)}) custom-call(bf16[1024,384]{1,0:T(8,128)(2,1)} %bitcast.14, bf16[128,1280]{1,0:T(8,128)(2,1)} %get-tuple-element.54.refs_0_, bf16[128,1280]{1,0:T(8,128)(2,1)} %copy-done.8, bf16[128,1280]{1,0:T(8,128)(2,1)} %copy-done.5, bf16[128,1280]{1,0:T(8,128)(2,1)} %copy-done.9, ...), custom_call_target="tpu_custom_call" | custom-call | flops 805306368 | bytes 4194304 | tf_op jit(solution)/shard_map/pallas_call | solution.py:194
  36.7 3.1 %collective-permute-start.7 = (bf16[256,128]{1,0:T(8,128)(2,1)}, bf16[256,128]{1,0:T(8,128)(2,1)S(1)}, u32[]{:S(2)}, u32[]{:S(2)}) collective-permute-start(bf16[256,128]{1,0:T(8,128)(2,1)} %get-tuple-element.57), channel_id=1, source_target_pairs={{0,4},{4,0},{8,12},{12,8},{1,5},{5,1},{9,13},{13,9},{2,6},{6,2},{1... | collective-permute-start | bytes 196616 | tf_op jit(solution)/shard_map/ppermute | solution.py:24
  39.8 4.0 %collective-permute-start.8 = (bf16[256,128]{1,0:T(8,128)(2,1)}, bf16[256,128]{1,0:T(8,128)(2,1)S(1)}, u32[]{:S(2)}, u32[]{:S(2)}) collective-permute-start(bf16[256,128]{1,0:T(8,128)(2,1)} %get-tuple-element.57), channel_id=1, source_target_pairs={{0,8},{4,12},{8,0},{12,4},{1,9},{5,13},{9,1},{13,5},{2,10},{6,14},... | collective-permute-start | bytes 196616 | tf_op jit(solution)/shard_map/ppermute | solution.py:24
  43.8 3.3 %shard_map.79.turned_far = bf16[1024,1024]{1,0:T(8,128)(2,1)} custom-call(bf16[128,1280]{1,0:T(8,128)(2,1)} %get-tuple-element.54.refs_0_, bf16[128,1280]{1,0:T(8,128)(2,1)} %copy-done.8, bf16[128,1280]{1,0:T(8,128)(2,1)} %copy-done.5, bf16[128,1280]{1,0:T(8,128)(2,1)} %copy-done.9, bf16[128,1280]{1,0:T(8,128)(2,1)} %copy-done.6, ...), custom_call_target="tpu_custom_call" | custom-call | bytes 4194304 | tf_op jit(solution)/shard_map/pallas_call | solution.py:343
  48.1 1.4 %collective-permute-done.9.refs_3_.refs_5_ = bf16[256,128]{1,0:T(8,128)(2,1)S(1)} collective-permute-done((bf16[256,128]{1,0:T(8,128)(2,1)}, bf16[256,128]{1,0:T(8,128)(2,1)S(1)}, u32[]{:S(2)}, u32[]{:S(2)}) %collective-permute-start.9) | collective-permute-done | bytes 65568 | tf_op jit(solution)/shard_map/ppermute | solution.py:24
  49.5 2.9 %collective-permute-start.10 = (bf16[128,128]{1,0:T(8,128)(2,1)S(1)}, bf16[128,128]{1,0:T(8,128)(2,1)S(1)}, u32[]{:S(2)}, u32[]{:S(2)}) collective-permute-start(bf16[128,128]{1,0:T(8,128)(2,1)S(1)} %shard_map.80), channel_id=1, source_target_pairs={{0,32},{32,0},{1,33},{33,1},{2,34},{34,2},{3,35},{35,3},{4,36},{36... | collective-permute-start | bytes 98312 | tf_op jit(solution)/shard_map/ppermute | solution.py:24
  52.4 1.4 %collective-permute-done.10.refs_6_ = bf16[128,128]{1,0:T(8,128)(2,1)S(1)} collective-permute-done((bf16[128,128]{1,0:T(8,128)(2,1)S(1)}, bf16[128,128]{1,0:T(8,128)(2,1)S(1)}, u32[]{:S(2)}, u32[]{:S(2)}) %collective-permute-start.10) | collective-permute-done | bytes 32800 | tf_op jit(solution)/shard_map/ppermute | solution.py:24
  54.6 1.1 collective-permute-start.11
  55.7 5.6 %collective-permute-start.12 = (bf16[256,128]{1,0:T(8,128)(2,1)S(1)}, bf16[256,128]{1,0:T(8,128)(2,1)S(1)}, u32[]{:S(2)}, u32[]{:S(2)}) collective-permute-start(bf16[256,128]{1,0:T(8,128)(2,1)S(1)} %get-tuple-element.72.refs_0_.refs_5_), channel_id=1, source_target_pairs={{0,8},{4,12},{8,0},{12,4},{1,9},{5,13},{9,1},{13,5},{2,10},{6,14},... | collective-permute-start | bytes 196616 | tf_op jit(solution)/shard_map/ppermute | solution.py:24
  61.3 2.4 %collective-permute-done.12.refs_2_.refs_7_ = bf16[256,128]{1,0:T(8,128)(2,1)S(1)} collective-permute-done((bf16[256,128]{1,0:T(8,128)(2,1)S(1)}, bf16[256,128]{1,0:T(8,128)(2,1)S(1)}, u32[]{:S(2)}, u32[]{:S(2)}) %collective-permute-start.12) | collective-permute-done | bytes 65568 | tf_op jit(solution)/shard_map/ppermute | solution.py:24
  63.7 3.3 %collective-permute-done.13.refs_3_.refs_8_ = bf16[256,128]{1,0:T(8,128)(2,1)S(1)} collective-permute-done((bf16[256,128]{1,0:T(8,128)(2,1)S(1)}, bf16[256,128]{1,0:T(8,128)(2,1)S(1)}, u32[]{:S(2)}, u32[]{:S(2)}) %collective-permute-start.13) | collective-permute-done | bytes 65568 | tf_op jit(solution)/shard_map/ppermute | solution.py:24
  67.0 3.0 %collective-permute-start.14 = (bf16[128,128]{1,0:T(8,128)(2,1)S(1)}, bf16[128,128]{1,0:T(8,128)(2,1)S(1)}, u32[]{:S(2)}, u32[]{:S(2)}) collective-permute-start(bf16[128,128]{1,0:T(8,128)(2,1)S(1)} %shard_map.82), channel_id=1, source_target_pairs={{0,32},{32,0},{1,33},{33,1},{2,34},{34,2},{3,35},{35,3},{4,36},{36... | collective-permute-start | bytes 98312 | tf_op jit(solution)/shard_map/ppermute | solution.py:24
  70.1 1.3 %shard_map.83 = (bf16[1024,256]{1,0:T(8,128)(2,1)S(1)}, f32[1024,128]{1,0:T(8,128)S(1)}, f32[1024,128]{1,0:T(8,128)S(1)}) custom-call(bf16[1024,128]{1,0:T(8,128)(2,1)S(1)} %get-tuple-element.62.refs_0_, bf16[1024,128]{1,0:T(8,128)(2,1)S(1)} %get-tuple-element.60.refs_1_.refs_0_, bf16[1024,128]{1,0:T(8,128)(2,1)S(1)} %get-tuple-element.61.refs_2_.refs_1_, ...), custom_call_target="tpu_custom_call" | custom-call | flops 536870912 | bytes 3997696 | tf_op jit(solution)/shard_map/pallas_call | solution.py:76
  71.6 1.7 %shard_map.84 = (bf16[1024,384]{1,0:T(8,128)(2,1)}, bf16[2,128,512]{2,1,0:T(8,128)(2,1)}, bf16[2,128,512]{2,1,0:T(8,128)(2,1)}, bf16[2,128,512]{2,1,0:T(8,128)(2,1)}, bf16[2,128,512]{2,1,0:T(8,128)(2,1)}) custom-call(bf16[1024,128]{1,0:T(8,128)(2,1)S(1)} %get-tuple-element.60.refs_1_.refs_0_, bf16[1024,128]{1,0:T(8,128)(2,1)S(1)} %get-tuple-element.61.refs_2_.refs_1_, ...), custom_call_target="tpu_custom_call" | custom-call | flops 134217728 | bytes 4227072 | tf_op jit(solution)/shard_map/pallas_call | solution.py:76
  73.3 3.9 %shard_map.85 = bf16[1088,384]{1,0:T(8,128)(2,1)} custom-call(bf16[1024,384]{1,0:T(8,128)(2,1)} %get-tuple-element.84.joined_far, f32[8,128]{1,0:T(8,128)} %copy-done.2, bf16[1024,1024]{1,0:T(8,128)(2,1)} %shard_map.79.turned_far), custom_call_target="tpu_custom_call" | custom-call | flops 805306368 | bytes 4194304 | tf_op jit(solution)/shard_map/pallas_call | solution.py:386
  77.3 3.8 %all-to-all-start.1 = ((bf16[4,272,384]{2,1,0:T(8,128)(2,1)}), bf16[4,272,384]{2,1,0:T(8,128)(2,1)S(1)}, u32[]{:S(2)}, u32[]{:S(2)}) async-start(bf16[4,272,384]{2,1,0:T(8,128)(2,1)} %bitcast.13), calls=%async_computation.1 | async-start | bytes 1671168 | tf_op jit(solution)/shard_map/all_to_all | solution.py:507
  81.1 1.9 %collective-permute-start.16 = (bf16[2,128,512]{2,1,0:T(8,128)(2,1)S(1)}, bf16[2,128,512]{2,1,0:T(8,128)(2,1)S(1)}, u32[]{:S(2)}, u32[]{:S(2)}) collective-permute-start(bf16[2,128,512]{2,1,0:T(8,128)(2,1)S(1)} %copy-done.23), channel_id=1, source_target_pairs={{0,2},{2,0},{16,18},{18,16},{1,3},{3,1},{17,19},{19,17},{4,6},{6,4... | collective-permute-start | bytes 786440 | tf_op jit(solution)/shard_map/ppermute | solution.py:24
  83.1 0.9 collective-permute-start.17
  84.0 1.2 collective-permute-start.18
  85.1 4.6 %all-to-all-done.1 = bf16[4,272,384]{2,1,0:T(8,128)(2,1)S(1)} async-done(((bf16[4,272,384]{2,1,0:T(8,128)(2,1)}), bf16[4,272,384]{2,1,0:T(8,128)(2,1)S(1)}, u32[]{:S(2)}, u32[]{:S(2)}) %all-to-all-start.1) | async-done | bytes 835616 | tf_op jit(solution)/shard_map/all_to_all | solution.py:507
  90.6 13.3 %all-to-all-start.2 = ((bf16[64,16,128]{2,1,0:T(8,128)(2,1)}), bf16[64,16,128]{2,1,0:T(8,128)(2,1)S(1)}, u32[]{:S(2)}, u32[]{:S(2)}) async-start(bf16[64,16,128]{2,1,0:T(8,128)(2,1)} %bitcast.15), calls=%async_computation.2 | async-start | bytes 524288 | tf_op jit(solution)/shard_map/all_to_all | solution.py:512
  107.5 4.6 %shard_map.87 = (bf16[128,512]{1,0:T(8,128)(2,1)}, bf16[128,512]{1,0:T(8,128)(2,1)}, bf16[128,1024]{1,0:T(8,128)(2,1)}) custom-call(bf16[512,3072]{1,0:T(8,128)(2,1)} %all-gather.2.cloned.1.call-done.refs_0_, bf16[2,128,512]{2,1,0:T(8,128)(2,1)} %get-tuple-element.80.refs_1_, bf16[2,128,512]{2,1,0:T(8,128)(2,1)} %copy-done.16, ...), custom_call_target="tpu_custom_call" | custom-call | flops 805306368 | bytes 5767168 | tf_op jit(solution)/shard_map/pallas_call | solution.py:76
  112.5 3.3 %all-to-all-done.2 = bf16[64,16,128]{2,1,0:T(8,128)(2,1)S(1)} async-done(((bf16[64,16,128]{2,1,0:T(8,128)(2,1)}), bf16[64,16,128]{2,1,0:T(8,128)(2,1)S(1)}, u32[]{:S(2)}, u32[]{:S(2)}) %all-to-all-start.2) | async-done | bytes 262176 | tf_op jit(solution)/shard_map/all_to_all | solution.py:512
  115.8 0.9 copy-done.1
  (86 shorter events, 9.1 us)
Async XLA Ops:
  9.7 9.9 %collective-permute-start = (bf16[128,1280]{1,0:T(8,128)(2,1)}, bf16[128,1280]{1,0:T(8,128)(2,1)S(1)}, u32[]{:S(2)}, u32[]{:S(2)}) collective-permute-start(bf16[128,1280]{1,0:T(8,128)(2,1)} %get-tuple-element.53), channel_id=1, source_target_pairs={{0,2},{2,0},{16,18},{18,16},{1,3},{3,1},{17,19},{19,17},{4,6},{6,4... | collective-permute-start | bytes 983048 | tf_op jit(solution)/shard_map/ppermute | solution.py:24
  12.3 11.7 %collective-permute-start.3 = (bf16[128,1280]{1,0:T(8,128)(2,1)}, bf16[128,1280]{1,0:T(8,128)(2,1)S(1)}, u32[]{:S(2)}, u32[]{:S(2)}) collective-permute-start(bf16[128,1280]{1,0:T(8,128)(2,1)} %get-tuple-element.55), channel_id=1, source_target_pairs={{0,16},{2,18},{16,0},{18,2},{1,17},{3,19},{17,1},{19,3},{4,20},{6,... | collective-permute-start | bytes 983048 | tf_op jit(solution)/shard_map/ppermute | solution.py:24
  13.6 16.1 %collective-permute-start.5 = (bf16[128,1280]{1,0:T(8,128)(2,1)}, bf16[128,1280]{1,0:T(8,128)(2,1)S(1)}, u32[]{:S(2)}, u32[]{:S(2)}) collective-permute-start(bf16[128,1280]{1,0:T(8,128)(2,1)} %get-tuple-element.56), channel_id=1, source_target_pairs={{0,18},{2,16},{16,2},{18,0},{1,19},{3,17},{17,3},{19,1},{4,22},{6,... | collective-permute-start | bytes 983048 | tf_op jit(solution)/shard_map/ppermute | solution.py:24
  13.6 16.2 %all-to-all-start = ((bf16[4,256,384]{2,1,0:T(8,128)(2,1)}), bf16[4,256,384]{2,1,0:T(8,128)(2,1)S(1)}, u32[]{:S(2)}, u32[]{:S(2)}) async-start(bf16[4,256,384]{2,1,0:T(8,128)(2,1)} %bitcast.16), calls=%async_computation | async-start | bytes 1572864 | tf_op jit(solution)/shard_map/all_to_all | solution.py:467
  17.6 89.2 %all-gather.2.cloned.1.call-start = ((), (), s32[]{:S(2)}) async-start(), calls=%async_computation.3 | async-start | bytes 3932160 | tf_op jit(solution)/shard_map/all_gather | solution.py:476
  19.6 11.7 %copy-start.5 = (bf16[128,1280]{1,0:T(8,128)(2,1)}, bf16[128,1280]{1,0:T(8,128)(2,1)S(1)}, u32[]{:S(2)}) copy-start(bf16[128,1280]{1,0:T(8,128)(2,1)S(1)} %collective-permute-done.refs_2_) | copy-start | bytes 983044
  19.7 10.1 %collective-permute-start.1 = (bf16[128,1280]{1,0:T(8,128)(2,1)S(1)}, bf16[128,1280]{1,0:T(8,128)(2,1)S(1)}, u32[]{:S(2)}, u32[]{:S(2)}) collective-permute-start(bf16[128,1280]{1,0:T(8,128)(2,1)S(1)} %copy-done.4), channel_id=1, source_target_pairs={{0,1},{1,0},{2,3},{3,2},{4,5},{5,4},{6,7},{7,6},{8,9},{9,8},{10,11... | collective-permute-start | bytes 983048 | tf_op jit(solution)/shard_map/ppermute | solution.py:24
  23.9 5.8 %collective-permute-start.2 = (bf16[128,1280]{1,0:T(8,128)(2,1)S(1)}, bf16[128,1280]{1,0:T(8,128)(2,1)S(1)}, u32[]{:S(2)}, u32[]{:S(2)}) collective-permute-start(bf16[128,1280]{1,0:T(8,128)(2,1)S(1)} %collective-permute-done.refs_2_), channel_id=1, source_target_pairs={{0,1},{1,0},{2,3},{3,2},{4,5},{5,4},{6,7},{7,6},{8,9},{9,8},{10,11... | collective-permute-start | bytes 983048 | tf_op jit(solution)/shard_map/ppermute | solution.py:24
  24.0 6.9 %collective-permute-start.4 = (bf16[128,1280]{1,0:T(8,128)(2,1)S(1)}, bf16[128,1280]{1,0:T(8,128)(2,1)S(1)}, u32[]{:S(2)}, u32[]{:S(2)}) collective-permute-start(bf16[128,1280]{1,0:T(8,128)(2,1)S(1)} %collective-permute-done.3.refs_4_), channel_id=1, source_target_pairs={{0,1},{1,0},{2,3},{3,2},{4,5},{5,4},{6,7},{7,6},{8,9},{9,8},{10,11... | collective-permute-start | bytes 983048 | tf_op jit(solution)/shard_map/ppermute | solution.py:24
  29.6 1.7 %collective-permute-start.6 = (bf16[128,1280]{1,0:T(8,128)(2,1)S(1)}, bf16[128,1280]{1,0:T(8,128)(2,1)S(1)}, u32[]{:S(2)}, u32[]{:S(2)}) collective-permute-start(bf16[128,1280]{1,0:T(8,128)(2,1)S(1)} %collective-permute-done.5.refs_6_), channel_id=1, source_target_pairs={{0,1},{1,0},{2,3},{3,2},{4,5},{5,4},{6,7},{7,6},{8,9},{9,8},{10,11... | collective-permute-start | bytes 983048 | tf_op jit(solution)/shard_map/ppermute | solution.py:24
  36.7 15.7 %copy-start.20 = (bf16[1024]{0:T(1024)(128)(2,1)S(1)}, bf16[1024]{0:T(1024)(128)(2,1)}, u32[]{:S(2)}) copy-start(bf16[1024]{0:T(1024)(128)(2,1)} %param.6) | copy-start | bytes 6148
  36.7 11.3 %collective-permute-start.7 = (bf16[256,128]{1,0:T(8,128)(2,1)}, bf16[256,128]{1,0:T(8,128)(2,1)S(1)}, u32[]{:S(2)}, u32[]{:S(2)}) collective-permute-start(bf16[256,128]{1,0:T(8,128)(2,1)} %get-tuple-element.57), channel_id=1, source_target_pairs={{0,4},{4,0},{8,12},{12,8},{1,5},{5,1},{9,13},{13,9},{2,6},{6,2},{1... | collective-permute-start | bytes 196616 | tf_op jit(solution)/shard_map/ppermute | solution.py:24
  39.8 8.3 %collective-permute-start.8 = (bf16[256,128]{1,0:T(8,128)(2,1)}, bf16[256,128]{1,0:T(8,128)(2,1)S(1)}, u32[]{:S(2)}, u32[]{:S(2)}) collective-permute-start(bf16[256,128]{1,0:T(8,128)(2,1)} %get-tuple-element.57), channel_id=1, source_target_pairs={{0,8},{4,12},{8,0},{12,4},{1,9},{5,13},{9,1},{13,5},{2,10},{6,14},... | collective-permute-start | bytes 196616 | tf_op jit(solution)/shard_map/ppermute | solution.py:24
  43.8 5.6 %collective-permute-start.9 = (bf16[256,128]{1,0:T(8,128)(2,1)}, bf16[256,128]{1,0:T(8,128)(2,1)S(1)}, u32[]{:S(2)}, u32[]{:S(2)}) collective-permute-start(bf16[256,128]{1,0:T(8,128)(2,1)} %get-tuple-element.57), channel_id=1, source_target_pairs={{0,12},{4,8},{8,4},{12,0},{1,13},{5,9},{9,5},{13,1},{2,14},{6,10},... | collective-permute-start | bytes 196616 | tf_op jit(solution)/shard_map/ppermute | solution.py:24
  49.5 4.4 %collective-permute-start.10 = (bf16[128,128]{1,0:T(8,128)(2,1)S(1)}, bf16[128,128]{1,0:T(8,128)(2,1)S(1)}, u32[]{:S(2)}, u32[]{:S(2)}) collective-permute-start(bf16[128,128]{1,0:T(8,128)(2,1)S(1)} %shard_map.80), channel_id=1, source_target_pairs={{0,32},{32,0},{1,33},{33,1},{2,34},{34,2},{3,35},{35,3},{4,36},{36... | collective-permute-start | bytes 98312 | tf_op jit(solution)/shard_map/ppermute | solution.py:24
  54.6 17.0 %copy-start.2 = (f32[8,128]{1,0:T(8,128)}, f32[8,128]{1,0:T(8,128)S(1)}, u32[]{:S(2)}) copy-start(f32[8,128]{1,0:T(8,128)S(1)} %get-tuple-element.85.gain_far) | copy-start | bytes 12292
  54.6 6.6 %collective-permute-start.11 = (bf16[256,128]{1,0:T(8,128)(2,1)S(1)}, bf16[256,128]{1,0:T(8,128)(2,1)S(1)}, u32[]{:S(2)}, u32[]{:S(2)}) collective-permute-start(bf16[256,128]{1,0:T(8,128)(2,1)S(1)} %get-tuple-element.72.refs_0_.refs_5_), channel_id=1, source_target_pairs={{0,4},{4,0},{8,12},{12,8},{1,5},{5,1},{9,13},{13,9},{2,6},{6,2},{1... | collective-permute-start | bytes 196616 | tf_op jit(solution)/shard_map/ppermute | solution.py:24
  55.7 8.0 %collective-permute-start.12 = (bf16[256,128]{1,0:T(8,128)(2,1)S(1)}, bf16[256,128]{1,0:T(8,128)(2,1)S(1)}, u32[]{:S(2)}, u32[]{:S(2)}) collective-permute-start(bf16[256,128]{1,0:T(8,128)(2,1)S(1)} %get-tuple-element.72.refs_0_.refs_5_), channel_id=1, source_target_pairs={{0,8},{4,12},{8,0},{12,4},{1,9},{5,13},{9,1},{13,5},{2,10},{6,14},... | collective-permute-start | bytes 196616 | tf_op jit(solution)/shard_map/ppermute | solution.py:24
  61.3 5.8 %collective-permute-start.13 = (bf16[256,128]{1,0:T(8,128)(2,1)S(1)}, bf16[256,128]{1,0:T(8,128)(2,1)S(1)}, u32[]{:S(2)}, u32[]{:S(2)}) collective-permute-start(bf16[256,128]{1,0:T(8,128)(2,1)S(1)} %get-tuple-element.72.refs_0_.refs_5_), channel_id=1, source_target_pairs={{0,12},{4,8},{8,4},{12,0},{1,13},{5,9},{9,5},{13,1},{2,14},{6,10},... | collective-permute-start | bytes 196616 | tf_op jit(solution)/shard_map/ppermute | solution.py:24
  67.0 4.6 %collective-permute-start.14 = (bf16[128,128]{1,0:T(8,128)(2,1)S(1)}, bf16[128,128]{1,0:T(8,128)(2,1)S(1)}, u32[]{:S(2)}, u32[]{:S(2)}) collective-permute-start(bf16[128,128]{1,0:T(8,128)(2,1)S(1)} %shard_map.82), channel_id=1, source_target_pairs={{0,32},{32,0},{1,33},{33,1},{2,34},{34,2},{3,35},{35,3},{4,36},{36... | collective-permute-start | bytes 98312 | tf_op jit(solution)/shard_map/ppermute | solution.py:24
  73.3 10.6 %copy-start.21 = (bf16[2,128,512]{2,1,0:T(8,128)(2,1)S(1)}, bf16[2,128,512]{2,1,0:T(8,128)(2,1)}, u32[]{:S(2)}) copy-start(bf16[2,128,512]{2,1,0:T(8,128)(2,1)} %get-tuple-element.83) | copy-start | bytes 786436
  77.3 26.6 %copy-start.12 = (bf16[2,128,512]{2,1,0:T(8,128)(2,1)S(1)}, bf16[2,128,512]{2,1,0:T(8,128)(2,1)}, u32[]{:S(2)}) copy-start(bf16[2,128,512]{2,1,0:T(8,128)(2,1)} %get-tuple-element.80.refs_1_) | copy-start | bytes 786436
  77.3 12.4 %all-to-all-start.1 = ((bf16[4,272,384]{2,1,0:T(8,128)(2,1)}), bf16[4,272,384]{2,1,0:T(8,128)(2,1)S(1)}, u32[]{:S(2)}, u32[]{:S(2)}) async-start(bf16[4,272,384]{2,1,0:T(8,128)(2,1)} %bitcast.13), calls=%async_computation.1 | async-start | bytes 1671168 | tf_op jit(solution)/shard_map/all_to_all | solution.py:507
  81.1 23.3 %collective-permute-start.16 = (bf16[2,128,512]{2,1,0:T(8,128)(2,1)S(1)}, bf16[2,128,512]{2,1,0:T(8,128)(2,1)S(1)}, u32[]{:S(2)}, u32[]{:S(2)}) collective-permute-start(bf16[2,128,512]{2,1,0:T(8,128)(2,1)S(1)} %copy-done.23), channel_id=1, source_target_pairs={{0,2},{2,0},{16,18},{18,16},{1,3},{3,1},{17,19},{19,17},{4,6},{6,4... | collective-permute-start | bytes 786440 | tf_op jit(solution)/shard_map/ppermute | solution.py:24
  83.1 21.3 %collective-permute-start.17 = (bf16[2,128,512]{2,1,0:T(8,128)(2,1)S(1)}, bf16[2,128,512]{2,1,0:T(8,128)(2,1)S(1)}, u32[]{:S(2)}, u32[]{:S(2)}) collective-permute-start(bf16[2,128,512]{2,1,0:T(8,128)(2,1)S(1)} %copy-done.22), channel_id=1, source_target_pairs={{0,16},{2,18},{16,0},{18,2},{1,17},{3,19},{17,1},{19,3},{4,20},{6,... | collective-permute-start | bytes 786440 | tf_op jit(solution)/shard_map/ppermute | solution.py:24
  84.0 20.4 %collective-permute-start.18 = (bf16[2,128,512]{2,1,0:T(8,128)(2,1)S(1)}, bf16[2,128,512]{2,1,0:T(8,128)(2,1)S(1)}, u32[]{:S(2)}, u32[]{:S(2)}) collective-permute-start(bf16[2,128,512]{2,1,0:T(8,128)(2,1)S(1)} %copy-done.21), channel_id=1, source_target_pairs={{0,18},{2,16},{16,2},{18,0},{1,19},{3,17},{17,3},{19,1},{4,22},{6,... | collective-permute-start | bytes 786440 | tf_op jit(solution)/shard_map/ppermute | solution.py:24
  90.6 25.3 %all-to-all-start.2 = ((bf16[64,16,128]{2,1,0:T(8,128)(2,1)}), bf16[64,16,128]{2,1,0:T(8,128)(2,1)S(1)}, u32[]{:S(2)}, u32[]{:S(2)}) async-start(bf16[64,16,128]{2,1,0:T(8,128)(2,1)} %bitcast.15), calls=%async_computation.2 | async-start | bytes 524288 | tf_op jit(solution)/shard_map/all_to_all | solution.py:512
  103.8 1.7 %collective-permute-start.15 = (bf16[2,128,512]{2,1,0:T(8,128)(2,1)S(1)}, bf16[2,128,512]{2,1,0:T(8,128)(2,1)S(1)}, u32[]{:S(2)}, u32[]{:S(2)}) collective-permute-start(bf16[2,128,512]{2,1,0:T(8,128)(2,1)S(1)} %copy-done.12), channel_id=1, source_target_pairs={{0,1},{1,0},{2,3},{3,2},{4,5},{5,4},{6,7},{7,6},{8,9},{9,8},{10,11... | collective-permute-start | bytes 786440 | tf_op jit(solution)/shard_map/ppermute | solution.py:24
  104.4 1.6 %collective-permute-start.19 = (bf16[2,128,512]{2,1,0:T(8,128)(2,1)S(1)}, bf16[2,128,512]{2,1,0:T(8,128)(2,1)S(1)}, u32[]{:S(2)}, u32[]{:S(2)}) collective-permute-start(bf16[2,128,512]{2,1,0:T(8,128)(2,1)S(1)} %collective-permute-done.16.refs_3_), channel_id=1, source_target_pairs={{0,1},{1,0},{2,3},{3,2},{4,5},{5,4},{6,7},{7,6},{8,9},{9,8},{10,11... | collective-permute-start | bytes 786440 | tf_op jit(solution)/shard_map/ppermute | solution.py:24
  104.6 1.9 %collective-permute-start.20 = (bf16[2,128,512]{2,1,0:T(8,128)(2,1)S(1)}, bf16[2,128,512]{2,1,0:T(8,128)(2,1)S(1)}, u32[]{:S(2)}, u32[]{:S(2)}) collective-permute-start(bf16[2,128,512]{2,1,0:T(8,128)(2,1)S(1)} %collective-permute-done.17.refs_5_), channel_id=1, source_target_pairs={{0,1},{1,0},{2,3},{3,2},{4,5},{5,4},{6,7},{7,6},{8,9},{9,8},{10,11... | collective-permute-start | bytes 786440 | tf_op jit(solution)/shard_map/ppermute | solution.py:24
  105.0 1.8 %collective-permute-start.21 = (bf16[2,128,512]{2,1,0:T(8,128)(2,1)S(1)}, bf16[2,128,512]{2,1,0:T(8,128)(2,1)S(1)}, u32[]{:S(2)}, u32[]{:S(2)}) collective-permute-start(bf16[2,128,512]{2,1,0:T(8,128)(2,1)S(1)} %collective-permute-done.18.refs_7_), channel_id=1, source_target_pairs={{0,1},{1,0},{2,3},{3,2},{4,5},{5,4},{6,7},{7,6},{8,9},{9,8},{10,11... | collective-permute-start | bytes 786440 | tf_op jit(solution)/shard_map/ppermute | solution.py:24
  112.2 3.7 %collective-permute-start.22 = (bf16[128,512]{1,0:T(8,128)(2,1)}, bf16[128,512]{1,0:T(8,128)(2,1)S(1)}, u32[]{:S(2)}, u32[]{:S(2)}) collective-permute-start(bf16[128,512]{1,0:T(8,128)(2,1)} %get-tuple-element.91), channel_id=1, source_target_pairs={{0,1},{1,0},{2,3},{3,2},{4,5},{5,4},{6,7},{7,6},{8,9},{9,8},{10,11... | collective-permute-start | bytes 393224 | tf_op jit(solution)/shard_map/ppermute | solution.py:24
  (19 other events, 65.0 us)
Sparse Core Ops, SparseCore 0:
  36.8 43.6 all-gather.1

commit v6 on v4

--- a/solution.py
+++ b/solution.py
@@ -408,13 +408,24 @@
         out[j * 16 : j * 16 + 16, :] = message.astype(BF)
 
 
+def add_second(ready, finish, pieces, out):
+    ready()
+    rows = pieces.shape[0] // 4
+    for yl in range(2):
+        total = pieces[yl * rows : (yl + 1) * rows, :].astype(F32) + pieces[
+            (2 + yl) * rows : (3 + yl) * rows, :
+        ].astype(F32)
+        for j in range(16):
+            out[j * 32 + yl * 16 : j * 32 + yl * 16 + 16, :] = total[j * 16 : j * 16 + 16]
+
+
 def add_up(ready, finish, pieces, keep, got, weight_grad, gain_grad, input_grad):
     ready()
     d = HEAD_DIM
     for h in range(HEADS):
         yl, low = h // 4, h % 4
-        places = [((yh * 2 + yl) * 4 + run) * 4 + low for yh in range(2) for run in range(4)]
-        total = sum(pieces[i * 16 : i * 16 + 16, :].astype(F32) for i in places) / 4
+        places = [(run * 4 + low) * 32 + yl * 16 for run in range(4)]
+        total = sum(pieces[at : at + 16, :] for at in places) / 4
         for part in range(3):
             at = (part * HEADS + h) * d
             weight_grad[:, at : at + d] = total[part * 4 : part * 4 + 4]
@@ -478,7 +489,9 @@
     (sums,) = call(add_first, (shape((width, d), BF),), sums, near_in=True, limit=12)
     *late, _ = together(*late, sums)
     late = [x for side in late for x in (side, swap(side, "c", 1, 2))]
-    sums = lax.all_to_all(sums, SEQ, 0, 0, tiled=True)
+    sums = lax.all_to_all(sums, ("yh", "yl"), 0, 0, tiled=True)
+    (sums,) = call(add_second, (shape((width // 2, d), F32),), sums, near_in=True, limit=12)
+    sums = lax.all_to_all(sums, ("zh", "zm", "zl", "c"), 0, 0, tiled=True)
     half = shape((n, width // 2), BF)
     keep, send, attended = call(
         at_home, (half, half, shape((n, inner), BF)), w_mine, *late,

time: 125 us -> 133 us (1.064)
  blocking collectives: 0 us -> 10.1 us
  starting transfers between devices: 59.8 us -> 57.5 us
    all_to_all x0 -> x1, blocking collectives: none -> 10.1 us  [local(): sums = lax.all_to_all(sums, ('yh', 'yl'), 0, 0, tiled=True)]
    all_to_all x1, starting transfers between devices: 13.3 us -> 11.1 us  [local(): sums = lax.all_to_all(sums, ('zh', 'zm', 'zl', 'c'), 0, 0, tiled=True)]
    pallas_call x9 -> x10, Pallas kernels: 11 us -> 11.7 us  [call(): pl.pallas_call(kernel, out_shape=[o if near_out else pltpu.HBM(o.shape, o...]
where the time goes in v6:
time: 133 us
  starting transfers between devices  57.5 us (43%)
  Pallas kernels  24.8 us (19%)
  waiting for transfers between devices  19 us (14%)
  between operations  14.4 us (11%)
  blocking collectives  10.1 us (8%)
  local copies, waits for them, and re-layouts  7.01 us (5%)
    ppermute x23, starting transfers between devices, swap(): return lax.ppermute(x, axes, [(i, i ^ bit) for i in range(count)])  38.6 us
    pallas_call x10, Pallas kernels, call(): pl.pallas_call(kernel, out_shape=[o if near_out else pltpu.HBM(o.shape, o...  11.7 us
    ppermute x23, waiting for transfers between devices, swap(): return lax.ppermute(x, axes, [(i, i ^ bit) for i in range(count)])  11.2 us
    all_to_all x1, starting transfers between devices, local(): sums = lax.all_to_all(sums, ('zh', 'zm', 'zl', 'c'), 0, 0, tiled=True)  11.1 us
    all_to_all x1, blocking collectives, local(): sums = lax.all_to_all(sums, ('yh', 'yl'), 0, 0, tiled=True)  10.1 us
    unnamed x56, local copies, waits for them, and re-layouts  7 us
    all_to_all x1, waiting for transfers between devices, local(): sums = lax.all_to_all(weight_part, 'dp', 0, 0, tiled=True)  4.53 us
    pallas_call x1, Pallas kernels, project(): pl.pallas_call(kernel, out_shape=[column, column, column, shape((2 * d, d...  4.4 us
  transfers between devices with their start and end apart: 27, of which 13 were waited for; matrix products, arithmetic and copies ran while one was open for 0% of the time, Pallas kernels for 13%

profile of v6, /device:TPU:1, one launch (start us, length us, event | category | flops | bytes accessed | tf_op | source)
XLA Modules:
  0.0 132.8 jit_solution(3766238306685039526)
XLA Ops:
  7.2 2.5 %shard_map.76 = (bf16[1024,384]{1,0:T(8,128)(2,1)}, bf16[128,1280]{1,0:T(8,128)(2,1)}, bf16[128,1280]{1,0:T(8,128)(2,1)}, bf16[128,1280]{1,0:T(8,128)(2,1)}, bf16[128,1280]{1,0:T(8,128)(2,1)}) custom-call(bf16[256,3072]{1,0:T(8,128)(2,1)} %weight.3, bf16[128,1024]{1,0:T(8,128)(2,1)} %bitcast.21, bf16[128,1024]{1,0:T(8,128)(2,1)} %bitcast.22), custom_call_target="tpu_custom_call" | custom-call | bytes 2097152 | tf_op jit(solution)/shard_map/pallas_call | solution.py:126
  9.7 2.6 %collective-permute-start = (bf16[128,1280]{1,0:T(8,128)(2,1)}, bf16[128,1280]{1,0:T(8,128)(2,1)S(1)}, u32[]{:S(2)}, u32[]{:S(2)}) collective-permute-start(bf16[128,1280]{1,0:T(8,128)(2,1)} %get-tuple-element.56), channel_id=1, source_target_pairs={{0,2},{2,0},{16,18},{18,16},{1,3},{3,1},{17,19},{19,17},{4,6},{6,4... | collective-permute-start | bytes 983048 | tf_op jit(solution)/shard_map/ppermute | solution.py:24
  12.2 1.3 collective-permute-start.3
  13.5 4.0 %all-to-all-start = ((bf16[4,256,384]{2,1,0:T(8,128)(2,1)}), bf16[4,256,384]{2,1,0:T(8,128)(2,1)S(1)}, u32[]{:S(2)}, u32[]{:S(2)}) async-start(bf16[4,256,384]{2,1,0:T(8,128)(2,1)} %bitcast.20), calls=%async_computation | async-start | bytes 1572864 | tf_op jit(solution)/shard_map/all_to_all | solution.py:451
  17.6 2.0 %shard_map.75 = bf16[128,3072]{1,0:T(8,128)(2,1)} custom-call(bf16[256,3072]{1,0:T(8,128)(2,1)} %weight.3), custom_call_target="tpu_custom_call" | custom-call | bytes 2097152 | tf_op jit(solution)/shard_map/pallas_call | solution.py:149
  19.7 4.2 %collective-permute-start.1 = (bf16[128,1280]{1,0:T(8,128)(2,1)S(1)}, bf16[128,1280]{1,0:T(8,128)(2,1)S(1)}, u32[]{:S(2)}, u32[]{:S(2)}) collective-permute-start(bf16[128,1280]{1,0:T(8,128)(2,1)S(1)} %copy-done.8), channel_id=1, source_target_pairs={{0,1},{1,0},{2,3},{3,2},{4,5},{5,4},{6,7},{7,6},{8,9},{9,8},{10,11... | collective-permute-start | bytes 983048 | tf_op jit(solution)/shard_map/ppermute | solution.py:24
  24.0 5.6 %collective-permute-start.4 = (bf16[128,1280]{1,0:T(8,128)(2,1)S(1)}, bf16[128,1280]{1,0:T(8,128)(2,1)S(1)}, u32[]{:S(2)}, u32[]{:S(2)}) collective-permute-start(bf16[128,1280]{1,0:T(8,128)(2,1)S(1)} %collective-permute-done.3.refs_4_), channel_id=1, source_target_pairs={{0,1},{1,0},{2,3},{3,2},{4,5},{5,4},{6,7},{7,6},{8,9},{9,8},{10,11... | collective-permute-start | bytes 983048 | tf_op jit(solution)/shard_map/ppermute | solution.py:24
  29.8 1.1 collective-permute-done.4.refs_5_
  32.1 4.4 %shard_map.77 = (bf16[1024,128]{1,0:T(8,128)(2,1)}, bf16[1024,128]{1,0:T(8,128)(2,1)}, bf16[1024,128]{1,0:T(8,128)(2,1)}, bf16[256,128]{1,0:T(8,128)(2,1)}, bf16[1024,128]{1,0:T(8,128)(2,1)}) custom-call(bf16[1024,384]{1,0:T(8,128)(2,1)} %bitcast.17, bf16[128,1280]{1,0:T(8,128)(2,1)} %get-tuple-element.57.refs_0_, bf16[128,1280]{1,0:T(8,128)(2,1)} %copy-done.12, ...), custom_call_target="tpu_custom_call" | custom-call | flops 805306368 | bytes 4194304 | tf_op jit(solution)/shard_map/pallas_call | solution.py:201
  36.5 3.1 %collective-permute-start.7 = (bf16[256,128]{1,0:T(8,128)(2,1)}, bf16[256,128]{1,0:T(8,128)(2,1)S(1)}, u32[]{:S(2)}, u32[]{:S(2)}) collective-permute-start(bf16[256,128]{1,0:T(8,128)(2,1)} %get-tuple-element.60.refs_4_), channel_id=1, source_target_pairs={{0,4},{4,0},{8,12},{12,8},{1,5},{5,1},{9,13},{13,9},{2,6},{6,2},{1... | collective-permute-start | bytes 196616 | tf_op jit(solution)/shard_map/ppermute | solution.py:24
  39.6 4.0 %collective-permute-start.8 = (bf16[256,128]{1,0:T(8,128)(2,1)}, bf16[256,128]{1,0:T(8,128)(2,1)S(1)}, u32[]{:S(2)}, u32[]{:S(2)}) collective-permute-start(bf16[256,128]{1,0:T(8,128)(2,1)} %get-tuple-element.60.refs_4_), channel_id=1, source_target_pairs={{0,8},{4,12},{8,0},{12,4},{1,9},{5,13},{9,1},{13,5},{2,10},{6,14},... | collective-permute-start | bytes 196616 | tf_op jit(solution)/shard_map/ppermute | solution.py:24
  43.6 0.9 copy-done
  45.5 0.9 copy-done.2
  49.5 2.8 %collective-permute-start.10 = (bf16[128,128]{1,0:T(8,128)(2,1)S(1)}, bf16[128,128]{1,0:T(8,128)(2,1)S(1)}, u32[]{:S(2)}, u32[]{:S(2)}) collective-permute-start(bf16[128,128]{1,0:T(8,128)(2,1)S(1)} %shard_map.79), channel_id=1, source_target_pairs={{0,32},{32,0},{1,33},{33,1},{2,34},{34,2},{3,35},{35,3},{4,36},{36... | collective-permute-start | bytes 98312 | tf_op jit(solution)/shard_map/ppermute | solution.py:24
  52.3 1.6 %collective-permute-done.10.refs_6_ = bf16[128,128]{1,0:T(8,128)(2,1)S(1)} collective-permute-done((bf16[128,128]{1,0:T(8,128)(2,1)S(1)}, bf16[128,128]{1,0:T(8,128)(2,1)S(1)}, u32[]{:S(2)}, u32[]{:S(2)}) %collective-permute-start.10) | collective-permute-done | bytes 32800 | tf_op jit(solution)/shard_map/ppermute | solution.py:24
  54.6 1.4 %collective-permute-start.11 = (bf16[256,128]{1,0:T(8,128)(2,1)S(1)}, bf16[256,128]{1,0:T(8,128)(2,1)S(1)}, u32[]{:S(2)}, u32[]{:S(2)}) collective-permute-start(bf16[256,128]{1,0:T(8,128)(2,1)S(1)} %get-tuple-element.78.refs_0_.refs_5_), channel_id=1, source_target_pairs={{0,4},{4,0},{8,12},{12,8},{1,5},{5,1},{9,13},{13,9},{2,6},{6,2},{1... | collective-permute-start | bytes 196616 | tf_op jit(solution)/shard_map/ppermute | solution.py:24
  56.0 5.0 %collective-permute-start.12 = (bf16[256,128]{1,0:T(8,128)(2,1)S(1)}, bf16[256,128]{1,0:T(8,128)(2,1)S(1)}, u32[]{:S(2)}, u32[]{:S(2)}) collective-permute-start(bf16[256,128]{1,0:T(8,128)(2,1)S(1)} %get-tuple-element.78.refs_0_.refs_5_), channel_id=1, source_target_pairs={{0,8},{4,12},{8,0},{12,4},{1,9},{5,13},{9,1},{13,5},{2,10},{6,14},... | collective-permute-start | bytes 196616 | tf_op jit(solution)/shard_map/ppermute | solution.py:24
  61.1 2.3 %collective-permute-done.12.refs_2_.refs_7_ = bf16[256,128]{1,0:T(8,128)(2,1)S(1)} collective-permute-done((bf16[256,128]{1,0:T(8,128)(2,1)S(1)}, bf16[256,128]{1,0:T(8,128)(2,1)S(1)}, u32[]{:S(2)}, u32[]{:S(2)}) %collective-permute-start.12) | collective-permute-done | bytes 65568 | tf_op jit(solution)/shard_map/ppermute | solution.py:24
  63.4 3.5 %collective-permute-done.13.refs_3_.refs_8_ = bf16[256,128]{1,0:T(8,128)(2,1)S(1)} collective-permute-done((bf16[256,128]{1,0:T(8,128)(2,1)S(1)}, bf16[256,128]{1,0:T(8,128)(2,1)S(1)}, u32[]{:S(2)}, u32[]{:S(2)}) %collective-permute-start.13) | collective-permute-done | bytes 65568 | tf_op jit(solution)/shard_map/ppermute | solution.py:24
  66.9 3.0 %collective-permute-start.14 = (bf16[128,128]{1,0:T(8,128)(2,1)S(1)}, bf16[128,128]{1,0:T(8,128)(2,1)S(1)}, u32[]{:S(2)}, u32[]{:S(2)}) collective-permute-start(bf16[128,128]{1,0:T(8,128)(2,1)S(1)} %shard_map.81), channel_id=1, source_target_pairs={{0,32},{32,0},{1,33},{33,1},{2,34},{34,2},{3,35},{35,3},{4,36},{36... | collective-permute-start | bytes 98312 | tf_op jit(solution)/shard_map/ppermute | solution.py:24
  69.9 1.3 %shard_map.82 = (bf16[1024,256]{1,0:T(8,128)(2,1)S(1)}, f32[1024,128]{1,0:T(8,128)S(1)}, f32[1024,128]{1,0:T(8,128)S(1)}) custom-call(bf16[1024,128]{1,0:T(8,128)(2,1)S(1)} %get-tuple-element.68.refs_0_, bf16[1024,128]{1,0:T(8,128)(2,1)S(1)} %get-tuple-element.66.refs_1_.refs_0_, bf16[1024,128]{1,0:T(8,128)(2,1)S(1)} %get-tuple-element.67.refs_2_.refs_1_, ...), custom_call_target="tpu_custom_call" | custom-call | flops 536870912 | bytes 3997696 | tf_op jit(solution)/shard_map/pallas_call | solution.py:76
  71.5 1.6 %shard_map.83 = (bf16[1024,384]{1,0:T(8,128)(2,1)}, bf16[2,128,512]{2,1,0:T(8,128)(2,1)}, bf16[2,128,512]{2,1,0:T(8,128)(2,1)}, bf16[2,128,512]{2,1,0:T(8,128)(2,1)}, bf16[2,128,512]{2,1,0:T(8,128)(2,1)}) custom-call(bf16[1024,128]{1,0:T(8,128)(2,1)S(1)} %get-tuple-element.66.refs_1_.refs_0_, bf16[1024,128]{1,0:T(8,128)(2,1)S(1)} %get-tuple-element.67.refs_2_.refs_1_, ...), custom_call_target="tpu_custom_call" | custom-call | flops 134217728 | bytes 4227072 | tf_op jit(solution)/shard_map/pallas_call | solution.py:76
  73.2 4.1 %shard_map.84 = bf16[1088,384]{1,0:T(8,128)(2,1)} custom-call(bf16[1024,384]{1,0:T(8,128)(2,1)} %get-tuple-element.90.joined_far, f32[8,128]{1,0:T(8,128)} %copy-done.6, bf16[128,1280]{1,0:T(8,128)(2,1)} %get-tuple-element.57.refs_0_, bf16[128,1280]{1,0:T(8,128)(2,1)} %copy-done.12, bf16[128,1280]{1,0:T(8,128)(2,1)} %copy-done.9, ...), custom_call_target="tpu_custom_call" | custom-call | flops 805306368 | bytes 4194304 | tf_op jit(solution)/shard_map/pallas_call | solution.py:359
  77.3 3.8 %all-to-all-start.1 = ((bf16[4,272,384]{2,1,0:T(8,128)(2,1)}), bf16[4,272,384]{2,1,0:T(8,128)(2,1)S(1)}, u32[]{:S(2)}, u32[]{:S(2)}) async-start(bf16[4,272,384]{2,1,0:T(8,128)(2,1)} %bitcast.16), calls=%async_computation.1 | async-start | bytes 1671168 | tf_op jit(solution)/shard_map/all_to_all | solution.py:488
  81.1 1.5 %collective-permute-start.15 = (bf16[2,128,512]{2,1,0:T(8,128)(2,1)S(1)}, bf16[2,128,512]{2,1,0:T(8,128)(2,1)S(1)}, u32[]{:S(2)}, u32[]{:S(2)}) collective-permute-start(bf16[2,128,512]{2,1,0:T(8,128)(2,1)S(1)} %copy-done.27), channel_id=1, source_target_pairs={{0,2},{2,0},{16,18},{18,16},{1,3},{3,1},{17,19},{19,17},{4,6},{6,4... | collective-permute-start | bytes 786440 | tf_op jit(solution)/shard_map/ppermute | solution.py:24
  82.6 1.4 %collective-permute-start.16 = (bf16[2,128,512]{2,1,0:T(8,128)(2,1)S(1)}, bf16[2,128,512]{2,1,0:T(8,128)(2,1)S(1)}, u32[]{:S(2)}, u32[]{:S(2)}) collective-permute-start(bf16[2,128,512]{2,1,0:T(8,128)(2,1)S(1)} %copy-done.26), channel_id=1, source_target_pairs={{0,16},{2,18},{16,0},{18,2},{1,17},{3,19},{17,1},{19,3},{4,20},{6,... | collective-permute-start | bytes 786440 | tf_op jit(solution)/shard_map/ppermute | solution.py:24
  84.0 1.2 collective-permute-start.17
  85.2 4.5 %all-to-all-done.1 = bf16[4,272,384]{2,1,0:T(8,128)(2,1)S(1)} async-done(((bf16[4,272,384]{2,1,0:T(8,128)(2,1)}), bf16[4,272,384]{2,1,0:T(8,128)(2,1)S(1)}, u32[]{:S(2)}, u32[]{:S(2)}) %all-to-all-start.1) | async-done | bytes 835616 | tf_op jit(solution)/shard_map/all_to_all | solution.py:488
  90.5 10.1 %all_to_all.45 = bf16[4,256,128]{2,1,0:T(8,128)(2,1)S(1)} all-to-all(bf16[4,256,128]{2,1,0:T(8,128)(2,1)} %bitcast.19), channel_id=1, replica_groups=mesh['dp'=4,'yh'=2,'yl'=2,'zh'=2,'zm'=2,'zl'=2,'c'=2] {'yh','yl'}, dimensions={0} | all-to-all | bytes 524288 | tf_op jit(solution)/shard_map/all_to_all | solution.py:492
  101.4 11.1 %all-to-all-start.3 = ((f32[16,32,128]{2,1,0:T(8,128)}), f32[16,32,128]{2,1,0:T(8,128)S(1)}, u32[]{:S(2)}, u32[]{:S(2)}) async-start(f32[16,32,128]{2,1,0:T(8,128)} %bitcast.18), calls=%async_computation.3 | async-start | bytes 524288 | tf_op jit(solution)/shard_map/all_to_all | solution.py:494
  116.0 4.6 %shard_map.86 = (bf16[128,512]{1,0:T(8,128)(2,1)}, bf16[128,512]{1,0:T(8,128)(2,1)}, bf16[128,1024]{1,0:T(8,128)(2,1)}) custom-call(bf16[512,3072]{1,0:T(8,128)(2,1)} %all-gather.2.cloned.1.call-done.refs_0_, bf16[2,128,512]{2,1,0:T(8,128)(2,1)} %get-tuple-element.92.refs_1_, bf16[2,128,512]{2,1,0:T(8,128)(2,1)} %copy-done.20, ...), custom_call_target="tpu_custom_call" | custom-call | flops 805306368 | bytes 5767168 | tf_op jit(solution)/shard_map/pallas_call | solution.py:76
  120.9 3.3 %all-to-all-done.3 = f32[16,32,128]{2,1,0:T(8,128)S(1)} async-done(((f32[16,32,128]{2,1,0:T(8,128)}), f32[16,32,128]{2,1,0:T(8,128)S(1)}, u32[]{:S(2)}, u32[]{:S(2)}) %all-to-all-start.3) | async-done | bytes 262176 | tf_op jit(solution)/shard_map/all_to_all | solution.py:494
  (95 shorter events, 13.4 us)
Async XLA Ops:
  9.7 9.9 %collective-permute-start = (bf16[128,1280]{1,0:T(8,128)(2,1)}, bf16[128,1280]{1,0:T(8,128)(2,1)S(1)}, u32[]{:S(2)}, u32[]{:S(2)}) collective-permute-start(bf16[128,1280]{1,0:T(8,128)(2,1)} %get-tuple-element.56), channel_id=1, source_target_pairs={{0,2},{2,0},{16,18},{18,16},{1,3},{3,1},{17,19},{19,17},{4,6},{6,4... | collective-permute-start | bytes 983048 | tf_op jit(solution)/shard_map/ppermute | solution.py:24
  12.2 11.7 %collective-permute-start.3 = (bf16[128,1280]{1,0:T(8,128)(2,1)}, bf16[128,1280]{1,0:T(8,128)(2,1)S(1)}, u32[]{:S(2)}, u32[]{:S(2)}) collective-permute-start(bf16[128,1280]{1,0:T(8,128)(2,1)} %get-tuple-element.58), channel_id=1, source_target_pairs={{0,16},{2,18},{16,0},{18,2},{1,17},{3,19},{17,1},{19,3},{4,20},{6,... | collective-permute-start | bytes 983048 | tf_op jit(solution)/shard_map/ppermute | solution.py:24
  13.5 16.1 %collective-permute-start.5 = (bf16[128,1280]{1,0:T(8,128)(2,1)}, bf16[128,1280]{1,0:T(8,128)(2,1)S(1)}, u32[]{:S(2)}, u32[]{:S(2)}) collective-permute-start(bf16[128,1280]{1,0:T(8,128)(2,1)} %get-tuple-element.59), channel_id=1, source_target_pairs={{0,18},{2,16},{16,2},{18,0},{1,19},{3,17},{17,3},{19,1},{4,22},{6,... | collective-permute-start | bytes 983048 | tf_op jit(solution)/shard_map/ppermute | solution.py:24
  13.5 16.2 %all-to-all-start = ((bf16[4,256,384]{2,1,0:T(8,128)(2,1)}), bf16[4,256,384]{2,1,0:T(8,128)(2,1)S(1)}, u32[]{:S(2)}, u32[]{:S(2)}) async-start(bf16[4,256,384]{2,1,0:T(8,128)(2,1)} %bitcast.20), calls=%async_computation | async-start | bytes 1572864 | tf_op jit(solution)/shard_map/all_to_all | solution.py:451
  17.6 97.8 %all-gather.2.cloned.1.call-start = ((), (), s32[]{:S(2)}) async-start(), calls=%async_computation.4 | async-start | bytes 3932160 | tf_op jit(solution)/shard_map/all_gather | solution.py:460
  19.6 32.6 %copy-start.24 = (bf16[1024]{0:T(1024)(128)(2,1)S(1)}, bf16[1024]{0:T(1024)(128)(2,1)}, u32[]{:S(2)}) copy-start(bf16[1024]{0:T(1024)(128)(2,1)} %param.6) | copy-start | bytes 6148
  19.6 11.7 %copy-start.9 = (bf16[128,1280]{1,0:T(8,128)(2,1)}, bf16[128,1280]{1,0:T(8,128)(2,1)S(1)}, u32[]{:S(2)}) copy-start(bf16[128,1280]{1,0:T(8,128)(2,1)S(1)} %collective-permute-done.refs_2_) | copy-start | bytes 983044
  19.7 10.1 %collective-permute-start.1 = (bf16[128,1280]{1,0:T(8,128)(2,1)S(1)}, bf16[128,1280]{1,0:T(8,128)(2,1)S(1)}, u32[]{:S(2)}, u32[]{:S(2)}) collective-permute-start(bf16[128,1280]{1,0:T(8,128)(2,1)S(1)} %copy-done.8), channel_id=1, source_target_pairs={{0,1},{1,0},{2,3},{3,2},{4,5},{5,4},{6,7},{7,6},{8,9},{9,8},{10,11... | collective-permute-start | bytes 983048 | tf_op jit(solution)/shard_map/ppermute | solution.py:24
  23.9 5.8 %collective-permute-start.2 = (bf16[128,1280]{1,0:T(8,128)(2,1)S(1)}, bf16[128,1280]{1,0:T(8,128)(2,1)S(1)}, u32[]{:S(2)}, u32[]{:S(2)}) collective-permute-start(bf16[128,1280]{1,0:T(8,128)(2,1)S(1)} %collective-permute-done.refs_2_), channel_id=1, source_target_pairs={{0,1},{1,0},{2,3},{3,2},{4,5},{5,4},{6,7},{7,6},{8,9},{9,8},{10,11... | collective-permute-start | bytes 983048 | tf_op jit(solution)/shard_map/ppermute | solution.py:24
  24.0 6.9 %collective-permute-start.4 = (bf16[128,1280]{1,0:T(8,128)(2,1)S(1)}, bf16[128,1280]{1,0:T(8,128)(2,1)S(1)}, u32[]{:S(2)}, u32[]{:S(2)}) collective-permute-start(bf16[128,1280]{1,0:T(8,128)(2,1)S(1)} %collective-permute-done.3.refs_4_), channel_id=1, source_target_pairs={{0,1},{1,0},{2,3},{3,2},{4,5},{5,4},{6,7},{7,6},{8,9},{9,8},{10,11... | collective-permute-start | bytes 983048 | tf_op jit(solution)/shard_map/ppermute | solution.py:24
  29.6 1.7 %collective-permute-start.6 = (bf16[128,1280]{1,0:T(8,128)(2,1)S(1)}, bf16[128,1280]{1,0:T(8,128)(2,1)S(1)}, u32[]{:S(2)}, u32[]{:S(2)}) collective-permute-start(bf16[128,1280]{1,0:T(8,128)(2,1)S(1)} %collective-permute-done.5.refs_6_), channel_id=1, source_target_pairs={{0,1},{1,0},{2,3},{3,2},{4,5},{5,4},{6,7},{7,6},{8,9},{9,8},{10,11... | collective-permute-start | bytes 983048 | tf_op jit(solution)/shard_map/ppermute | solution.py:24
  36.5 12.6 %collective-permute-start.7 = (bf16[256,128]{1,0:T(8,128)(2,1)}, bf16[256,128]{1,0:T(8,128)(2,1)S(1)}, u32[]{:S(2)}, u32[]{:S(2)}) collective-permute-start(bf16[256,128]{1,0:T(8,128)(2,1)} %get-tuple-element.60.refs_4_), channel_id=1, source_target_pairs={{0,4},{4,0},{8,12},{12,8},{1,5},{5,1},{9,13},{13,9},{2,6},{6,2},{1... | collective-permute-start | bytes 196616 | tf_op jit(solution)/shard_map/ppermute | solution.py:24
  39.6 9.5 %collective-permute-start.8 = (bf16[256,128]{1,0:T(8,128)(2,1)}, bf16[256,128]{1,0:T(8,128)(2,1)S(1)}, u32[]{:S(2)}, u32[]{:S(2)}) collective-permute-start(bf16[256,128]{1,0:T(8,128)(2,1)} %get-tuple-element.60.refs_4_), channel_id=1, source_target_pairs={{0,8},{4,12},{8,0},{12,4},{1,9},{5,13},{9,1},{13,5},{2,10},{6,14},... | collective-permute-start | bytes 196616 | tf_op jit(solution)/shard_map/ppermute | solution.py:24
  43.6 5.8 %collective-permute-start.9 = (bf16[256,128]{1,0:T(8,128)(2,1)}, bf16[256,128]{1,0:T(8,128)(2,1)S(1)}, u32[]{:S(2)}, u32[]{:S(2)}) collective-permute-start(bf16[256,128]{1,0:T(8,128)(2,1)} %get-tuple-element.60.refs_4_), channel_id=1, source_target_pairs={{0,12},{4,8},{8,4},{12,0},{1,13},{5,9},{9,5},{13,1},{2,14},{6,10},... | collective-permute-start | bytes 196616 | tf_op jit(solution)/shard_map/ppermute | solution.py:24
  49.5 4.4 %collective-permute-start.10 = (bf16[128,128]{1,0:T(8,128)(2,1)S(1)}, bf16[128,128]{1,0:T(8,128)(2,1)S(1)}, u32[]{:S(2)}, u32[]{:S(2)}) collective-permute-start(bf16[128,128]{1,0:T(8,128)(2,1)S(1)} %shard_map.79), channel_id=1, source_target_pairs={{0,32},{32,0},{1,33},{33,1},{2,34},{34,2},{3,35},{35,3},{4,36},{36... | collective-permute-start | bytes 98312 | tf_op jit(solution)/shard_map/ppermute | solution.py:24
  54.6 16.9 %copy-start.6 = (f32[8,128]{1,0:T(8,128)}, f32[8,128]{1,0:T(8,128)S(1)}, u32[]{:S(2)}) copy-start(f32[8,128]{1,0:T(8,128)S(1)} %get-tuple-element.91.gain_far) | copy-start | bytes 12292
  54.6 6.5 %collective-permute-start.11 = (bf16[256,128]{1,0:T(8,128)(2,1)S(1)}, bf16[256,128]{1,0:T(8,128)(2,1)S(1)}, u32[]{:S(2)}, u32[]{:S(2)}) collective-permute-start(bf16[256,128]{1,0:T(8,128)(2,1)S(1)} %get-tuple-element.78.refs_0_.refs_5_), channel_id=1, source_target_pairs={{0,4},{4,0},{8,12},{12,8},{1,5},{5,1},{9,13},{13,9},{2,6},{6,2},{1... | collective-permute-start | bytes 196616 | tf_op jit(solution)/shard_map/ppermute | solution.py:24
  56.0 7.4 %collective-permute-start.12 = (bf16[256,128]{1,0:T(8,128)(2,1)S(1)}, bf16[256,128]{1,0:T(8,128)(2,1)S(1)}, u32[]{:S(2)}, u32[]{:S(2)}) collective-permute-start(bf16[256,128]{1,0:T(8,128)(2,1)S(1)} %get-tuple-element.78.refs_0_.refs_5_), channel_id=1, source_target_pairs={{0,8},{4,12},{8,0},{12,4},{1,9},{5,13},{9,1},{13,5},{2,10},{6,14},... | collective-permute-start | bytes 196616 | tf_op jit(solution)/shard_map/ppermute | solution.py:24
  61.1 5.8 %collective-permute-start.13 = (bf16[256,128]{1,0:T(8,128)(2,1)S(1)}, bf16[256,128]{1,0:T(8,128)(2,1)S(1)}, u32[]{:S(2)}, u32[]{:S(2)}) collective-permute-start(bf16[256,128]{1,0:T(8,128)(2,1)S(1)} %get-tuple-element.78.refs_0_.refs_5_), channel_id=1, source_target_pairs={{0,12},{4,8},{8,4},{12,0},{1,13},{5,9},{9,5},{13,1},{2,14},{6,10},... | collective-permute-start | bytes 196616 | tf_op jit(solution)/shard_map/ppermute | solution.py:24
  66.9 4.6 %collective-permute-start.14 = (bf16[128,128]{1,0:T(8,128)(2,1)S(1)}, bf16[128,128]{1,0:T(8,128)(2,1)S(1)}, u32[]{:S(2)}, u32[]{:S(2)}) collective-permute-start(bf16[128,128]{1,0:T(8,128)(2,1)S(1)} %shard_map.81), channel_id=1, source_target_pairs={{0,32},{32,0},{1,33},{33,1},{2,34},{34,2},{3,35},{35,3},{4,36},{36... | collective-permute-start | bytes 98312 | tf_op jit(solution)/shard_map/ppermute | solution.py:24
  73.2 10.8 %copy-start.25 = (bf16[2,128,512]{2,1,0:T(8,128)(2,1)S(1)}, bf16[2,128,512]{2,1,0:T(8,128)(2,1)}, u32[]{:S(2)}) copy-start(bf16[2,128,512]{2,1,0:T(8,128)(2,1)} %get-tuple-element.89) | copy-start | bytes 786436
  77.3 35.3 %copy-start.16 = (bf16[2,128,512]{2,1,0:T(8,128)(2,1)S(1)}, bf16[2,128,512]{2,1,0:T(8,128)(2,1)}, u32[]{:S(2)}) copy-start(bf16[2,128,512]{2,1,0:T(8,128)(2,1)} %get-tuple-element.92.refs_1_) | copy-start | bytes 786436
  77.3 12.4 %all-to-all-start.1 = ((bf16[4,272,384]{2,1,0:T(8,128)(2,1)}), bf16[4,272,384]{2,1,0:T(8,128)(2,1)S(1)}, u32[]{:S(2)}, u32[]{:S(2)}) async-start(bf16[4,272,384]{2,1,0:T(8,128)(2,1)} %bitcast.16), calls=%async_computation.1 | async-start | bytes 1671168 | tf_op jit(solution)/shard_map/all_to_all | solution.py:488
  81.1 31.4 %collective-permute-start.15 = (bf16[2,128,512]{2,1,0:T(8,128)(2,1)S(1)}, bf16[2,128,512]{2,1,0:T(8,128)(2,1)S(1)}, u32[]{:S(2)}, u32[]{:S(2)}) collective-permute-start(bf16[2,128,512]{2,1,0:T(8,128)(2,1)S(1)} %copy-done.27), channel_id=1, source_target_pairs={{0,2},{2,0},{16,18},{18,16},{1,3},{3,1},{17,19},{19,17},{4,6},{6,4... | collective-permute-start | bytes 786440 | tf_op jit(solution)/shard_map/ppermute | solution.py:24
  82.6 29.9 %collective-permute-start.16 = (bf16[2,128,512]{2,1,0:T(8,128)(2,1)S(1)}, bf16[2,128,512]{2,1,0:T(8,128)(2,1)S(1)}, u32[]{:S(2)}, u32[]{:S(2)}) collective-permute-start(bf16[2,128,512]{2,1,0:T(8,128)(2,1)S(1)} %copy-done.26), channel_id=1, source_target_pairs={{0,16},{2,18},{16,0},{18,2},{1,17},{3,19},{17,1},{19,3},{4,20},{6,... | collective-permute-start | bytes 786440 | tf_op jit(solution)/shard_map/ppermute | solution.py:24
  84.0 28.6 %collective-permute-start.17 = (bf16[2,128,512]{2,1,0:T(8,128)(2,1)S(1)}, bf16[2,128,512]{2,1,0:T(8,128)(2,1)S(1)}, u32[]{:S(2)}, u32[]{:S(2)}) collective-permute-start(bf16[2,128,512]{2,1,0:T(8,128)(2,1)S(1)} %copy-done.25), channel_id=1, source_target_pairs={{0,18},{2,16},{16,2},{18,0},{1,19},{3,17},{17,3},{19,1},{4,22},{6,... | collective-permute-start | bytes 786440 | tf_op jit(solution)/shard_map/ppermute | solution.py:24
  101.4 22.8 %all-to-all-start.3 = ((f32[16,32,128]{2,1,0:T(8,128)}), f32[16,32,128]{2,1,0:T(8,128)S(1)}, u32[]{:S(2)}, u32[]{:S(2)}) async-start(f32[16,32,128]{2,1,0:T(8,128)} %bitcast.18), calls=%async_computation.3 | async-start | bytes 524288 | tf_op jit(solution)/shard_map/all_to_all | solution.py:494
  112.6 1.6 %collective-permute-start.18 = (bf16[2,128,512]{2,1,0:T(8,128)(2,1)S(1)}, bf16[2,128,512]{2,1,0:T(8,128)(2,1)S(1)}, u32[]{:S(2)}, u32[]{:S(2)}) collective-permute-start(bf16[2,128,512]{2,1,0:T(8,128)(2,1)S(1)} %copy-done.16), channel_id=1, source_target_pairs={{0,1},{1,0},{2,3},{3,2},{4,5},{5,4},{6,7},{7,6},{8,9},{9,8},{10,11... | collective-permute-start | bytes 786440 | tf_op jit(solution)/shard_map/ppermute | solution.py:24
  112.8 1.8 %collective-permute-start.19 = (bf16[2,128,512]{2,1,0:T(8,128)(2,1)S(1)}, bf16[2,128,512]{2,1,0:T(8,128)(2,1)S(1)}, u32[]{:S(2)}, u32[]{:S(2)}) collective-permute-start(bf16[2,128,512]{2,1,0:T(8,128)(2,1)S(1)} %collective-permute-done.15.refs_3_), channel_id=1, source_target_pairs={{0,1},{1,0},{2,3},{3,2},{4,5},{5,4},{6,7},{7,6},{8,9},{9,8},{10,11... | collective-permute-start | bytes 786440 | tf_op jit(solution)/shard_map/ppermute | solution.py:24
  113.2 1.8 %collective-permute-start.20 = (bf16[2,128,512]{2,1,0:T(8,128)(2,1)S(1)}, bf16[2,128,512]{2,1,0:T(8,128)(2,1)S(1)}, u32[]{:S(2)}, u32[]{:S(2)}) collective-permute-start(bf16[2,128,512]{2,1,0:T(8,128)(2,1)S(1)} %collective-permute-done.16.refs_5_), channel_id=1, source_target_pairs={{0,1},{1,0},{2,3},{3,2},{4,5},{5,4},{6,7},{7,6},{8,9},{9,8},{10,11... | collective-permute-start | bytes 786440 | tf_op jit(solution)/shard_map/ppermute | solution.py:24
  113.3 2.0 %collective-permute-start.21 = (bf16[2,128,512]{2,1,0:T(8,128)(2,1)S(1)}, bf16[2,128,512]{2,1,0:T(8,128)(2,1)S(1)}, u32[]{:S(2)}, u32[]{:S(2)}) collective-permute-start(bf16[2,128,512]{2,1,0:T(8,128)(2,1)S(1)} %collective-permute-done.17.refs_7_), channel_id=1, source_target_pairs={{0,1},{1,0},{2,3},{3,2},{4,5},{5,4},{6,7},{7,6},{8,9},{9,8},{10,11... | collective-permute-start | bytes 786440 | tf_op jit(solution)/shard_map/ppermute | solution.py:24
  120.7 3.5 %collective-permute-start.22 = (bf16[128,512]{1,0:T(8,128)(2,1)}, bf16[128,512]{1,0:T(8,128)(2,1)S(1)}, u32[]{:S(2)}, u32[]{:S(2)}) collective-permute-start(bf16[128,512]{1,0:T(8,128)(2,1)} %get-tuple-element.97), channel_id=1, source_target_pairs={{0,1},{1,0},{2,3},{3,2},{4,5},{5,4},{6,7},{7,6},{8,9},{9,8},{10,11... | collective-permute-start | bytes 393224 | tf_op jit(solution)/shard_map/ppermute | solution.py:24
  (23 other events, 60.1 us)
Sparse Core Ops, SparseCore 0:
  36.6 43.6 all-gather.1
